TPU v7x, 32 devices: a whole 2x2x4 slice. The times are simulated.
32 devices in a mesh: runs: 2 (over y), gz: 4 (over x, core), gx: 4 (over z).
Axes of the slice: x: 2, y: 2, z: 4, core: 2. Of those that a mesh axis runs over, the one named last changes fastest.
Arguments:
- magnetic: float32 [3, 64, 64, 1024], P(None, 'gx', 'gz', 'runs'), parts along dimension 3, may hold values from -12 to 12
- friction: float32 [64], P('gz'), may hold values from 0.3 to 3
Outputs:
- relaxed: float32 [3, 64, 64, 1024], P(None, 'gx', 'gz', 'runs'), parts along dimension 3
- potential: float32 [3, 64, 64, 1024], P(None, 'gx', 'gz', 'runs'), parts along dimension 3
There are 2 independent parts, one for each index of `runs`. A program takes and returns all parts, laid end to end along the dimension named above; an argument that names none is the same for every part. Nothing has to cross between parts.
All inputs are finite; a program needn't handle non-finite values.
Results may differ from a plain program's by a relative error of at most 0.00017.
Values sent between devices are 32-bit elements; how exact they have to be, the bound alone decides.
No kernel may reach another device: no remote copies, remote signals or barrier semaphores. Data moves between devices by JAX's collectives and lax.ppermute only.
A program may use at most 64 MiB of HBM per device.

v0:
```python
import functools

import jax
import jax.numpy as jnp
from jax import lax
from jax.experimental import pallas as pl
from jax.experimental.pallas import tpu as pltpu
from jax.sharding import PartitionSpec as P

DESCENTS = 2
RELAX = 2

step_scale = 0.5
time_step = 0.2

LANES = 128
ROWS = 8
HALO = 4
BASE = 8


def pairings(count):
    first = [(i, i ^ 1) for i in range(count) if i ^ 1 < count]
    second = [(i, i + 1 if i % 2 else i - 1) for i in range(count)]
    return first, [pair for pair in second if 0 <= pair[1] < count]


def is_even(axis):
    return lax.axis_index(axis) % 2 == 0


def edges(cells, axis, dim):
    far = cells.shape[dim] - HALO
    even = is_even(axis)
    first = lax.dynamic_slice_in_dim(cells, jnp.where(even, far, 0), HALO, dim)
    second = lax.dynamic_slice_in_dim(cells, jnp.where(even, 0, far), HALO, dim)
    return first, second


def swapped(pair, axis):
    first, second = pairings(lax.axis_size(axis))
    return lax.ppermute(pair[0], axis, first), lax.ppermute(pair[1], axis, second)


def shared(tile_copies):
    return lax.all_to_all(tile_copies, ("gz", "gx"), 0, 0)


def y_diff(blocks, lane):
    count = len(blocks)
    after = [pltpu.roll(b, LANES - 1, 1) for b in blocks]
    before = [pltpu.roll(b, 1, 1) for b in blocks]
    return [
        jnp.where(lane == LANES - 1, after[(j + 1) % count], after[j])
        - jnp.where(lane == 0, before[(j - 1) % count], before[j])
        for j in range(count)
    ]


def cross(a, b):
    return (a[1] * b[2] - a[2] * b[1], a[2] * b[0] - a[0] * b[2], a[0] * b[1] - a[1] * b[0])


def dot(a, b):
    return a[0] * b[0] + a[1] * b[1] + a[2] * b[2]


def iotas():
    return (
        lax.broadcasted_iota(jnp.int32, (ROWS, LANES), 0),
        lax.broadcasted_iota(jnp.int32, (ROWS, LANES), 1),
    )


def windows(low, high):
    return [low + ROWS * w for w in range(-(-(high - low) // ROWS))]


def own_place(cx, cz):
    return (
        lax.axis_index("gx") * cx,
        lax.axis_size("gx") * cx,
        lax.axis_index("gz") * cz,
        lax.axis_size("gz") * cz,
    )


def descent_stages(bp, bx0, halo, cx, cz, blocks, omega_ref, lane):
    planes = cx + 2 * halo + 2

    def plane(x, _):
        at = x + (bx0 - halo - 1)
        for r in windows(BASE - halo - 1, BASE + cz + halo + 1):
            def ld(c, j, dx=0, dz=0):
                return bp[c, at + dx, j, r + dz : r + dz + ROWS, :]

            dy = [y_diff([ld(c, j) for j in range(blocks)], lane) for c in range(3)]
            for j in range(blocks):
                field = [ld(c, j) for c in range(3)]
                dx = [ld(c, j, dx=1) - ld(c, j, dx=-1) for c in range(3)]
                dz = [ld(c, j, dz=1) - ld(c, j, dz=-1) for c in range(3)]
                current = (dy[2][j] - dz[1], dz[0] - dx[2], dx[1] - dy[0][j])
                spread = dx[0] + dy[1][j] + dz[2]
                square = jnp.maximum(dot(field, field), 1.0)
                inverse = 0.5 / square
                lorentz = cross(current, field)
                omega = [(lorentz[c] - spread * field[c]) * inverse for c in range(3)]
                twist = cross(omega, field)
                along = dot(omega, field)
                for k, value in enumerate([*twist, along, *omega, *current, spread]):
                    omega_ref[k, x, j, r : r + ROWS, :] = value
        return 0

    lax.fori_loop(0, planes, plane, 0)


def doubled_force(bp, bx0, omega_ref, at, x, r, blocks, lane):
    def ld(k, j, dx=0, dz=0):
        return omega_ref[k, at + dx, j, r + dz : r + dz + ROWS, :]

    dy = {k: y_diff([ld(k, j) for j in range(blocks)], lane) for k in (0, 2, 3)}
    for j in range(blocks):
        field = [bp[c, x + bx0, j, r : r + ROWS, :] for c in range(3)]
        omega = [ld(4 + c, j) for c in range(3)]
        current = [ld(7 + c, j) for c in range(3)]
        spread = ld(10, j)

        def dx(k):
            return ld(k, j, dx=1) - ld(k, j, dx=-1)

        def dz(k):
            return ld(k, j, dz=1) - ld(k, j, dz=-1)

        curled = (dy[2][j] - dz(1) - dx(3), dz(0) - dx(2) - dy[3][j], dx(1) - dy[0][j] - dz(3))
        bent = cross(omega, current)
        size = dot(omega, omega)
        twice = size + size
        force = [curled[c] - bent[c] + omega[c] * spread + twice * field[c] for c in range(3)]
        yield j, force, field, size, spread


def density_of(field, size, spread):
    square = dot(field, field)
    return size * jnp.maximum(square, 1.0) + 0.25 * (spread * spread) * jnp.maximum(1.0 - square, 0.0)


def store_sums(sums_ref, functional, slope, rows):
    functional = jnp.sum(functional, axis=0, keepdims=True)
    slope = jnp.sum(slope, axis=0, keepdims=True)
    tile = jnp.where(rows == 0, functional, jnp.where(rows == 1, slope, 0.0))
    for k in range(sums_ref.shape[0]):
        sums_ref[k] = tile


def half_rate(sums_ref, cells):
    total = sums_ref[0]
    for k in range(1, sums_ref.shape[0]):
        total = total + sums_ref[k]
    functional = jnp.sum(total[0:1], axis=1, keepdims=True) / cells
    slope = jnp.sum(total[1:2], axis=1, keepdims=True) * 0.25 / cells
    return (0.5 * step_scale) * functional / (slope + 1e-6)


def first_kernel(
    core, face_xa, face_xb, face_za, face_zb, corner_a, corner_b, bp, fp, sums_ref, omega_ref
):
    _, cx, cz, ny = core.shape
    blocks = ny // LANES
    rows, lane = iotas()
    even_x, even_z = is_even("gx"), is_even("gz")
    x_first, x_all, z_first, z_all = own_place(cx, cz)
    top = BASE + cz

    def z_halos(plane, c, j, a, b):
        bp[c, plane, j, BASE - HALO : BASE, :] = jnp.where(even_z, b, a)
        bp[c, plane, j, top : top + HALO, :] = jnp.where(even_z, a, b)

    def own(x, _):
        for c in range(3):
            for j in range(blocks):
                cut = slice(j * LANES, (j + 1) * LANES)
                for z in range(0, cz, ROWS):
                    bp[c, x + HALO, j, BASE + z : BASE + z + ROWS, :] = core[c, x, z : z + ROWS, cut]
                z_halos(x + HALO, c, j, face_za[c, x, :, cut], face_zb[c, x, :, cut])
        return 0

    def rim(x, _):
        for c in range(3):
            for j in range(blocks):
                cut = slice(j * LANES, (j + 1) * LANES)
                for low, plane in ((True, x), (False, x + HALO + cx)):
                    use_a = even_x != low
                    for z in range(0, cz, ROWS):
                        bp[c, plane, j, BASE + z : BASE + z + ROWS, :] = jnp.where(
                            use_a, face_xa[c, x, z : z + ROWS, cut], face_xb[c, x, z : z + ROWS, cut]
                        )
                    corner = jnp.where(use_a, corner_a[c, x, :, cut], corner_b[c, x, :, cut])
                    z_halos(plane, c, j, corner[:HALO], corner[HALO:])
        return 0

    lax.fori_loop(0, cx, own, 0)
    lax.fori_loop(0, HALO, rim, 0)

    halo = HALO - 2
    descent_stages(bp, HALO, halo, cx, cz, blocks, omega_ref, lane)

    def plane(x, sums):
        functional, slope = sums
        own_x = (x >= halo) & (x < halo + cx)
        there = x_first + x - halo
        inside_x = (there >= 0) & (there < x_all)
        for r in windows(BASE - halo, BASE + cz + halo):
            height = rows + (r - BASE)
            owned = (height >= 0) & (height < cz) & own_x
            inside = (height + z_first >= 0) & (height + z_first < z_all) & inside_x
            for j, force, field, size, spread in doubled_force(bp, HALO - halo, omega_ref, x + 1, x, r, blocks, lane):
                functional = functional + jnp.where(owned, density_of(field, size, spread), 0.0)
                slope = slope + jnp.where(owned, dot(force, force), 0.0)
                for c in range(3):
                    fp[c, x, j, r : r + ROWS, :] = jnp.where(inside, force[c], 0.0)
        return functional, slope

    zero = jnp.zeros((ROWS, LANES), jnp.float32)
    functional, slope = lax.fori_loop(0, cx + 2 * halo, plane, (zero, zero))
    store_sums(sums_ref, functional, slope, rows)


def second_kernel(
    cells, bp0, fp0, sums0, friction, core_b, core_f, face_xa, face_xb, face_za, face_zb, totals, sums_ref, bp, omega_ref
):
    _, cx, cz, ny = core_b.shape
    blocks = ny // LANES
    rows, lane = iotas()
    even_x, even_z = is_even("gx"), is_even("gz")
    rate = half_rate(sums0, cells)
    halo = HALO - 2

    def step(x, _):
        for c in range(3):
            for j in range(blocks):
                for r in range(0, cz + 2 * BASE, ROWS):
                    bp[c, x, j, r : r + ROWS, :] = (
                        bp0[c, x + HALO - halo, j, r : r + ROWS, :] + rate * fp0[c, x, j, r : r + ROWS, :]
                    )
        return 0

    lax.fori_loop(0, cx + 2 * halo, step, 0)
    descent_stages(bp, halo, 0, cx, cz, blocks, omega_ref, lane)

    def plane(x, sums):
        functional, slope = sums
        for z in range(0, cz, ROWS):
            r = BASE + z
            for j, force, field, size, spread in doubled_force(bp, halo, omega_ref, x + 1, x, r, blocks, lane):
                cut = slice(j * LANES, (j + 1) * LANES)
                functional = functional + density_of(field, size, spread)
                slope = slope + dot(force, force)
                for c in range(3):
                    core_b[c, x, z : z + ROWS, cut] = field[c]
                    core_f[c, x, z : z + ROWS, cut] = force[c]
        for j in range(blocks):
            cut = slice(j * LANES, (j + 1) * LANES)
            for k, (source, c) in enumerate(((core_f, 0), (core_f, 1), (core_b, 0), (core_b, 1))):
                low, high = source[c, x, 0:HALO, cut], source[c, x, cz - HALO : cz, cut]
                face_za[k * cx + x, :, cut] = jnp.where(even_z, high, low)
                face_zb[k * cx + x, :, cut] = jnp.where(even_z, low, high)
                column = source[c, x, 0:ROWS, cut]
                for z in range(ROWS, cz, ROWS):
                    column = column + source[c, x, z : z + ROWS, cut]
                totals[k * cx + x, :, cut] = jnp.sum(column, axis=0, keepdims=True)
        return functional, slope

    zero = jnp.zeros((ROWS, LANES), jnp.float32)
    functional, slope = lax.fori_loop(0, cx, plane, (zero, zero))
    store_sums(sums_ref, functional, slope, rows)

    def faces(x, _):
        for j in range(blocks):
            cut = slice(j * LANES, (j + 1) * LANES)
            for k, (source, c) in enumerate(((core_f, 0), (core_f, 1), (core_b, 0), (core_b, 1))):
                for z in range(0, cz, ROWS):
                    low = source[c, x, z : z + ROWS, cut]
                    high = source[c, x + cx - HALO, z : z + ROWS, cut]
                    face_xa[k, x, z : z + ROWS, cut] = jnp.where(even_x, high, low)
                    face_xb[k, x, z : z + ROWS, cut] = jnp.where(even_x, low, high)
        return 0

    lax.fori_loop(0, HALO, faces, 0)
    for j in range(blocks):
        cut = slice(j * LANES, (j + 1) * LANES)
        low, high = friction[0:HALO], friction[cz - HALO : cz]
        face_za[4 * cx, :, cut] = jnp.where(even_z, high, low)
        face_zb[4 * cx, :, cut] = jnp.where(even_z, low, high)


def third_kernel(
    cells,
    core_b,
    core_f,
    sums0,
    friction,
    face_xa,
    face_xb,
    face_za,
    face_zb,
    above,
    corner_a,
    corner_b,
    relaxed,
    potential,
    ap,
    bm,
    an,
    rub,
):
    _, cx, cz, ny = core_b.shape
    blocks = ny // LANES
    rows, lane = iotas()
    even_x, even_z = is_even("gx"), is_even("gz")
    x_first, x_all, z_first, z_all = own_place(cx, cz)
    rate = half_rate(sums0, cells)
    top = BASE + cz

    rub[BASE:top] = friction[...]
    rub[BASE - HALO : BASE] = jnp.where(even_z, face_zb[4 * cx, :, :LANES], face_za[4 * cx, :, :LANES])
    rub[top : top + HALO] = jnp.where(even_z, face_za[4 * cx, :, :LANES], face_zb[4 * cx, :, :LANES])
    for r in range(0, cz + 2 * BASE, ROWS):
        height = rows + (r - BASE) + z_first
        inside = (height >= 0) & (height < z_all)
        rub[r : r + ROWS] = jnp.where(inside, time_step / rub[r : r + ROWS], 0.0)

    def suffix(value):
        for reach in (1, 2, 4):
            value = value + jnp.where(rows < ROWS - reach, pltpu.roll(value, ROWS - reach, 0), 0.0)
        return value

    def prefix(value):
        for reach in (1, 2, 4):
            value = value + jnp.where(rows >= reach, pltpu.roll(value, reach, 0), 0.0)
        return value

    def column(c, plane, j, low, own, high, beyond):
        sign = 1.0 if c == 0 else -1.0
        out = 1 - c
        ap[out, plane, j, top : top + HALO, :] = high
        value = ap[out, plane, j, top : top + ROWS, :]
        ap[out, plane, j, top : top + ROWS, :] = sign * (beyond - (prefix(value) - value))
        carry = beyond
        for z in reversed(range(0, cz, ROWS)):
            value = suffix(own[z // ROWS]) + carry
            ap[out, plane, j, BASE + z : BASE + z + ROWS, :] = sign * value
            carry = value[0:1]
        ap[out, plane, j, BASE - HALO : BASE, :] = low
        value = suffix(ap[out, plane, j, 0:BASE, :]) + carry
        ap[out, plane, j, 0:BASE, :] = jnp.where(z_first > 0, sign * value, 0.0)

    def own_plane(x, _):
        for j in range(blocks):
            cut = slice(j * LANES, (j + 1) * LANES)
            for c in range(3):
                own = [
                    core_b[c, x, z : z + ROWS, cut] + rate * core_f[c, x, z : z + ROWS, cut]
                    for z in range(0, cz, ROWS)
                ]
                for z in range(0, cz, ROWS):
                    relaxed[c, x, z : z + ROWS, cut] = own[z // ROWS]
                if c == 2:
                    continue
                a, b = [
                    face[(2 + c) * cx + x, :, cut] + rate * face[c * cx + x, :, cut] for face in (face_za, face_zb)
                ]
                beyond = above[(2 + c) * cx + x, :, cut] + rate * above[c * cx + x, :, cut]
                column(c, x + HALO, j, jnp.where(even_z, b, a), own, jnp.where(even_z, a, b), beyond)
        return 0

    lax.fori_loop(0, cx, own_plane, 0)

    def rim_plane(x, _):
        for j in range(blocks):
            cut = slice(j * LANES, (j + 1) * LANES)
            for low, plane in ((True, x), (False, x + HALO + cx)):
                use_a = even_x != low

                def picked(k, span):
                    return jnp.where(use_a, face_xa[k, x, span, cut], face_xb[k, x, span, cut])

                for c in range(2):
                    own = [
                        picked(2 + c, slice(z, z + ROWS)) + rate * picked(c, slice(z, z + ROWS))
                        for z in range(0, cz, ROWS)
                    ]
                    corner = [jnp.where(use_a, corner_a[k, x, :, cut], corner_b[k, x, :, cut]) for k in (2 + c, c)]
                    corner = corner[0] + rate * corner[1]
                    column(c, plane, j, corner[4:8], own, jnp.concatenate([corner[1:4], corner[3:4]], 0), corner[0:1])
        return 0

    lax.fori_loop(0, HALO, rim_plane, 0)

    def induced(a_ref, ax0, halo, flat):
        def plane(x, _):
            at = x + (ax0 - halo - 1)
            there = x_first + x - halo - 1
            inside_x = (there >= 0) & (there < x_all)
            for r in windows(BASE - halo - 1, top + halo + 1):
                height = rows + (r - BASE) + z_first
                inside = (height >= 0) & (height < z_all) & inside_x

                def ld(c, j, dx=0, dz=0):
                    return a_ref[c, at + dx, j, r + dz : r + dz + ROWS, :]

                dy = {c: y_diff([ld(c, j) for j in range(blocks)], lane) for c in ((0,) if flat else (0, 2))}
                for j in range(blocks):
                    curl_x = ld(1, j, dz=-1) - ld(1, j, dz=1)
                    curl_y = ld(0, j, dz=1) - ld(0, j, dz=-1)
                    curl_z = ld(1, j, dx=1) - ld(1, j, dx=-1) - dy[0][j]
                    if not flat:
                        curl_x = curl_x + dy[2][j]
                        curl_y = curl_y - (ld(2, j, dx=1) - ld(2, j, dx=-1))
                    for c, value in enumerate((curl_x, curl_y, curl_z)):
                        bm[c, x, j, r : r + ROWS, :] = jnp.where(inside, value, 0.0)
            return 0

        lax.fori_loop(0, cx + 2 * halo + 2, plane, 0)

    def pushed(x, r):
        def ld(c, j, dx=0, dz=0):
            return bm[c, x + dx, j, r + dz : r + dz + ROWS, :]

        dy = [y_diff([ld(c, j) for j in range(blocks)], lane) if c != 1 else None for c in range(3)]
        weight = rub[r : r + ROWS]
        for j in range(blocks):
            field = [ld(c, j) for c in range(3)]
            current = (
                dy[2][j] - (ld(1, j, dz=1) - ld(1, j, dz=-1)),
                (ld(0, j, dz=1) - ld(0, j, dz=-1)) - (ld(2, j, dx=1) - ld(2, j, dx=-1)),
                (ld(1, j, dx=1) - ld(1, j, dx=-1)) - dy[0][j],
            )
            square = dot(field, field)
            scale = weight * (0.0625 / jnp.maximum(0.25 * square, 1.0))
            both = dot(current, field)
            yield j, [scale * (field[c] * both - current[c] * square) for c in range(3)]

    halo = HALO - 2
    induced(ap, HALO, halo, True)

    def first_step(x, _):
        for r in windows(BASE - halo, top + halo):
            for j, change in pushed(x + 1, r):
                for c in range(2):
                    an[c, x, j, r : r + ROWS, :] = ap[c, x + HALO - halo, j, r : r + ROWS, :] + change[c]
                an[2, x, j, r : r + ROWS, :] = change[2]
        return 0

    lax.fori_loop(0, cx + 2 * halo, first_step, 0)
    induced(an, halo, 0, False)

    def last_step(x, _):
        for z in range(0, cz, ROWS):
            for j, change in pushed(x + 1, BASE + z):
                cut = slice(j * LANES, (j + 1) * LANES)
                for c in range(3):
                    potential[c, x, z : z + ROWS, cut] = (
                        an[c, x + halo, j, BASE + z : BASE + z + ROWS, :] + change[c]
                    )
        return 0

    lax.fori_loop(0, cx, last_step, 0)


def pack_kernel(*refs):
    *parts, face_za, face_zb, above, corner_a, corner_b = refs
    cx = above.shape[0] // 4
    even_x, even_z = is_even("gx"), is_even("gz")
    total = parts[0][...]
    for part in parts[1:]:
        total = total + part[...]
    above[...] = total

    def plane(x, _):
        for k in range(4):
            packed = []
            for at in (x, x + cx - HALO):
                a, b = face_za[k * cx + at], face_zb[k * cx + at]
                low, high = jnp.where(even_z, b, a), jnp.where(even_z, a, b)
                packed.append(jnp.concatenate([above[k * cx + at], high[0 : HALO - 1], low], axis=0))
            corner_a[k, x] = jnp.where(even_x, packed[1], packed[0])
            corner_b[k, x] = jnp.where(even_x, packed[0], packed[1])
        return 0

    lax.fori_loop(0, HALO, plane, 0)


def call(kernel, outs, *args, scratch=(), cost=0):
    shapes = [jax.ShapeDtypeStruct(shape, jnp.float32) for shape in outs]
    return pl.pallas_call(
        kernel,
        out_shape=shapes,
        in_specs=[pl.BlockSpec(memory_space=pltpu.VMEM)] * len(args),
        out_specs=[pl.BlockSpec(memory_space=pltpu.VMEM)] * len(outs),
        scratch_shapes=[pltpu.VMEM(shape, jnp.float32) for shape in scratch],
        compiler_params=pltpu.CompilerParams(vmem_limit_bytes=56 * 1024 * 1024),
        cost_estimate=pl.CostEstimate(flops=cost, bytes_accessed=cost // 10, transcendentals=0),
    )(*args)


def body(magnetic, friction):
    _, cx, cz, ny = magnetic.shape
    blocks = ny // LANES
    height = cz + 2 * BASE
    count_z, count_x = lax.axis_size("gz"), lax.axis_size("gx")
    devices = count_z * count_x
    cells = cx * cz * ny * devices
    work = cx * cz * ny * 200

    def padded(components, layers):
        return (components, cx + 2 * layers, blocks, height, LANES)

    tiles = (devices, ROWS, LANES)
    core = (3, cx, cz, ny)
    rubbed = jnp.broadcast_to(friction[:, None], (cz, LANES))

    faces_x = swapped(edges(magnetic, "gx", 1), "gx")
    faces_z = swapped(edges(magnetic, "gz", 2), "gz")
    corners = swapped(edges(jnp.concatenate(faces_z, axis=2), "gx", 1), "gx")
    bp, fp, sums = call(
        first_kernel,
        [padded(3, HALO), padded(3, HALO - 2), tiles],
        magnetic,
        *faces_x,
        *faces_z,
        *corners,
        scratch=[padded(11, HALO - 1)],
        cost=2 * work,
    )
    core_b, core_f, *faces, totals, sums = call(
        functools.partial(second_kernel, cells),
        [core, core, (4, HALO, cz, ny), (4, HALO, cz, ny), (4 * cx + 1, HALO, ny), (4 * cx + 1, HALO, ny), (4 * cx, 1, ny), tiles],
        bp,
        fp,
        shared(sums),
        rubbed,
        scratch=[padded(3, HALO - 2), padded(11, 1)],
        cost=work,
    )
    below = [
        lax.ppermute(totals, "gz", [(i, i - steps) for i in range(steps, count_z)]) for steps in range(1, count_z)
    ]
    faces_z = swapped(faces[2:], "gz")
    faces_x = swapped(faces[:2], "gx")
    sums = shared(sums)
    above, *corners = call(
        pack_kernel,
        [(4 * cx, 1, ny), (4, HALO, 2 * HALO, ny), (4, HALO, 2 * HALO, ny)],
        *below,
        *faces_z,
        cost=work // 50,
    )
    corners = swapped(corners, "gx")
    return tuple(
        call(
            functools.partial(third_kernel, cells),
            [core, core],
            core_b,
            core_f,
            sums,
            rubbed,
            *faces_x,
            *faces_z,
            above,
            *corners,
            scratch=[padded(2, HALO), padded(3, HALO - 1), padded(3, HALO - 2), (height, LANES)],
            cost=work,
        )
    )


def solution(mesh):
    return jax.shard_map(
        body,
        mesh=mesh,
        in_specs=(P(None, "gx", "gz", "runs"), P("gz")),
        out_specs=(P(None, "gx", "gz", "runs"), P(None, "gx", "gz", "runs")),
        check_vma=False,
    )
```

profile of v0, /device:TPU:0, one launch (start us, length us, event | category | flops | bytes accessed | tf_op | source)
XLA Modules:
  0.0 119.3 jit_solution(6019627539748137400)
XLA Ops:
  0.6 0.0 copy-start
  0.7 1.7 %constant_dynamic-slice_fusion = (f32[3,16,4,512]{3,2,1,0:T(4,128)S(1)}, f32[3,16,4,512]{3,2,1,0:T(4,128)S(1)}) fusion(f32[3,16,16,512]{3,2,1,0:T(8,128)} %core.1, s32[]{:T(128)S(6)} %select_n.39, s32[]{:T(128)S(6)} %select_n.38), kind=kLoop, calls=%fused_computation.6 | loop fusion | bytes 1572872 | tf_op jit(solution)/shard_map/dynamic_slice | solution.py:36
  2.3 0.7 collective-permute-start.3
  3.0 4.3 %collective-permute-start.2 = (f32[3,16,4,512]{3,2,1,0:T(4,128)S(1)}, f32[3,16,4,512]{3,2,1,0:T(4,128)S(1)}, u32[]{:S(2)}, u32[]{:S(2)}) collective-permute-start(f32[3,16,4,512]{3,2,1,0:T(4,128)S(1)} %get-tuple-element.31), channel_id=1, source_target_pairs={{0,4},{4,0},{8,12},{12,8},{1,5},{5,1},{9,13},{13,9},{2,6},{6,2},{1... | collective-permute-start | bytes 1179656 | tf_op jit(solution)/shard_map/ppermute | solution.py:42
  7.4 0.0 copy-done
  7.4 0.1 constant_dynamic-slice_fusion.2
  7.4 0.7 collective-permute-start.1
  8.1 4.4 %collective-permute-start = (f32[3,4,16,512]{3,2,1,0:T(8,128)S(1)}, f32[3,4,16,512]{3,2,1,0:T(8,128)S(1)}, u32[]{:S(2)}, u32[]{:S(2)}) collective-permute-start(f32[3,4,16,512]{3,2,1,0:T(8,128)S(1)} %get-tuple-element.33), channel_id=1, source_target_pairs={{0,1},{1,0},{2,3},{3,2},{4,5},{5,4},{6,7},{7,6},{8,9},{9,8},{10,11... | collective-permute-start | bytes 1179656 | tf_op jit(solution)/shard_map/ppermute | solution.py:42
  12.6 0.0 collective-permute-done.3.face_zb
  12.6 0.0 collective-permute-done.2.face_za
  12.6 0.0 copy-start.4
  12.6 0.1 fusion
  12.7 0.7 collective-permute-start.5
  13.4 0.0 copy-start.16
  13.4 1.8 %collective-permute-start.4 = (f32[3,4,8,512]{3,2,1,0:T(8,128)S(1)}, f32[3,4,8,512]{3,2,1,0:T(8,128)S(1)}, u32[]{:S(2)}, u32[]{:S(2)}) collective-permute-start(f32[3,4,8,512]{3,2,1,0:T(8,128)S(1)} %get-tuple-element.35), channel_id=1, source_target_pairs={{0,1},{1,0},{2,3},{3,2},{4,5},{5,4},{6,7},{7,6},{8,9},{9,8},{10,11... | collective-permute-start | bytes 589832 | tf_op jit(solution)/shard_map/ppermute | solution.py:42
  15.2 0.0 collective-permute-done.1.face_xb
  15.2 7.4 %collective-permute-done.face_xa = f32[3,4,16,512]{3,2,1,0:T(8,128)S(1)} collective-permute-done((f32[3,4,16,512]{3,2,1,0:T(8,128)S(1)}, f32[3,4,16,512]{3,2,1,0:T(8,128)S(1)}, u32[]{:S(2)}, u32[]{:S(2)}) %collective-permute-start) | collective-permute-done | bytes 393248 | tf_op jit(solution)/shard_map/ppermute | solution.py:42
  22.5 0.0 collective-permute-done.5.corner_b
  22.5 3.3 %collective-permute-done.4.corner_a = f32[3,4,8,512]{3,2,1,0:T(8,128)S(1)} collective-permute-done((f32[3,4,8,512]{3,2,1,0:T(8,128)S(1)}, f32[3,4,8,512]{3,2,1,0:T(8,128)S(1)}, u32[]{:S(2)}, u32[]{:S(2)}) %collective-permute-start.4) | collective-permute-done | bytes 196640 | tf_op jit(solution)/shard_map/ppermute | solution.py:42
  25.8 0.0 copy-done.3
  25.8 0.0 copy-done.4
  25.8 0.0 copy-done.7
  25.8 0.0 copy-done.8
  25.8 0.0 copy-done.11
  25.9 0.0 copy-start.12
  25.9 0.7 copy-done.12
  26.5 13.9 %shard_map.41 = (f32[3,24,4,32,128]{4,3,2,1,0:T(8,128)}, f32[3,20,4,32,128]{4,3,2,1,0:T(8,128)}, f32[16,8,128]{2,1,0:T(8,128)}) custom-call(f32[3,16,16,512]{3,2,1,0:T(8,128)} %core.1, f32[3,4,16,512]{3,2,1,0:T(8,128)} %copy-done.8, f32[3,4,16,512]{3,2,1,0:T(8,128)} %copy-done.7, f32[3,16,4,512]{3,2,1,0:T(4,128)} %copy-done.4, f32[3,16,4,512]{3,2,1,0:T(4,128)} %copy-done.3, ...), custom_call_target="tpu_custom_call" | custom-call | flops 52428800 | bytes 5242880 | tf_op jit(solution)/shard_map/pallas_call | solution.py:495
  40.4 10.7 %all_to_all.10.sums0 = f32[16,8,128]{2,1,0:T(8,128)} all-to-all(f32[16,8,128]{2,1,0:T(8,128)} %get-tuple-element.18), channel_id=1, replica_groups=mesh['runs'=2,'gz'=4,'gx'=4] {'gz','gx'}, dimensions={0} | all-to-all | bytes 131072 | tf_op jit(solution)/shard_map/all_to_all | solution.py:46
  51.2 0.0 copy-done.16
  51.2 0.7 broadcast_in_dim.2.friction
  51.8 13.4 %shard_map.42 = (f32[3,16,16,512]{3,2,1,0:T(8,128)}, f32[3,16,16,512]{3,2,1,0:T(8,128)}, f32[4,4,16,512]{3,2,1,0:T(8,128)}, f32[4,4,16,512]{3,2,1,0:T(8,128)}, f...) custom-call(f32[3,24,4,32,128]{4,3,2,1,0:T(8,128)} %get-tuple-element.16.bp0, ...), custom_call_target="tpu_custom_call" | custom-call | flops 26214400 | bytes 2621440 | tf_op jit(solution)/shard_map/pallas_call | solution.py:495
  65.2 0.1 collective-permute-start.8
  65.3 0.7 collective-permute-start.9
  66.0 1.3 %collective-permute-start.12 = (f32[64,1,512]{2,1,0:T(1,128)}, f32[64,1,512]{2,1,0:T(1,128)S(1)}, u32[]{:S(2)}, u32[]{:S(2)}) collective-permute-start(f32[64,1,512]{2,1,0:T(1,128)} %get-tuple-element.26), channel_id=1, source_target_pairs={{12,0},{13,1},{14,2},{15,3},{28,16},{29,17},{30,18},{31,19}} | collective-permute-start | bytes 393224 | tf_op jit(solution)/shard_map/ppermute | solution.py:546
  67.3 1.3 %collective-permute-start.11 = (f32[64,1,512]{2,1,0:T(1,128)}, f32[64,1,512]{2,1,0:T(1,128)S(1)}, u32[]{:S(2)}, u32[]{:S(2)}) collective-permute-start(f32[64,1,512]{2,1,0:T(1,128)} %get-tuple-element.26), channel_id=1, source_target_pairs={{8,0},{12,4},{9,1},{13,5},{10,2},{14,6},{11,3},{15,7},{24,16},{28,... | collective-permute-start | bytes 393224 | tf_op jit(solution)/shard_map/ppermute | solution.py:546
  68.6 0.4 collective-permute-start.6
  69.0 4.9 %collective-permute-done.12.refs_2_ = f32[64,1,512]{2,1,0:T(1,128)S(1)} collective-permute-done((f32[64,1,512]{2,1,0:T(1,128)}, f32[64,1,512]{2,1,0:T(1,128)S(1)}, u32[]{:S(2)}, u32[]{:S(2)}) %collective-permute-start.12) | collective-permute-done | bytes 131104 | tf_op jit(solution)/shard_map/ppermute | solution.py:546
  73.9 0.7 collective-permute-start.7
  74.6 6.3 %collective-permute-done.11.refs_1_ = f32[64,1,512]{2,1,0:T(1,128)S(1)} collective-permute-done((f32[64,1,512]{2,1,0:T(1,128)}, f32[64,1,512]{2,1,0:T(1,128)S(1)}, u32[]{:S(2)}, u32[]{:S(2)}) %collective-permute-start.11) | collective-permute-done | bytes 131104 | tf_op jit(solution)/shard_map/ppermute | solution.py:546
  80.9 1.3 %collective-permute-start.10 = (f32[64,1,512]{2,1,0:T(1,128)}, f32[64,1,512]{2,1,0:T(1,128)S(1)}, u32[]{:S(2)}, u32[]{:S(2)}) collective-permute-start(f32[64,1,512]{2,1,0:T(1,128)} %get-tuple-element.26), channel_id=1, source_target_pairs={{4,0},{8,4},{12,8},{5,1},{9,5},{13,9},{6,2},{10,6},{14,10},{7,3},{... | collective-permute-start | bytes 393224 | tf_op jit(solution)/shard_map/ppermute | solution.py:546
  82.2 2.2 %collective-permute-done.10.refs_0_ = f32[64,1,512]{2,1,0:T(1,128)S(1)} collective-permute-done((f32[64,1,512]{2,1,0:T(1,128)}, f32[64,1,512]{2,1,0:T(1,128)S(1)}, u32[]{:S(2)}, u32[]{:S(2)}) %collective-permute-start.10) | collective-permute-done | bytes 131104 | tf_op jit(solution)/shard_map/ppermute | solution.py:546
  84.3 0.0 collective-permute-done.8.refs_3_.face_za
  84.3 0.0 collective-permute-done.9.refs_4_.face_zb
  84.3 0.0 copy-done.13
  84.3 0.0 copy-done.14
  84.4 0.6 copy-done.15
  85.0 0.2 copy-done.1
  85.2 0.8 copy-done.2
  86.0 2.3 %shard_map.43 = (f32[64,1,512]{2,1,0:T(1,128)}, f32[4,4,8,512]{3,2,1,0:T(8,128)}, f32[4,4,8,512]{3,2,1,0:T(8,128)}) custom-call(f32[64,1,512]{2,1,0:T(1,128)} %copy-done.15, f32[64,1,512]{2,1,0:T(1,128)} %copy-done.14, f32[64,1,512]{2,1,0:T(1,128)} %copy-done.13, f32[65,4,512]{2,1,0:T(4,128)} %copy-done.1, f32[65,4,512]{2,1,0:T(4,128)} %copy-done.2), custom_call_target="tpu_custom_call" | custom-call | flops 524288 | bytes 52428 | tf_op jit(solution)/shard_map/pallas_call | solution.py:495
  88.3 0.3 collective-permute-start.13
  88.7 0.7 collective-permute-start.14
  89.3 12.9 %all_to_all.11.sums0 = f32[16,8,128]{2,1,0:T(8,128)} all-to-all(f32[16,8,128]{2,1,0:T(8,128)} %get-tuple-element.21), channel_id=1, replica_groups=mesh['runs'=2,'gz'=4,'gx'=4] {'gz','gx'}, dimensions={0} | all-to-all | bytes 131072 | tf_op jit(solution)/shard_map/all_to_all | solution.py:46
  102.2 0.0 collective-permute-done.6.face_xa
  102.2 0.0 collective-permute-done.7.face_xb
  102.2 0.0 copy-start.6
  102.2 0.0 collective-permute-done.13.corner_a
  102.2 0.0 copy-start.9
  102.2 0.0 collective-permute-done.14.corner_b
  102.3 0.0 copy-start.10
  102.3 0.7 copy-done.5
  103.0 0.2 copy-done.6
  103.2 0.1 copy-done.9
  103.3 0.1 copy-done.10
  103.4 16.0 %shard_map.44 = (f32[3,16,16,512]{3,2,1,0:T(8,128)}, f32[3,16,16,512]{3,2,1,0:T(8,128)}) custom-call(f32[3,16,16,512]{3,2,1,0:T(8,128)} %get-tuple-element.19.core_b, f32[3,16,16,512]{3,2,1,0:T(8,128)} %get-tuple-element.20.core_f, f32[16,8,128]{2,1,0:T(8,128)} %all_to_all.11.sums0, f32[16,128]{1,0:T(8,128)} %broadcast_in_dim.2.friction, ...), custom_call_target="tpu_custom_call" | custom-call | flops 26214400 | bytes 2621440 | tf_op jit(solution)/shard_map/pallas_call | solution.py:495
  (10 shorter events, 0.0 us)
Async XLA Ops:
  0.6 6.7 %copy-start = (f32[3,16,16,512]{3,2,1,0:T(8,128)S(1)}, f32[3,16,16,512]{3,2,1,0:T(8,128)}, u32[]{:S(2)}) copy-start(f32[3,16,16,512]{3,2,1,0:T(8,128)} %core.1) | copy-start | bytes 4718596
  2.3 10.2 %collective-permute-start.3 = (f32[3,16,4,512]{3,2,1,0:T(4,128)S(1)}, f32[3,16,4,512]{3,2,1,0:T(4,128)S(1)}, u32[]{:S(2)}, u32[]{:S(2)}) collective-permute-start(f32[3,16,4,512]{3,2,1,0:T(4,128)S(1)} %get-tuple-element.30), channel_id=1, source_target_pairs={{4,8},{8,4},{5,9},{9,5},{6,10},{10,6},{7,11},{11,7},{20,24},{24,20... | collective-permute-start | bytes 1179656 | tf_op jit(solution)/shard_map/ppermute | solution.py:42
  3.0 9.6 %collective-permute-start.2 = (f32[3,16,4,512]{3,2,1,0:T(4,128)S(1)}, f32[3,16,4,512]{3,2,1,0:T(4,128)S(1)}, u32[]{:S(2)}, u32[]{:S(2)}) collective-permute-start(f32[3,16,4,512]{3,2,1,0:T(4,128)S(1)} %get-tuple-element.31), channel_id=1, source_target_pairs={{0,4},{4,0},{8,12},{12,8},{1,5},{5,1},{9,13},{13,9},{2,6},{6,2},{1... | collective-permute-start | bytes 1179656 | tf_op jit(solution)/shard_map/ppermute | solution.py:42
  7.4 7.7 %collective-permute-start.1 = (f32[3,4,16,512]{3,2,1,0:T(8,128)S(1)}, f32[3,4,16,512]{3,2,1,0:T(8,128)S(1)}, u32[]{:S(2)}, u32[]{:S(2)}) collective-permute-start(f32[3,4,16,512]{3,2,1,0:T(8,128)S(1)} %get-tuple-element.32), channel_id=1, source_target_pairs={{1,2},{2,1},{5,6},{6,5},{9,10},{10,9},{13,14},{14,13},{17,18},{18,... | collective-permute-start | bytes 1179656 | tf_op jit(solution)/shard_map/ppermute | solution.py:42
  8.1 14.4 %collective-permute-start = (f32[3,4,16,512]{3,2,1,0:T(8,128)S(1)}, f32[3,4,16,512]{3,2,1,0:T(8,128)S(1)}, u32[]{:S(2)}, u32[]{:S(2)}) collective-permute-start(f32[3,4,16,512]{3,2,1,0:T(8,128)S(1)} %get-tuple-element.33), channel_id=1, source_target_pairs={{0,1},{1,0},{2,3},{3,2},{4,5},{5,4},{6,7},{7,6},{8,9},{9,8},{10,11... | collective-permute-start | bytes 1179656 | tf_op jit(solution)/shard_map/ppermute | solution.py:42
  12.6 13.3 %copy-start.3 = (f32[3,16,4,512]{3,2,1,0:T(4,128)}, f32[3,16,4,512]{3,2,1,0:T(4,128)S(1)}, u32[]{:S(2)}) copy-start(f32[3,16,4,512]{3,2,1,0:T(4,128)S(1)} %collective-permute-done.3.face_zb) | copy-start | bytes 1179652
  12.6 13.3 %copy-start.4 = (f32[3,16,4,512]{3,2,1,0:T(4,128)}, f32[3,16,4,512]{3,2,1,0:T(4,128)S(1)}, u32[]{:S(2)}) copy-start(f32[3,16,4,512]{3,2,1,0:T(4,128)S(1)} %collective-permute-done.2.face_za) | copy-start | bytes 1179652
  12.7 9.8 %collective-permute-start.5 = (f32[3,4,8,512]{3,2,1,0:T(8,128)S(1)}, f32[3,4,8,512]{3,2,1,0:T(8,128)S(1)}, u32[]{:S(2)}, u32[]{:S(2)}) collective-permute-start(f32[3,4,8,512]{3,2,1,0:T(8,128)S(1)} %get-tuple-element.34), channel_id=1, source_target_pairs={{1,2},{2,1},{5,6},{6,5},{9,10},{10,9},{13,14},{14,13},{17,18},{18,... | collective-permute-start | bytes 589832 | tf_op jit(solution)/shard_map/ppermute | solution.py:42
  13.4 37.8 %copy-start.16 = (f32[16]{0:T(128)S(1)}, f32[16]{0:T(128)}, u32[]{:S(2)}) copy-start(f32[16]{0:T(128)} %param.3) | copy-start | bytes 196
  13.4 12.4 %collective-permute-start.4 = (f32[3,4,8,512]{3,2,1,0:T(8,128)S(1)}, f32[3,4,8,512]{3,2,1,0:T(8,128)S(1)}, u32[]{:S(2)}, u32[]{:S(2)}) collective-permute-start(f32[3,4,8,512]{3,2,1,0:T(8,128)S(1)} %get-tuple-element.35), channel_id=1, source_target_pairs={{0,1},{1,0},{2,3},{3,2},{4,5},{5,4},{6,7},{7,6},{8,9},{9,8},{10,11... | collective-permute-start | bytes 589832 | tf_op jit(solution)/shard_map/ppermute | solution.py:42
  15.2 10.7 %copy-start.7 = (f32[3,4,16,512]{3,2,1,0:T(8,128)}, f32[3,4,16,512]{3,2,1,0:T(8,128)S(1)}, u32[]{:S(2)}) copy-start(f32[3,4,16,512]{3,2,1,0:T(8,128)S(1)} %collective-permute-done.1.face_xb) | copy-start | bytes 1179652
  22.5 3.3 %copy-start.8 = (f32[3,4,16,512]{3,2,1,0:T(8,128)}, f32[3,4,16,512]{3,2,1,0:T(8,128)S(1)}, u32[]{:S(2)}) copy-start(f32[3,4,16,512]{3,2,1,0:T(8,128)S(1)} %collective-permute-done.face_xa) | copy-start | bytes 1179652
  22.5 3.3 %copy-start.11 = (f32[3,4,8,512]{3,2,1,0:T(8,128)}, f32[3,4,8,512]{3,2,1,0:T(8,128)S(1)}, u32[]{:S(2)}) copy-start(f32[3,4,8,512]{3,2,1,0:T(8,128)S(1)} %collective-permute-done.5.corner_b) | copy-start | bytes 589828
  25.9 0.7 copy-start.12
  65.2 19.1 %collective-permute-start.8 = (f32[65,4,512]{2,1,0:T(4,128)}, f32[65,4,512]{2,1,0:T(4,128)S(1)}, u32[]{:S(2)}, u32[]{:S(2)}) collective-permute-start(f32[65,4,512]{2,1,0:T(4,128)} %get-tuple-element.24), channel_id=1, source_target_pairs={{0,4},{4,0},{8,12},{12,8},{1,5},{5,1},{9,13},{13,9},{2,6},{6,2},{1... | collective-permute-start | bytes 1597448 | tf_op jit(solution)/shard_map/ppermute | solution.py:42
  65.3 19.0 %collective-permute-start.9 = (f32[65,4,512]{2,1,0:T(4,128)}, f32[65,4,512]{2,1,0:T(4,128)S(1)}, u32[]{:S(2)}, u32[]{:S(2)}) collective-permute-start(f32[65,4,512]{2,1,0:T(4,128)} %get-tuple-element.25), channel_id=1, source_target_pairs={{4,8},{8,4},{5,9},{9,5},{6,10},{10,6},{7,11},{11,7},{20,24},{24,20... | collective-permute-start | bytes 1597448 | tf_op jit(solution)/shard_map/ppermute | solution.py:42
  66.0 7.9 %collective-permute-start.12 = (f32[64,1,512]{2,1,0:T(1,128)}, f32[64,1,512]{2,1,0:T(1,128)S(1)}, u32[]{:S(2)}, u32[]{:S(2)}) collective-permute-start(f32[64,1,512]{2,1,0:T(1,128)} %get-tuple-element.26), channel_id=1, source_target_pairs={{12,0},{13,1},{14,2},{15,3},{28,16},{29,17},{30,18},{31,19}} | collective-permute-start | bytes 393224 | tf_op jit(solution)/shard_map/ppermute | solution.py:546
  67.3 13.6 %collective-permute-start.11 = (f32[64,1,512]{2,1,0:T(1,128)}, f32[64,1,512]{2,1,0:T(1,128)S(1)}, u32[]{:S(2)}, u32[]{:S(2)}) collective-permute-start(f32[64,1,512]{2,1,0:T(1,128)} %get-tuple-element.26), channel_id=1, source_target_pairs={{8,0},{12,4},{9,1},{13,5},{10,2},{14,6},{11,3},{15,7},{24,16},{28,... | collective-permute-start | bytes 393224 | tf_op jit(solution)/shard_map/ppermute | solution.py:546
  68.6 33.6 %collective-permute-start.6 = (f32[4,4,16,512]{3,2,1,0:T(8,128)}, f32[4,4,16,512]{3,2,1,0:T(8,128)S(1)}, u32[]{:S(2)}, u32[]{:S(2)}) collective-permute-start(f32[4,4,16,512]{3,2,1,0:T(8,128)} %get-tuple-element.22), channel_id=1, source_target_pairs={{0,1},{1,0},{2,3},{3,2},{4,5},{5,4},{6,7},{7,6},{8,9},{9,8},{10,11... | collective-permute-start | bytes 1572872 | tf_op jit(solution)/shard_map/ppermute | solution.py:42
  73.9 10.4 %copy-start.13 = (f32[64,1,512]{2,1,0:T(1,128)}, f32[64,1,512]{2,1,0:T(1,128)S(1)}, u32[]{:S(2)}) copy-start(f32[64,1,512]{2,1,0:T(1,128)S(1)} %collective-permute-done.12.refs_2_) | copy-start | bytes 393220
  73.9 28.3 %collective-permute-start.7 = (f32[4,4,16,512]{3,2,1,0:T(8,128)}, f32[4,4,16,512]{3,2,1,0:T(8,128)S(1)}, u32[]{:S(2)}, u32[]{:S(2)}) collective-permute-start(f32[4,4,16,512]{3,2,1,0:T(8,128)} %get-tuple-element.23), channel_id=1, source_target_pairs={{1,2},{2,1},{5,6},{6,5},{9,10},{10,9},{13,14},{14,13},{17,18},{18,... | collective-permute-start | bytes 1572872 | tf_op jit(solution)/shard_map/ppermute | solution.py:42
  80.9 3.5 %copy-start.14 = (f32[64,1,512]{2,1,0:T(1,128)}, f32[64,1,512]{2,1,0:T(1,128)S(1)}, u32[]{:S(2)}) copy-start(f32[64,1,512]{2,1,0:T(1,128)S(1)} %collective-permute-done.11.refs_1_) | copy-start | bytes 393220
  80.9 3.4 %collective-permute-start.10 = (f32[64,1,512]{2,1,0:T(1,128)}, f32[64,1,512]{2,1,0:T(1,128)S(1)}, u32[]{:S(2)}, u32[]{:S(2)}) collective-permute-start(f32[64,1,512]{2,1,0:T(1,128)} %get-tuple-element.26), channel_id=1, source_target_pairs={{4,0},{8,4},{12,8},{5,1},{9,5},{13,9},{6,2},{10,6},{14,10},{7,3},{... | collective-permute-start | bytes 393224 | tf_op jit(solution)/shard_map/ppermute | solution.py:546
  84.3 0.7 copy-start.15
  84.3 0.8 copy-start.1
  85.2 0.8 copy-start.2
  88.3 13.9 %collective-permute-start.13 = (f32[4,4,8,512]{3,2,1,0:T(8,128)}, f32[4,4,8,512]{3,2,1,0:T(8,128)S(1)}, u32[]{:S(2)}, u32[]{:S(2)}) collective-permute-start(f32[4,4,8,512]{3,2,1,0:T(8,128)} %get-tuple-element.28), channel_id=1, source_target_pairs={{0,1},{1,0},{2,3},{3,2},{4,5},{5,4},{6,7},{7,6},{8,9},{9,8},{10,11... | collective-permute-start | bytes 786440 | tf_op jit(solution)/shard_map/ppermute | solution.py:42
  88.7 13.6 %collective-permute-start.14 = (f32[4,4,8,512]{3,2,1,0:T(8,128)}, f32[4,4,8,512]{3,2,1,0:T(8,128)S(1)}, u32[]{:S(2)}, u32[]{:S(2)}) collective-permute-start(f32[4,4,8,512]{3,2,1,0:T(8,128)} %get-tuple-element.29), channel_id=1, source_target_pairs={{1,2},{2,1},{5,6},{6,5},{9,10},{10,9},{13,14},{14,13},{17,18},{18,... | collective-permute-start | bytes 786440 | tf_op jit(solution)/shard_map/ppermute | solution.py:42
  102.2 0.8 copy-start.5
  102.2 1.0 copy-start.6
  102.2 1.0 copy-start.9
  102.3 1.1 copy-start.10
where the time goes:
time: 120 us; the launch traced here: 119 us
  Pallas kernels  45.5 us (38%)
  waiting for transfers between devices  24 us (20%)
  blocking collectives  23.6 us (20%)
  starting transfers between devices  19.4 us (16%)
  local copies, waits for them, and re-layouts  5.82 us (5%)
    pallas_call x4, Pallas kernels, call(): pl.pallas_call(kernel, out_shape=shapes, in_specs=[pl.BlockSpec(memory_sp...  45.5 us
    all_to_all x2, blocking collectives, shared(): return lax.all_to_all(tile_copies, ('gz', 'gx'), 0, 0)  23.6 us
    ppermute x3, waiting for transfers between devices, body(): lax.ppermute(totals, 'gz', [(i, i - steps) for i in range(steps, count_z)])  13.3 us
    ppermute x6, starting transfers between devices, swapped(): lax.ppermute(pair[0], axis, first)  11.4 us
    ppermute x6, waiting for transfers between devices, swapped(): lax.ppermute(pair[0], axis, first)  10.7 us
    ppermute x6, starting transfers between devices, swapped(): lax.ppermute(pair[1], axis, second)  4.08 us
    ppermute x3, starting transfers between devices, body(): lax.ppermute(totals, 'gz', [(i, i - steps) for i in range(steps, count_z)])  3.86 us
    unnamed x34, local copies, waits for them, and re-layouts  3.43 us
  transfers between devices with their start and end apart: 15, of which 5 were waited for; matrix products, arithmetic and copies ran while one was open for 0% of the time, Pallas kernels for 2%

commit v1 on v0

--- a/solution.py
+++ b/solution.py
@@ -19,10 +19,31 @@
 BASE = 8
 
 
-def pairings(count):
-    first = [(i, i ^ 1) for i in range(count) if i ^ 1 < count]
-    second = [(i, i + 1 if i % 2 else i - 1) for i in range(count)]
-    return first, [pair for pair in second if 0 <= pair[1] < count]
+AXES = ("runs", "gz", "gx")
+
+
+def pairings(axis):
+    sizes = [lax.axis_size(name) for name in AXES]
+    along = AXES.index(axis)
+    places = [(r, z, x) for r in range(sizes[0]) for z in range(sizes[1]) for x in range(sizes[2])]
+
+    def flat(place):
+        return (place[0] * sizes[1] + place[1]) * sizes[2] + place[2]
+
+    def moved(place, name, to):
+        return tuple(to if name == other else at for other, at in zip(AXES, place))
+
+    first, second = [], []
+    for place in places:
+        at = place[along]
+        if at ^ 1 < sizes[along]:
+            first.append((flat(place), flat(moved(place, axis, at ^ 1))))
+        to = at + 1 if at % 2 else at - 1
+        if 0 <= to < sizes[along]:
+            second.append((flat(place), flat(moved(place, axis, to))))
+        elif sizes[0] % 2 == 0:
+            second.append((flat(place), flat(moved(place, "runs", place[0] ^ 1))))
+    return first, second
 
 
 def is_even(axis):
@@ -38,23 +59,42 @@
 
 
 def swapped(pair, axis):
-    first, second = pairings(lax.axis_size(axis))
-    return lax.ppermute(pair[0], axis, first), lax.ppermute(pair[1], axis, second)
+    first, second = pairings(axis)
+    return lax.ppermute(pair[0], AXES, first), lax.ppermute(pair[1], AXES, second)
+
+
+def sorted_out(axis, first, second):
+    at = lax.axis_index(axis)
+    even = at % 2 == 0
+    low = jnp.where(at > 0, jnp.where(even, second, first), 0.0)
+    high = jnp.where(at < lax.axis_size(axis) - 1, jnp.where(even, first, second), 0.0)
+    return low, high
 
 
 def shared(tile_copies):
     return lax.all_to_all(tile_copies, ("gz", "gx"), 0, 0)
 
 
-def y_diff(blocks, lane):
-    count = len(blocks)
-    after = [pltpu.roll(b, LANES - 1, 1) for b in blocks]
-    before = [pltpu.roll(b, 1, 1) for b in blocks]
-    return [
-        jnp.where(lane == LANES - 1, after[(j + 1) % count], after[j])
-        - jnp.where(lane == 0, before[(j - 1) % count], before[j])
-        for j in range(count)
-    ]
+def y_diff(blocks):
+    wide = [pltpu.roll(blocks[-1], 1, 1), *blocks, pltpu.roll(blocks[0], LANES - 1, 1)]
+    return [wide[j + 2] - wide[j] for j in range(len(blocks))]
+
+
+def dealing(ny, back):
+    blocks = ny // LANES
+    source = lax.broadcasted_iota(jnp.int32, (ny, ny), 0)
+    target = lax.broadcasted_iota(jnp.int32, (ny, ny), 1)
+    if back:
+        source, target = target, source
+    return ((target % LANES) * blocks + target // LANES == source).astype(jnp.bfloat16)
+
+
+def dealt(value, matrix):
+    rows = value.shape[0]
+    high = value.astype(jnp.bfloat16)
+    rest = (value - high.astype(jnp.float32)).astype(jnp.bfloat16)
+    both = jnp.dot(jnp.concatenate([high, rest], axis=0), matrix, preferred_element_type=jnp.float32)
+    return both[:rows] + both[rows:]
 
 
 def cross(a, b):
@@ -65,11 +105,8 @@
     return a[0] * b[0] + a[1] * b[1] + a[2] * b[2]
 
 
-def iotas():
-    return (
-        lax.broadcasted_iota(jnp.int32, (ROWS, LANES), 0),
-        lax.broadcasted_iota(jnp.int32, (ROWS, LANES), 1),
-    )
+def row_index():
+    return lax.broadcasted_iota(jnp.int32, (ROWS, LANES), 0)
 
 
 def windows(low, high):
@@ -85,7 +122,7 @@
     )
 
 
-def descent_stages(bp, bx0, halo, cx, cz, blocks, omega_ref, lane):
+def descent_stages(bp, bx0, halo, cx, cz, blocks, omega_ref):
     planes = cx + 2 * halo + 2
 
     def plane(x, _):
@@ -94,7 +131,7 @@
             def ld(c, j, dx=0, dz=0):
                 return bp[c, at + dx, j, r + dz : r + dz + ROWS, :]
 
-            dy = [y_diff([ld(c, j) for j in range(blocks)], lane) for c in range(3)]
+            dy = [y_diff([ld(c, j) for j in range(blocks)]) for c in range(3)]
             for j in range(blocks):
                 field = [ld(c, j) for c in range(3)]
                 dx = [ld(c, j, dx=1) - ld(c, j, dx=-1) for c in range(3)]
@@ -114,11 +151,11 @@
     lax.fori_loop(0, planes, plane, 0)
 
 
-def doubled_force(bp, bx0, omega_ref, at, x, r, blocks, lane):
+def doubled_force(bp, bx0, omega_ref, at, x, r, blocks):
     def ld(k, j, dx=0, dz=0):
         return omega_ref[k, at + dx, j, r + dz : r + dz + ROWS, :]
 
-    dy = {k: y_diff([ld(k, j) for j in range(blocks)], lane) for k in (0, 2, 3)}
+    dy = {k: y_diff([ld(k, j) for j in range(blocks)]) for k in (0, 2, 3)}
     for j in range(blocks):
         field = [bp[c, x + bx0, j, r : r + ROWS, :] for c in range(3)]
         omega = [ld(4 + c, j) for c in range(3)]
@@ -161,19 +198,38 @@
     return (0.5 * step_scale) * functional / (slope + 1e-6)
 
 
+def entry_kernel(magnetic, core, face_xa, face_xb, face_za, face_zb, held, arrived):
+    _, cx, cz, ny = magnetic.shape
+    even_x, even_z = is_even("gx"), is_even("gz")
+    copies = [pltpu.make_async_copy(magnetic.at[c], held.at[c], arrived.at[c]) for c in range(3)]
+    for copy in copies:
+        copy.start()
+    matrix = dealing(ny, False)
+    for c in range(3):
+        copies[c].wait()
+        value = dealt(held[c].reshape(cx * cz, ny), matrix).reshape(cx, cz, ny)
+        core[c] = value
+        low, high = value[:HALO], value[cx - HALO :]
+        face_xa[c] = jnp.where(even_x, high, low)
+        face_xb[c] = jnp.where(even_x, low, high)
+        low, high = value[:, :HALO], value[:, cz - HALO :]
+        face_za[c] = jnp.where(even_z, high, low)
+        face_zb[c] = jnp.where(even_z, low, high)
+
+
 def first_kernel(
     core, face_xa, face_xb, face_za, face_zb, corner_a, corner_b, bp, fp, sums_ref, omega_ref
 ):
     _, cx, cz, ny = core.shape
     blocks = ny // LANES
-    rows, lane = iotas()
-    even_x, even_z = is_even("gx"), is_even("gz")
+    rows = row_index()
     x_first, x_all, z_first, z_all = own_place(cx, cz)
     top = BASE + cz
 
     def z_halos(plane, c, j, a, b):
-        bp[c, plane, j, BASE - HALO : BASE, :] = jnp.where(even_z, b, a)
-        bp[c, plane, j, top : top + HALO, :] = jnp.where(even_z, a, b)
+        low, high = sorted_out("gz", a, b)
+        bp[c, plane, j, BASE - HALO : BASE, :] = low
+        bp[c, plane, j, top : top + HALO, :] = high
 
     def own(x, _):
         for c in range(3):
@@ -188,21 +244,22 @@
         for c in range(3):
             for j in range(blocks):
                 cut = slice(j * LANES, (j + 1) * LANES)
-                for low, plane in ((True, x), (False, x + HALO + cx)):
-                    use_a = even_x != low
-                    for z in range(0, cz, ROWS):
-                        bp[c, plane, j, BASE + z : BASE + z + ROWS, :] = jnp.where(
-                            use_a, face_xa[c, x, z : z + ROWS, cut], face_xb[c, x, z : z + ROWS, cut]
-                        )
-                    corner = jnp.where(use_a, corner_a[c, x, :, cut], corner_b[c, x, :, cut])
-                    z_halos(plane, c, j, corner[:HALO], corner[HALO:])
+                planes = (x, x + HALO + cx)
+                for z in range(0, cz, ROWS):
+                    span = slice(z, z + ROWS)
+                    both = sorted_out("gx", face_xa[c, x, span, cut], face_xb[c, x, span, cut])
+                    for plane, value in zip(planes, both):
+                        bp[c, plane, j, BASE + z : BASE + z + ROWS, :] = value
+                both = sorted_out("gx", corner_a[c, x, :, cut], corner_b[c, x, :, cut])
+                for plane, value in zip(planes, both):
+                    z_halos(plane, c, j, value[:HALO], value[HALO:])
         return 0
 
     lax.fori_loop(0, cx, own, 0)
     lax.fori_loop(0, HALO, rim, 0)
 
     halo = HALO - 2
-    descent_stages(bp, HALO, halo, cx, cz, blocks, omega_ref, lane)
+    descent_stages(bp, HALO, halo, cx, cz, blocks, omega_ref)
 
     def plane(x, sums):
         functional, slope = sums
@@ -213,7 +270,7 @@
             height = rows + (r - BASE)
             owned = (height >= 0) & (height < cz) & own_x
             inside = (height + z_first >= 0) & (height + z_first < z_all) & inside_x
-            for j, force, field, size, spread in doubled_force(bp, HALO - halo, omega_ref, x + 1, x, r, blocks, lane):
+            for j, force, field, size, spread in doubled_force(bp, HALO - halo, omega_ref, x + 1, x, r, blocks):
                 functional = functional + jnp.where(owned, density_of(field, size, spread), 0.0)
                 slope = slope + jnp.where(owned, dot(force, force), 0.0)
                 for c in range(3):
@@ -221,16 +278,16 @@
         return functional, slope
 
     zero = jnp.zeros((ROWS, LANES), jnp.float32)
-    functional, slope = lax.fori_loop(0, cx + 2 * halo, plane, (zero, zero))
+    functional, slope = lax.fori_loop(0, cx + 2 * halo, plane, (zero, zero), unroll=4)
     store_sums(sums_ref, functional, slope, rows)
 
 
 def second_kernel(
-    cells, bp0, fp0, sums0, friction, core_b, core_f, face_xa, face_xb, face_za, face_zb, totals, sums_ref, bp, omega_ref
+    cells, bp0, fp0, sums0, friction, core_b, core_f, face_xa, face_xb, face_za, face_zb, sums_ref, bp, omega_ref
 ):
     _, cx, cz, ny = core_b.shape
     blocks = ny // LANES
-    rows, lane = iotas()
+    rows = row_index()
     even_x, even_z = is_even("gx"), is_even("gz")
     rate = half_rate(sums0, cells)
     halo = HALO - 2
@@ -244,14 +301,14 @@
                     )
         return 0
 
-    lax.fori_loop(0, cx + 2 * halo, step, 0)
-    descent_stages(bp, halo, 0, cx, cz, blocks, omega_ref, lane)
+    lax.fori_loop(0, cx + 2 * halo, step, 0, unroll=2)
+    descent_stages(bp, halo, 0, cx, cz, blocks, omega_ref)
 
     def plane(x, sums):
         functional, slope = sums
         for z in range(0, cz, ROWS):
             r = BASE + z
-            for j, force, field, size, spread in doubled_force(bp, halo, omega_ref, x + 1, x, r, blocks, lane):
+            for j, force, field, size, spread in doubled_force(bp, halo, omega_ref, x + 1, x, r, blocks):
                 cut = slice(j * LANES, (j + 1) * LANES)
                 functional = functional + density_of(field, size, spread)
                 slope = slope + dot(force, force)
@@ -267,11 +324,11 @@
                 column = source[c, x, 0:ROWS, cut]
                 for z in range(ROWS, cz, ROWS):
                     column = column + source[c, x, z : z + ROWS, cut]
-                totals[k * cx + x, :, cut] = jnp.sum(column, axis=0, keepdims=True)
+                face_za[4 * cx + 1 + x, k : k + 1, cut] = jnp.sum(column, axis=0, keepdims=True)
         return functional, slope
 
     zero = jnp.zeros((ROWS, LANES), jnp.float32)
-    functional, slope = lax.fori_loop(0, cx, plane, (zero, zero))
+    functional, slope = lax.fori_loop(0, cx, plane, (zero, zero), unroll=4)
     store_sums(sums_ref, functional, slope, rows)
 
     def faces(x, _):
@@ -315,15 +372,15 @@
 ):
     _, cx, cz, ny = core_b.shape
     blocks = ny // LANES
-    rows, lane = iotas()
-    even_x, even_z = is_even("gx"), is_even("gz")
+    rows = row_index()
     x_first, x_all, z_first, z_all = own_place(cx, cz)
     rate = half_rate(sums0, cells)
     top = BASE + cz
 
     rub[BASE:top] = friction[...]
-    rub[BASE - HALO : BASE] = jnp.where(even_z, face_zb[4 * cx, :, :LANES], face_za[4 * cx, :, :LANES])
-    rub[top : top + HALO] = jnp.where(even_z, face_za[4 * cx, :, :LANES], face_zb[4 * cx, :, :LANES])
+    low, high = sorted_out("gz", face_za[4 * cx, :, :LANES], face_zb[4 * cx, :, :LANES])
+    rub[BASE - HALO : BASE] = low
+    rub[top : top + HALO] = high
     for r in range(0, cz + 2 * BASE, ROWS):
         height = rows + (r - BASE) + z_first
         inside = (height >= 0) & (height < z_all)
@@ -369,29 +426,26 @@
                 a, b = [
                     face[(2 + c) * cx + x, :, cut] + rate * face[c * cx + x, :, cut] for face in (face_za, face_zb)
                 ]
-                beyond = above[(2 + c) * cx + x, :, cut] + rate * above[c * cx + x, :, cut]
-                column(c, x + HALO, j, jnp.where(even_z, b, a), own, jnp.where(even_z, a, b), beyond)
-        return 0
-
-    lax.fori_loop(0, cx, own_plane, 0)
+                low, high = sorted_out("gz", a, b)
+                column(c, x + HALO, j, low, own, high, above[x, c : c + 1, cut])
+        return 0
+
+    lax.fori_loop(0, cx, own_plane, 0, unroll=2)
 
     def rim_plane(x, _):
         for j in range(blocks):
             cut = slice(j * LANES, (j + 1) * LANES)
-            for low, plane in ((True, x), (False, x + HALO + cx)):
-                use_a = even_x != low
-
-                def picked(k, span):
-                    return jnp.where(use_a, face_xa[k, x, span, cut], face_xb[k, x, span, cut])
-
-                for c in range(2):
-                    own = [
-                        picked(2 + c, slice(z, z + ROWS)) + rate * picked(c, slice(z, z + ROWS))
-                        for z in range(0, cz, ROWS)
-                    ]
-                    corner = [jnp.where(use_a, corner_a[k, x, :, cut], corner_b[k, x, :, cut]) for k in (2 + c, c)]
-                    corner = corner[0] + rate * corner[1]
-                    column(c, plane, j, corner[4:8], own, jnp.concatenate([corner[1:4], corner[3:4]], 0), corner[0:1])
+            for c in range(2):
+                own = []
+                for z in range(0, cz, ROWS):
+                    span = slice(z, z + ROWS)
+                    a, b = [face[2 + c, x, span, cut] + rate * face[c, x, span, cut] for face in (face_xa, face_xb)]
+                    own.append(sorted_out("gx", a, b))
+                corners = sorted_out("gx", corner_a[c, x, :, cut], corner_b[c, x, :, cut])
+                for side, plane in enumerate((x, x + HALO + cx)):
+                    corner = corners[side]
+                    high = jnp.concatenate([corner[1:4], corner[3:4]], 0)
+                    column(c, plane, j, corner[4:8], [pair[side] for pair in own], high, corner[0:1])
         return 0
 
     lax.fori_loop(0, HALO, rim_plane, 0)
@@ -408,7 +462,7 @@
                 def ld(c, j, dx=0, dz=0):
                     return a_ref[c, at + dx, j, r + dz : r + dz + ROWS, :]
 
-                dy = {c: y_diff([ld(c, j) for j in range(blocks)], lane) for c in ((0,) if flat else (0, 2))}
+                dy = {c: y_diff([ld(c, j) for j in range(blocks)]) for c in ((0,) if flat else (0, 2))}
                 for j in range(blocks):
                     curl_x = ld(1, j, dz=-1) - ld(1, j, dz=1)
                     curl_y = ld(0, j, dz=1) - ld(0, j, dz=-1)
@@ -420,13 +474,13 @@
                         bm[c, x, j, r : r + ROWS, :] = jnp.where(inside, value, 0.0)
             return 0
 
-        lax.fori_loop(0, cx + 2 * halo + 2, plane, 0)
+        lax.fori_loop(0, cx + 2 * halo + 2, plane, 0, unroll=6)
 
     def pushed(x, r):
         def ld(c, j, dx=0, dz=0):
             return bm[c, x + dx, j, r + dz : r + dz + ROWS, :]
 
-        dy = [y_diff([ld(c, j) for j in range(blocks)], lane) if c != 1 else None for c in range(3)]
+        dy = [y_diff([ld(c, j) for j in range(blocks)]) if c != 1 else None for c in range(3)]
         weight = rub[r : r + ROWS]
         for j in range(blocks):
             field = [ld(c, j) for c in range(3)]
@@ -451,7 +505,7 @@
                 an[2, x, j, r : r + ROWS, :] = change[2]
         return 0
 
-    lax.fori_loop(0, cx + 2 * halo, first_step, 0)
+    lax.fori_loop(0, cx + 2 * halo, first_step, 0, unroll=2)
     induced(an, halo, 0, False)
 
     def last_step(x, _):
@@ -464,41 +518,53 @@
                     )
         return 0
 
-    lax.fori_loop(0, cx, last_step, 0)
-
-
-def pack_kernel(*refs):
-    *parts, face_za, face_zb, above, corner_a, corner_b = refs
-    cx = above.shape[0] // 4
-    even_x, even_z = is_even("gx"), is_even("gz")
-    total = parts[0][...]
-    for part in parts[1:]:
-        total = total + part[...]
-    above[...] = total
+    lax.fori_loop(0, cx, last_step, 0, unroll=2)
+    matrix = dealing(ny, True)
+    for out in (relaxed, potential):
+        out[...] = dealt(out[...].reshape(3 * cx * cz, ny), matrix).reshape(3, cx, cz, ny)
+
+
+def pack_kernel(cells, count, *refs):
+    columns, (face_za, face_zb, sums0, above, corner_a, corner_b) = refs[:count], refs[count:]
+    cx = above.shape[0]
+    even_x = is_even("gx")
+    place = lax.axis_index("gz")
+    rate = half_rate(sums0, cells)
+
+    def total(x, _):
+        column = jnp.zeros(columns[0].shape[1:], jnp.float32)
+        for level, part in enumerate(columns):
+            column = column + jnp.where((place >> level) % 2 == 0, part[x], 0.0)
+        above[x] = column[2:4] + rate * column[0:2]
+        return 0
+
+    lax.fori_loop(0, cx, total, 0)
 
     def plane(x, _):
-        for k in range(4):
+        for c in range(2):
             packed = []
             for at in (x, x + cx - HALO):
-                a, b = face_za[k * cx + at], face_zb[k * cx + at]
-                low, high = jnp.where(even_z, b, a), jnp.where(even_z, a, b)
-                packed.append(jnp.concatenate([above[k * cx + at], high[0 : HALO - 1], low], axis=0))
-            corner_a[k, x] = jnp.where(even_x, packed[1], packed[0])
-            corner_b[k, x] = jnp.where(even_x, packed[0], packed[1])
+                a, b = [face[(2 + c) * cx + at] + rate * face[c * cx + at] for face in (face_za, face_zb)]
+                low, high = sorted_out("gz", a, b)
+                packed.append(jnp.concatenate([above[at, c : c + 1], high[0 : HALO - 1], low], axis=0))
+            corner_a[c, x] = jnp.where(even_x, packed[1], packed[0])
+            corner_b[c, x] = jnp.where(even_x, packed[0], packed[1])
         return 0
 
     lax.fori_loop(0, HALO, plane, 0)
 
 
-def call(kernel, outs, *args, scratch=(), cost=0):
+def call(kernel, outs, *args, scratch=(), cost=0, limit=8, outside=0):
     shapes = [jax.ShapeDtypeStruct(shape, jnp.float32) for shape in outs]
     return pl.pallas_call(
         kernel,
         out_shape=shapes,
-        in_specs=[pl.BlockSpec(memory_space=pltpu.VMEM)] * len(args),
+        in_specs=[
+            pl.BlockSpec(memory_space=pltpu.HBM if k < outside else pltpu.VMEM) for k in range(len(args))
+        ],
         out_specs=[pl.BlockSpec(memory_space=pltpu.VMEM)] * len(outs),
-        scratch_shapes=[pltpu.VMEM(shape, jnp.float32) for shape in scratch],
-        compiler_params=pltpu.CompilerParams(vmem_limit_bytes=56 * 1024 * 1024),
+        scratch_shapes=[pltpu.VMEM(item, jnp.float32) if isinstance(item, tuple) else item for item in scratch],
+        compiler_params=pltpu.CompilerParams(vmem_limit_bytes=limit * 1024 * 1024),
         cost_estimate=pl.CostEstimate(flops=cost, bytes_accessed=cost // 10, transcendentals=0),
     )(*args)
 
@@ -519,8 +585,17 @@
     core = (3, cx, cz, ny)
     rubbed = jnp.broadcast_to(friction[:, None], (cz, LANES))
 
-    faces_x = swapped(edges(magnetic, "gx", 1), "gx")
-    faces_z = swapped(edges(magnetic, "gz", 2), "gz")
+    magnetic, *faces = call(
+        entry_kernel,
+        [core, *[(3, HALO, cz, ny)] * 2, *[(3, cx, HALO, ny)] * 2],
+        magnetic,
+        scratch=[core, pltpu.SemaphoreType.DMA((3,))],
+        outside=1,
+        cost=work,
+        limit=16,
+    )
+    faces_x = swapped(faces[:2], "gx")
+    faces_z = swapped(faces[2:], "gz")
     corners = swapped(edges(jnp.concatenate(faces_z, axis=2), "gx", 1), "gx")
     bp, fp, sums = call(
         first_kernel,
@@ -531,28 +606,36 @@
         *corners,
         scratch=[padded(11, HALO - 1)],
         cost=2 * work,
+        limit=18,
     )
-    core_b, core_f, *faces, totals, sums = call(
+    core_b, core_f, *faces, sums = call(
         functools.partial(second_kernel, cells),
-        [core, core, (4, HALO, cz, ny), (4, HALO, cz, ny), (4 * cx + 1, HALO, ny), (4 * cx + 1, HALO, ny), (4 * cx, 1, ny), tiles],
+        [core, core, (4, HALO, cz, ny), (4, HALO, cz, ny), (5 * cx + 1, HALO, ny), (4 * cx + 1, HALO, ny), tiles],
         bp,
         fp,
         shared(sums),
         rubbed,
         scratch=[padded(3, HALO - 2), padded(11, 1)],
         cost=work,
+        limit=19,
     )
-    below = [
-        lax.ppermute(totals, "gz", [(i, i - steps) for i in range(steps, count_z)]) for steps in range(1, count_z)
-    ]
     faces_z = swapped(faces[2:], "gz")
     faces_x = swapped(faces[:2], "gx")
     sums = shared(sums)
+    columns = [faces_z[0][4 * cx + 1 :]]
+    group = faces[2][4 * cx + 1 :] + columns[0]
+    stride = 2
+    while stride < count_z:
+        columns.append(lax.ppermute(group, "gz", [(i, i ^ stride) for i in range(count_z)]))
+        stride *= 2
+        if stride < count_z:
+            group = group + columns[-1]
     above, *corners = call(
-        pack_kernel,
-        [(4 * cx, 1, ny), (4, HALO, 2 * HALO, ny), (4, HALO, 2 * HALO, ny)],
-        *below,
+        functools.partial(pack_kernel, cells, len(columns)),
+        [(cx, 2, ny), (2, HALO, 2 * HALO, ny), (2, HALO, 2 * HALO, ny)],
+        *columns,
         *faces_z,
+        sums,
         cost=work // 50,
     )
     corners = swapped(corners, "gx")
@@ -570,6 +653,7 @@
             *corners,
             scratch=[padded(2, HALO), padded(3, HALO - 1), padded(3, HALO - 2), (height, LANES)],
             cost=work,
+            limit=16,
         )
     )
 

time: 120 us -> 84.7 us (0.71)
  Pallas kernels: 45.5 us -> 24.6 us
  starting transfers between devices: 19.4 us -> 13.2 us
  waiting for transfers between devices: 24 us -> 18.6 us
  local copies, waits for them, and re-layouts: 5.82 us -> 1.47 us
  blocking collectives: 23.6 us -> 25.8 us
    pallas_call x4 -> x5, Pallas kernels: 45.5 us -> 24.6 us  [call(): pl.pallas_call(kernel, out_shape=shapes, in_specs=[pl.BlockSpec(memory_sp...]
    ppermute x15 -> x13, starting transfers between devices: 19.4 us -> 13.2 us  [the longest x6 8.2 us: swapped(): lax.ppermute(pair[1], AXES, second)]
    ppermute x15 -> x13, waiting for transfers between devices: 24 us -> 18.6 us  [the longest x6 13.3 us: swapped(): lax.ppermute(pair[1], AXES, second)]
    all_to_all x2, blocking collectives: 23.6 us -> 25.8 us  [shared(): return lax.all_to_all(tile_copies, ('gz', 'gx'), 0, 0)]
    unnamed x34 -> x4, local copies, waits for them, and re-layouts: 3.43 us -> 1.4 us
    dynamic_slice x2 -> x0, local copies, waits for them, and re-layouts: 1.72 us -> none  [edges(): second = lax.dynamic_slice_in_dim(cells, jnp.where(even, 0, far), HALO, dim)]
  transfers between devices with their start and end apart: 15 -> 13, of which waited for: 5 -> 7; matrix products, arithmetic and copies ran while one was open for 0% -> 0% of each run, Pallas kernels for 2% -> 1%
where the time goes in v1:
time: 84.7 us; the launch traced here: 84.5 us
  blocking collectives  25.8 us (30%)
  Pallas kernels  24.6 us (29%)
  waiting for transfers between devices  18.6 us (22%)
  starting transfers between devices  13.2 us (16%)
  local copies, waits for them, and re-layouts  1.47 us (2%)
    all_to_all x2, blocking collectives, shared(): return lax.all_to_all(tile_copies, ('gz', 'gx'), 0, 0)  25.8 us
    pallas_call x5, Pallas kernels, call(): pl.pallas_call(kernel, out_shape=shapes, in_specs=[pl.BlockSpec(memory_sp...  24.6 us
    ppermute x6, waiting for transfers between devices, swapped(): lax.ppermute(pair[1], AXES, second)  13.3 us
    ppermute x6, starting transfers between devices, swapped(): lax.ppermute(pair[1], AXES, second)  8.2 us
    ppermute x6, waiting for transfers between devices, swapped(): lax.ppermute(pair[0], AXES, first)  5.29 us
    ppermute x6, starting transfers between devices, swapped(): lax.ppermute(pair[0], AXES, first)  3.42 us
  transfers between devices with their start and end apart: 13, of which 7 were waited for; matrix products, arithmetic and copies ran while one was open for 0% of the time, Pallas kernels for 1%

profile of v1, /device:TPU:0, one launch (start us, length us, event | category | flops | bytes accessed | tf_op | source)
XLA Modules:
  0.0 84.5 jit_solution(17188015354628125510)
XLA Ops:
  0.6 0.0 copy-start
  0.6 1.4 %copy-done = f32[3,16,16,512]{3,2,1,0:T(8,128)S(1)} copy-done((f32[3,16,16,512]{3,2,1,0:T(8,128)S(1)}, f32[3,16,16,512]{3,2,1,0:T(8,128)}, u32[]{:S(2)}) %copy-start) | copy-done | bytes 1572888
  2.0 2.7 %shard_map.41 = (f32[3,16,16,512]{3,2,1,0:T(8,128)S(1)}, f32[3,4,16,512]{3,2,1,0:T(8,128)}, f32[3,4,16,512]{3,2,1,0:T(8,128)S(1)}, f32[3,16,4,512]{3,2,1,0:T(4,128)}, f32[3,16,4,512]{3,2,1,0:T(4,128)}) custom-call(f32[3,16,16,512]{3,2,1,0:T(8,128)S(1)} %copy-done), custom_call_target="tpu_custom_call" | custom-call | flops 26214400 | bytes 2621440 | tf_op jit(solution)/shard_map/pallas_call | solution.py:559
  4.7 0.5 collective-permute-start.2
  5.2 2.6 %collective-permute-start.3 = (f32[3,16,4,512]{3,2,1,0:T(4,128)}, f32[3,16,4,512]{3,2,1,0:T(4,128)S(1)}, u32[]{:S(2)}, u32[]{:S(2)}) collective-permute-start(f32[3,16,4,512]{3,2,1,0:T(4,128)} %get-tuple-element.24), channel_id=1, source_target_pairs={{0,16},{1,17},{2,18},{3,19},{4,8},{5,9},{6,10},{7,11},{8,4},{9,5},... | collective-permute-start | bytes 1179656 | tf_op jit(solution)/shard_map/ppermute | solution.py:63
  7.8 1.6 %collective-permute-start = (f32[3,4,16,512]{3,2,1,0:T(8,128)}, f32[3,4,16,512]{3,2,1,0:T(8,128)S(1)}, u32[]{:S(2)}, u32[]{:S(2)}) collective-permute-start(f32[3,4,16,512]{3,2,1,0:T(8,128)} %get-tuple-element.21), channel_id=1, source_target_pairs={{0,1},{1,0},{2,3},{3,2},{4,5},{5,4},{6,7},{7,6},{8,9},{9,8},{10,11... | collective-permute-start | bytes 1179656 | tf_op jit(solution)/shard_map/ppermute | solution.py:63
  9.4 0.5 collective-permute-start.1
  9.9 0.0 collective-permute-done.2.face_za
  9.9 5.9 %collective-permute-done.3.face_zb = f32[3,16,4,512]{3,2,1,0:T(4,128)S(1)} collective-permute-done((f32[3,16,4,512]{3,2,1,0:T(4,128)}, f32[3,16,4,512]{3,2,1,0:T(4,128)S(1)}, u32[]{:S(2)}, u32[]{:S(2)}) %collective-permute-start.3) | collective-permute-done | bytes 393248 | tf_op jit(solution)/shard_map/ppermute | solution.py:63
  15.8 0.1 fusion
  15.9 2.4 %collective-permute-start.5 = (f32[3,4,8,512]{3,2,1,0:T(8,128)S(1)}, f32[3,4,8,512]{3,2,1,0:T(8,128)S(1)}, u32[]{:S(2)}, u32[]{:S(2)}) collective-permute-start(f32[3,4,8,512]{3,2,1,0:T(8,128)S(1)} %get-tuple-element.38), channel_id=1, source_target_pairs={{0,16},{1,2},{2,1},{3,19},{4,20},{5,6},{6,5},{7,23},{8,24},{9,10},... | collective-permute-start | bytes 589832 | tf_op jit(solution)/shard_map/ppermute | solution.py:63
  18.4 0.0 collective-permute-start.4
  18.4 1.4 %collective-permute-done.face_xa = f32[3,4,16,512]{3,2,1,0:T(8,128)S(1)} collective-permute-done((f32[3,4,16,512]{3,2,1,0:T(8,128)}, f32[3,4,16,512]{3,2,1,0:T(8,128)S(1)}, u32[]{:S(2)}, u32[]{:S(2)}) %collective-permute-start) | collective-permute-done | bytes 393248 | tf_op jit(solution)/shard_map/ppermute | solution.py:63
  19.8 4.4 %collective-permute-done.1.face_xb = f32[3,4,16,512]{3,2,1,0:T(8,128)S(1)} collective-permute-done((f32[3,4,16,512]{3,2,1,0:T(8,128)S(1)}, f32[3,4,16,512]{3,2,1,0:T(8,128)S(1)}, u32[]{:S(2)}, u32[]{:S(2)}) %collective-permute-start.1) | collective-permute-done | bytes 393248 | tf_op jit(solution)/shard_map/ppermute | solution.py:63
  24.1 2.3 %collective-permute-done.5.corner_b = f32[3,4,8,512]{3,2,1,0:T(8,128)S(1)} collective-permute-done((f32[3,4,8,512]{3,2,1,0:T(8,128)S(1)}, f32[3,4,8,512]{3,2,1,0:T(8,128)S(1)}, u32[]{:S(2)}, u32[]{:S(2)}) %collective-permute-start.5) | collective-permute-done | bytes 196640 | tf_op jit(solution)/shard_map/ppermute | solution.py:63
  26.4 0.0 collective-permute-done.4.corner_a
  26.4 0.0 copy-start.1
  26.4 6.5 %shard_map.42 = (f32[3,24,4,32,128]{4,3,2,1,0:T(8,128)S(1)}, f32[3,20,4,32,128]{4,3,2,1,0:T(8,128)S(1)}, f32[16,8,128]{2,1,0:T(8,128)S(1)}) custom-call(f32[3,16,16,512]{3,2,1,0:T(8,128)S(1)} %get-tuple-element.20.core, f32[3,4,16,512]{3,2,1,0:T(8,128)S(1)} %collective-permute-done.face_xa, f32[3,4,16,512]{3,2,1,0:T(8,128)S(1)} %collective-permute-done.1.face_xb, ...), custom_call_target="tpu_custom_call" | custom-call | flops 52428800 | bytes 5242880 | tf_op jit(solution)/shard_map/pallas_call | solution.py:559
  32.9 11.9 %all_to_all.10.sums0 = f32[16,8,128]{2,1,0:T(8,128)S(1)} all-to-all(f32[16,8,128]{2,1,0:T(8,128)S(1)} %get-tuple-element.27), channel_id=1, replica_groups=mesh['runs'=2,'gz'=4,'gx'=4] {'gz','gx'}, dimensions={0} | all-to-all | bytes 131072 | tf_op jit(solution)/shard_map/all_to_all | solution.py:75
  44.8 0.0 copy-done.1
  44.8 0.1 broadcast_in_dim.2.friction
  44.9 5.4 %shard_map.43 = (f32[3,16,16,512]{3,2,1,0:T(8,128)S(1)}, f32[3,16,16,512]{3,2,1,0:T(8,128)S(1)}, f32[4,4,16,512]{3,2,1,0:T(8,128)S(1)}, f32[4,4,16,512]{3,2,1,0:...) custom-call(f32[3,24,4,32,128]{4,3,2,1,0:T(8,128)S(1)} %get-tuple-element.25.bp0, ...), custom_call_target="tpu_custom_call" | custom-call | flops 26214400 | bytes 2621440 | tf_op jit(solution)/shard_map/pallas_call | solution.py:559
  50.4 0.2 collective-permute-start.8
  50.5 1.5 %collective-permute-start.9 = (f32[65,4,512]{2,1,0:T(4,128)S(1)}, f32[65,4,512]{2,1,0:T(4,128)S(1)}, u32[]{:S(2)}, u32[]{:S(2)}) collective-permute-start(f32[65,4,512]{2,1,0:T(4,128)S(1)} %get-tuple-element.34), channel_id=1, source_target_pairs={{0,16},{1,17},{2,18},{3,19},{4,8},{5,9},{6,10},{7,11},{8,4},{9,5},... | collective-permute-start | bytes 1597448 | tf_op jit(solution)/shard_map/ppermute | solution.py:63
  52.1 0.3 collective-permute-start.6
  52.4 0.5 collective-permute-start.7
  52.9 0.0 collective-permute-done.8.refs_2_.face_za
  53.0 1.6 %collective-permute-start.10 = (f32[16,4,512]{2,1,0:T(4,128)S(1)}, f32[16,4,512]{2,1,0:T(4,128)S(1)}, u32[]{:S(2)}, u32[]{:S(2)}) collective-permute-start(f32[16,4,512]{2,1,0:T(4,128)S(1)} %get-tuple-element.40), channel_id=1, source_target_pairs={{0,8},{4,12},{8,0},{12,4},{1,9},{5,13},{9,1},{13,5},{2,10},{6,14},... | collective-permute-start | bytes 393224 | tf_op jit(solution)/shard_map/ppermute | solution.py:629
  54.5 13.9 %all_to_all.11.refs_4_.sums0 = f32[16,8,128]{2,1,0:T(8,128)S(1)} all-to-all(f32[16,8,128]{2,1,0:T(8,128)S(1)} %get-tuple-element.30), channel_id=1, replica_groups=mesh['runs'=2,'gz'=4,'gx'=4] {'gz','gx'}, dimensions={0} | all-to-all | bytes 131072 | tf_op jit(solution)/shard_map/all_to_all | solution.py:75
  68.5 0.0 collective-permute-done.9.refs_3_.face_zb
  68.5 0.0 collective-permute-done.10.refs_1_
  68.5 0.8 %shard_map.44 = (f32[16,2,512]{2,1,0:T(2,128)S(1)}, f32[2,4,8,512]{3,2,1,0:T(8,128)S(1)}, f32[2,4,8,512]{3,2,1,0:T(8,128)S(1)}) custom-call(f32[16,4,512]{2,1,0:T(4,128)S(1)} %get-tuple-element.41.refs_0_, f32[16,4,512]{2,1,0:T(4,128)S(1)} %collective-permute-done.10.refs_1_, f32[81,4,512]{2,1,0:T(4,128)S(1)} %collective-permute-done.8.refs_2_.face_za, ...), custom_call_target="tpu_custom_call" | custom-call | flops 524288 | bytes 52428 | tf_op jit(solution)/shard_map/pallas_call | solution.py:559
  69.3 0.8 collective-permute-start.11
  70.1 0.6 collective-permute-start.12
  70.7 0.0 collective-permute-done.6.face_xa
  70.7 0.3 collective-permute-done.7.face_xb
  71.0 3.9 %collective-permute-done.11.corner_a = f32[2,4,8,512]{3,2,1,0:T(8,128)S(1)} collective-permute-done((f32[2,4,8,512]{3,2,1,0:T(8,128)S(1)}, f32[2,4,8,512]{3,2,1,0:T(8,128)S(1)}, u32[]{:S(2)}, u32[]{:S(2)}) %collective-permute-start.11) | collective-permute-done | bytes 131104 | tf_op jit(solution)/shard_map/ppermute | solution.py:63
  74.9 0.5 collective-permute-done.12.corner_b
  75.4 9.2 %shard_map.45 = (f32[3,16,16,512]{3,2,1,0:T(8,128)}, f32[3,16,16,512]{3,2,1,0:T(8,128)}) custom-call(f32[3,16,16,512]{3,2,1,0:T(8,128)S(1)} %get-tuple-element.28.core_b, f32[3,16,16,512]{3,2,1,0:T(8,128)S(1)} %get-tuple-element.29.core_f, f32[16,8,128]{2,1,0:T(8,128)S(1)} %all_to_all.11.refs_4_.sums0, f32[16,128]{1,0:T(8,128)S(1)} %broadcast_in_dim.2.friction, ...), custom_call_target="tpu_custom_call" | custom-call | flops 26214400 | bytes 2621440 | tf_op jit(solution)/shard_map/pallas_call | solution.py:559
  (1 shorter events, 0.0 us)
Async XLA Ops:
  0.6 1.4 %copy-start = (f32[3,16,16,512]{3,2,1,0:T(8,128)S(1)}, f32[3,16,16,512]{3,2,1,0:T(8,128)}, u32[]{:S(2)}) copy-start(f32[3,16,16,512]{3,2,1,0:T(8,128)} %magnetic.1) | copy-start | bytes 4718596
  4.7 5.2 %collective-permute-start.2 = (f32[3,16,4,512]{3,2,1,0:T(4,128)}, f32[3,16,4,512]{3,2,1,0:T(4,128)S(1)}, u32[]{:S(2)}, u32[]{:S(2)}) collective-permute-start(f32[3,16,4,512]{3,2,1,0:T(4,128)} %get-tuple-element.23), channel_id=1, source_target_pairs={{0,4},{1,5},{2,6},{3,7},{4,0},{5,1},{6,2},{7,3},{8,12},{9,13},{10,... | collective-permute-start | bytes 1179656 | tf_op jit(solution)/shard_map/ppermute | solution.py:63
  5.2 10.6 %collective-permute-start.3 = (f32[3,16,4,512]{3,2,1,0:T(4,128)}, f32[3,16,4,512]{3,2,1,0:T(4,128)S(1)}, u32[]{:S(2)}, u32[]{:S(2)}) collective-permute-start(f32[3,16,4,512]{3,2,1,0:T(4,128)} %get-tuple-element.24), channel_id=1, source_target_pairs={{0,16},{1,17},{2,18},{3,19},{4,8},{5,9},{6,10},{7,11},{8,4},{9,5},... | collective-permute-start | bytes 1179656 | tf_op jit(solution)/shard_map/ppermute | solution.py:63
  7.8 12.0 %collective-permute-start = (f32[3,4,16,512]{3,2,1,0:T(8,128)}, f32[3,4,16,512]{3,2,1,0:T(8,128)S(1)}, u32[]{:S(2)}, u32[]{:S(2)}) collective-permute-start(f32[3,4,16,512]{3,2,1,0:T(8,128)} %get-tuple-element.21), channel_id=1, source_target_pairs={{0,1},{1,0},{2,3},{3,2},{4,5},{5,4},{6,7},{7,6},{8,9},{9,8},{10,11... | collective-permute-start | bytes 1179656 | tf_op jit(solution)/shard_map/ppermute | solution.py:63
  9.4 14.7 %collective-permute-start.1 = (f32[3,4,16,512]{3,2,1,0:T(8,128)S(1)}, f32[3,4,16,512]{3,2,1,0:T(8,128)S(1)}, u32[]{:S(2)}, u32[]{:S(2)}) collective-permute-start(f32[3,4,16,512]{3,2,1,0:T(8,128)S(1)} %get-tuple-element.22), channel_id=1, source_target_pairs={{0,16},{1,2},{2,1},{3,19},{4,20},{5,6},{6,5},{7,23},{8,24},{9,10},... | collective-permute-start | bytes 1179656 | tf_op jit(solution)/shard_map/ppermute | solution.py:63
  15.9 10.5 %collective-permute-start.5 = (f32[3,4,8,512]{3,2,1,0:T(8,128)S(1)}, f32[3,4,8,512]{3,2,1,0:T(8,128)S(1)}, u32[]{:S(2)}, u32[]{:S(2)}) collective-permute-start(f32[3,4,8,512]{3,2,1,0:T(8,128)S(1)} %get-tuple-element.38), channel_id=1, source_target_pairs={{0,16},{1,2},{2,1},{3,19},{4,20},{5,6},{6,5},{7,23},{8,24},{9,10},... | collective-permute-start | bytes 589832 | tf_op jit(solution)/shard_map/ppermute | solution.py:63
  18.4 8.0 %collective-permute-start.4 = (f32[3,4,8,512]{3,2,1,0:T(8,128)S(1)}, f32[3,4,8,512]{3,2,1,0:T(8,128)S(1)}, u32[]{:S(2)}, u32[]{:S(2)}) collective-permute-start(f32[3,4,8,512]{3,2,1,0:T(8,128)S(1)} %get-tuple-element.39), channel_id=1, source_target_pairs={{0,1},{1,0},{2,3},{3,2},{4,5},{5,4},{6,7},{7,6},{8,9},{9,8},{10,11... | collective-permute-start | bytes 589832 | tf_op jit(solution)/shard_map/ppermute | solution.py:63
  26.4 18.4 %copy-start.1 = (f32[16]{0:T(128)S(1)}, f32[16]{0:T(128)}, u32[]{:S(2)}) copy-start(f32[16]{0:T(128)} %param.3) | copy-start | bytes 196
  50.4 2.6 %collective-permute-start.8 = (f32[81,4,512]{2,1,0:T(4,128)S(1)}, f32[81,4,512]{2,1,0:T(4,128)S(1)}, u32[]{:S(2)}, u32[]{:S(2)}) collective-permute-start(f32[81,4,512]{2,1,0:T(4,128)S(1)} %get-tuple-element.33), channel_id=1, source_target_pairs={{0,4},{1,5},{2,6},{3,7},{4,0},{5,1},{6,2},{7,3},{8,12},{9,13},{10,... | collective-permute-start | bytes 1990664 | tf_op jit(solution)/shard_map/ppermute | solution.py:63
  50.5 17.9 %collective-permute-start.9 = (f32[65,4,512]{2,1,0:T(4,128)S(1)}, f32[65,4,512]{2,1,0:T(4,128)S(1)}, u32[]{:S(2)}, u32[]{:S(2)}) collective-permute-start(f32[65,4,512]{2,1,0:T(4,128)S(1)} %get-tuple-element.34), channel_id=1, source_target_pairs={{0,16},{1,17},{2,18},{3,19},{4,8},{5,9},{6,10},{7,11},{8,4},{9,5},... | collective-permute-start | bytes 1597448 | tf_op jit(solution)/shard_map/ppermute | solution.py:63
  52.1 18.7 %collective-permute-start.6 = (f32[4,4,16,512]{3,2,1,0:T(8,128)S(1)}, f32[4,4,16,512]{3,2,1,0:T(8,128)S(1)}, u32[]{:S(2)}, u32[]{:S(2)}) collective-permute-start(f32[4,4,16,512]{3,2,1,0:T(8,128)S(1)} %get-tuple-element.31), channel_id=1, source_target_pairs={{0,1},{1,0},{2,3},{3,2},{4,5},{5,4},{6,7},{7,6},{8,9},{9,8},{10,11... | collective-permute-start | bytes 1572872 | tf_op jit(solution)/shard_map/ppermute | solution.py:63
  52.4 18.6 %collective-permute-start.7 = (f32[4,4,16,512]{3,2,1,0:T(8,128)S(1)}, f32[4,4,16,512]{3,2,1,0:T(8,128)S(1)}, u32[]{:S(2)}, u32[]{:S(2)}) collective-permute-start(f32[4,4,16,512]{3,2,1,0:T(8,128)S(1)} %get-tuple-element.32), channel_id=1, source_target_pairs={{0,16},{1,2},{2,1},{3,19},{4,20},{5,6},{6,5},{7,23},{8,24},{9,10},... | collective-permute-start | bytes 1572872 | tf_op jit(solution)/shard_map/ppermute | solution.py:63
  53.0 15.5 %collective-permute-start.10 = (f32[16,4,512]{2,1,0:T(4,128)S(1)}, f32[16,4,512]{2,1,0:T(4,128)S(1)}, u32[]{:S(2)}, u32[]{:S(2)}) collective-permute-start(f32[16,4,512]{2,1,0:T(4,128)S(1)} %get-tuple-element.40), channel_id=1, source_target_pairs={{0,8},{4,12},{8,0},{12,4},{1,9},{5,13},{9,1},{13,5},{2,10},{6,14},... | collective-permute-start | bytes 393224 | tf_op jit(solution)/shard_map/ppermute | solution.py:629
  69.3 5.6 %collective-permute-start.11 = (f32[2,4,8,512]{3,2,1,0:T(8,128)S(1)}, f32[2,4,8,512]{3,2,1,0:T(8,128)S(1)}, u32[]{:S(2)}, u32[]{:S(2)}) collective-permute-start(f32[2,4,8,512]{3,2,1,0:T(8,128)S(1)} %get-tuple-element.36), channel_id=1, source_target_pairs={{0,1},{1,0},{2,3},{3,2},{4,5},{5,4},{6,7},{7,6},{8,9},{9,8},{10,11... | collective-permute-start | bytes 393224 | tf_op jit(solution)/shard_map/ppermute | solution.py:63
  70.1 5.2 %collective-permute-start.12 = (f32[2,4,8,512]{3,2,1,0:T(8,128)S(1)}, f32[2,4,8,512]{3,2,1,0:T(8,128)S(1)}, u32[]{:S(2)}, u32[]{:S(2)}) collective-permute-start(f32[2,4,8,512]{3,2,1,0:T(8,128)S(1)} %get-tuple-element.37), channel_id=1, source_target_pairs={{0,16},{1,2},{2,1},{3,19},{4,20},{5,6},{6,5},{7,23},{8,24},{9,10},... | collective-permute-start | bytes 393224 | tf_op jit(solution)/shard_map/ppermute | solution.py:63

commit v2 on v1

--- a/solution.py
+++ b/solution.py
@@ -122,11 +122,9 @@
     )
 
 
-def descent_stages(bp, bx0, halo, cx, cz, blocks, omega_ref):
-    planes = cx + 2 * halo + 2
-
+def descent_stages(bp, plane_of, planes, halo, cz, blocks, omega_ref):
     def plane(x, _):
-        at = x + (bx0 - halo - 1)
+        at = plane_of(x)
         for r in windows(BASE - halo - 1, BASE + cz + halo + 1):
             def ld(c, j, dx=0, dz=0):
                 return bp[c, at + dx, j, r + dz : r + dz + ROWS, :]
@@ -148,16 +146,16 @@
                     omega_ref[k, x, j, r : r + ROWS, :] = value
         return 0
 
-    lax.fori_loop(0, planes, plane, 0)
-
-
-def doubled_force(bp, bx0, omega_ref, at, x, r, blocks):
+    lax.fori_loop(0, planes, plane, 0, unroll=2)
+
+
+def doubled_force(bp, bat, omega_ref, at, r, blocks):
     def ld(k, j, dx=0, dz=0):
         return omega_ref[k, at + dx, j, r + dz : r + dz + ROWS, :]
 
     dy = {k: y_diff([ld(k, j) for j in range(blocks)]) for k in (0, 2, 3)}
     for j in range(blocks):
-        field = [bp[c, x + bx0, j, r : r + ROWS, :] for c in range(3)]
+        field = [bp[c, bat, j, r : r + ROWS, :] for c in range(3)]
         omega = [ld(4 + c, j) for c in range(3)]
         current = [ld(7 + c, j) for c in range(3)]
         spread = ld(10, j)
@@ -198,16 +196,12 @@
     return (0.5 * step_scale) * functional / (slope + 1e-6)
 
 
-def entry_kernel(magnetic, core, face_xa, face_xb, face_za, face_zb, held, arrived):
+def entry_kernel(magnetic, core, face_xa, face_xb, face_za, face_zb):
     _, cx, cz, ny = magnetic.shape
     even_x, even_z = is_even("gx"), is_even("gz")
-    copies = [pltpu.make_async_copy(magnetic.at[c], held.at[c], arrived.at[c]) for c in range(3)]
-    for copy in copies:
-        copy.start()
     matrix = dealing(ny, False)
     for c in range(3):
-        copies[c].wait()
-        value = dealt(held[c].reshape(cx * cz, ny), matrix).reshape(cx, cz, ny)
+        value = dealt(magnetic[c].reshape(cx * cz, ny), matrix).reshape(cx, cz, ny)
         core[c] = value
         low, high = value[:HALO], value[cx - HALO :]
         face_xa[c] = jnp.where(even_x, high, low)
@@ -217,34 +211,83 @@
         face_zb[c] = jnp.where(even_z, low, high)
 
 
-def first_kernel(
-    core, face_xa, face_xb, face_za, face_zb, corner_a, corner_b, bp, fp, sums_ref, omega_ref
-):
+def first_forces(bp, plane_of, omega_ref, omega_of, fp, planes, x_of, cx, cz, blocks, rows, sums):
+    halo = HALO - 2
+    x_first, x_all, z_first, z_all = own_place(cx, cz)
+
+    def plane(x, sums):
+        functional, slope = sums
+        own = x_of(x)
+        own_x = (own >= 0) & (own < cx)
+        inside_x = (own + x_first >= 0) & (own + x_first < x_all)
+        for r in windows(BASE - halo, BASE + cz + halo):
+            height = rows + (r - BASE)
+            owned = (height >= 0) & (height < cz) & own_x
+            inside = (height + z_first >= 0) & (height + z_first < z_all) & inside_x
+            for j, force, field, size, spread in doubled_force(bp, plane_of(x), omega_ref, omega_of(x), r, blocks):
+                functional = functional + jnp.where(owned, density_of(field, size, spread), 0.0)
+                slope = slope + jnp.where(owned, dot(force, force), 0.0)
+                for c in range(3):
+                    fp[c, x, j, r : r + ROWS, :] = jnp.where(inside, force[c], 0.0)
+        return functional, slope
+
+    return lax.fori_loop(0, planes, plane, sums, unroll=4)
+
+
+def z_halos(bp, c, plane, j, top, a, b):
+    low, high = sorted_out("gz", a, b)
+    bp[c, plane, j, BASE - HALO : BASE, :] = low
+    bp[c, plane, j, top : top + HALO, :] = high
+
+
+def inner_kernel(core, face_za, face_zb, bp, fp, sums_ref, omega_ref):
     _, cx, cz, ny = core.shape
     blocks = ny // LANES
-    rows = row_index()
-    x_first, x_all, z_first, z_all = own_place(cx, cz)
-    top = BASE + cz
-
-    def z_halos(plane, c, j, a, b):
-        low, high = sorted_out("gz", a, b)
-        bp[c, plane, j, BASE - HALO : BASE, :] = low
-        bp[c, plane, j, top : top + HALO, :] = high
+    halo = HALO - 2
 
     def own(x, _):
         for c in range(3):
             for j in range(blocks):
                 cut = slice(j * LANES, (j + 1) * LANES)
                 for z in range(0, cz, ROWS):
-                    bp[c, x + HALO, j, BASE + z : BASE + z + ROWS, :] = core[c, x, z : z + ROWS, cut]
-                z_halos(x + HALO, c, j, face_za[c, x, :, cut], face_zb[c, x, :, cut])
-        return 0
+                    bp[c, x, j, BASE + z : BASE + z + ROWS, :] = core[c, x, z : z + ROWS, cut]
+                z_halos(bp, c, x, j, BASE + cz, face_za[c, x, :, cut], face_zb[c, x, :, cut])
+        return 0
+
+    lax.fori_loop(0, cx, own, 0)
+    descent_stages(bp, lambda x: x + 1, cx - 2, halo, cz, blocks, omega_ref)
+    zero = jnp.zeros((ROWS, LANES), jnp.float32)
+    sums_ref[0], sums_ref[1] = first_forces(
+        bp,
+        lambda x: x + 2,
+        omega_ref,
+        lambda x: x + 1,
+        fp,
+        cx - 4,
+        lambda x: x + 2,
+        cx,
+        cz,
+        blocks,
+        row_index(),
+        (zero, zero),
+    )
+
+
+def outer_kernel(own, part, face_xa, face_xb, corner_a, corner_b, bp, fp, sums_ref, omega_ref):
+    _, cx, blocks, _, _ = own.shape
+    cz = face_xa.shape[2]
+    halo = HALO - 2
+    rows = row_index()
+    top = BASE + cz
 
     def rim(x, _):
         for c in range(3):
             for j in range(blocks):
                 cut = slice(j * LANES, (j + 1) * LANES)
-                planes = (x, x + HALO + cx)
+                planes = (x, x + 3 * HALO)
+                for r in range(0, top + BASE, ROWS):
+                    bp[c, x + HALO, j, r : r + ROWS, :] = own[c, x, j, r : r + ROWS, :]
+                    bp[c, x + 2 * HALO, j, r : r + ROWS, :] = own[c, x + cx - HALO, j, r : r + ROWS, :]
                 for z in range(0, cz, ROWS):
                     span = slice(z, z + ROWS)
                     both = sorted_out("gx", face_xa[c, x, span, cut], face_xb[c, x, span, cut])
@@ -252,38 +295,30 @@
                         bp[c, plane, j, BASE + z : BASE + z + ROWS, :] = value
                 both = sorted_out("gx", corner_a[c, x, :, cut], corner_b[c, x, :, cut])
                 for plane, value in zip(planes, both):
-                    z_halos(plane, c, j, value[:HALO], value[HALO:])
-        return 0
-
-    lax.fori_loop(0, cx, own, 0)
+                    z_halos(bp, c, plane, j, top, value[:HALO], value[HALO:])
+        return 0
+
     lax.fori_loop(0, HALO, rim, 0)
-
-    halo = HALO - 2
-    descent_stages(bp, HALO, halo, cx, cz, blocks, omega_ref)
-
-    def plane(x, sums):
-        functional, slope = sums
-        own_x = (x >= halo) & (x < halo + cx)
-        there = x_first + x - halo
-        inside_x = (there >= 0) & (there < x_all)
-        for r in windows(BASE - halo, BASE + cz + halo):
-            height = rows + (r - BASE)
-            owned = (height >= 0) & (height < cz) & own_x
-            inside = (height + z_first >= 0) & (height + z_first < z_all) & inside_x
-            for j, force, field, size, spread in doubled_force(bp, HALO - halo, omega_ref, x + 1, x, r, blocks):
-                functional = functional + jnp.where(owned, density_of(field, size, spread), 0.0)
-                slope = slope + jnp.where(owned, dot(force, force), 0.0)
-                for c in range(3):
-                    fp[c, x, j, r : r + ROWS, :] = jnp.where(inside, force[c], 0.0)
-        return functional, slope
-
-    zero = jnp.zeros((ROWS, LANES), jnp.float32)
-    functional, slope = lax.fori_loop(0, cx + 2 * halo, plane, (zero, zero), unroll=4)
+    descent_stages(bp, lambda x: x + 1 + jnp.where(x >= 6, 2, 0), 12, halo, cz, blocks, omega_ref)
+    functional, slope = first_forces(
+        bp,
+        lambda x: x + 2 + jnp.where(x >= 4, 4, 0),
+        omega_ref,
+        lambda x: x + 1 + jnp.where(x >= 4, 2, 0),
+        fp,
+        8,
+        lambda x: x - 2 + jnp.where(x >= 4, cx - 4, 0),
+        cx,
+        cz,
+        blocks,
+        rows,
+        (part[0], part[1]),
+    )
     store_sums(sums_ref, functional, slope, rows)
 
 
 def second_kernel(
-    cells, bp0, fp0, sums0, friction, core_b, core_f, face_xa, face_xb, face_za, face_zb, sums_ref, bp, omega_ref
+    cells, own_b, inner_f, outer_b, outer_f, sums0, friction, core_b, core_f, face_xa, face_xb, face_za, face_zb, sums_ref, bp, omega_ref
 ):
     _, cx, cz, ny = core_b.shape
     blocks = ny // LANES
@@ -292,23 +327,31 @@
     rate = half_rate(sums0, cells)
     halo = HALO - 2
 
-    def step(x, _):
+    def step(x, field, at, force, there):
         for c in range(3):
             for j in range(blocks):
                 for r in range(0, cz + 2 * BASE, ROWS):
                     bp[c, x, j, r : r + ROWS, :] = (
-                        bp0[c, x + HALO - halo, j, r : r + ROWS, :] + rate * fp0[c, x, j, r : r + ROWS, :]
+                        field[c, at, j, r : r + ROWS, :] + rate * force[c, there, j, r : r + ROWS, :]
                     )
-        return 0
-
-    lax.fori_loop(0, cx + 2 * halo, step, 0, unroll=2)
-    descent_stages(bp, halo, 0, cx, cz, blocks, omega_ref)
+
+    def inner_step(x, _):
+        step(x + 4, own_b, x + 2, inner_f, x)
+        return 0
+
+    lax.fori_loop(0, cx - 4, inner_step, 0, unroll=2)
+    for k in range(2):
+        step(k, outer_b, k + 2, outer_f, k)
+        step(k + 2, own_b, k, outer_f, k + 2)
+        step(k + cx, own_b, k + cx - 2, outer_f, k + 4)
+        step(k + cx + 2, outer_b, k + 12, outer_f, k + 6)
+    descent_stages(bp, lambda x: x + 1, cx + 2, 0, cz, blocks, omega_ref)
 
     def plane(x, sums):
         functional, slope = sums
         for z in range(0, cz, ROWS):
             r = BASE + z
-            for j, force, field, size, spread in doubled_force(bp, halo, omega_ref, x + 1, x, r, blocks):
+            for j, force, field, size, spread in doubled_force(bp, x + halo, omega_ref, x + 1, r, blocks):
                 cut = slice(j * LANES, (j + 1) * LANES)
                 functional = functional + density_of(field, size, spread)
                 slope = slope + dot(force, force)
@@ -350,30 +393,115 @@
         face_zb[4 * cx, :, cut] = jnp.where(even_z, low, high)
 
 
-def third_kernel(
-    cells,
-    core_b,
-    core_f,
-    sums0,
-    friction,
-    face_xa,
-    face_xb,
-    face_za,
-    face_zb,
-    above,
-    corner_a,
-    corner_b,
-    relaxed,
-    potential,
-    ap,
-    bm,
-    an,
-    rub,
+def suffix(value, rows):
+    for reach in (1, 2, 4):
+        value = value + jnp.where(rows < ROWS - reach, pltpu.roll(value, ROWS - reach, 0), 0.0)
+    return value
+
+
+def prefix(value, rows):
+    for reach in (1, 2, 4):
+        value = value + jnp.where(rows >= reach, pltpu.roll(value, reach, 0), 0.0)
+    return value
+
+
+def column(ap, c, plane, j, low, own, high, beyond, rows):
+    sign = 1.0 if c == 0 else -1.0
+    out = 1 - c
+    top = BASE + ROWS * len(own)
+    ap[out, plane, j, top : top + HALO, :] = high
+    value = ap[out, plane, j, top : top + ROWS, :]
+    ap[out, plane, j, top : top + ROWS, :] = sign * (beyond - (prefix(value, rows) - value))
+    carry = beyond
+    for k in reversed(range(len(own))):
+        value = suffix(own[k], rows) + carry
+        ap[out, plane, j, BASE + k * ROWS : BASE + (k + 1) * ROWS, :] = sign * value
+        carry = value[0:1]
+    ap[out, plane, j, BASE - HALO : BASE, :] = low
+    value = suffix(ap[out, plane, j, 0:BASE, :], rows) + carry
+    ap[out, plane, j, 0:BASE, :] = jnp.where(lax.axis_index("gz") > 0, sign * value, 0.0)
+
+
+def induced(a_ref, bm, planes, halo, at_of, out_of, own_of, flat, cx, cz, blocks, rows):
+    x_first, x_all, z_first, z_all = own_place(cx, cz)
+
+    def plane(x, _):
+        at, out = at_of(x), out_of(x)
+        there = x_first + own_of(x)
+        inside_x = (there >= 0) & (there < x_all)
+        for r in windows(BASE - halo, BASE + cz + halo):
+            height = rows + (r - BASE) + z_first
+            inside = (height >= 0) & (height < z_all) & inside_x
+
+            def ld(c, j, dx=0, dz=0):
+                return a_ref[c, at + dx, j, r + dz : r + dz + ROWS, :]
+
+            dy = {c: y_diff([ld(c, j) for j in range(blocks)]) for c in ((0,) if flat else (0, 2))}
+            for j in range(blocks):
+                curl_x = ld(1, j, dz=-1) - ld(1, j, dz=1)
+                curl_y = ld(0, j, dz=1) - ld(0, j, dz=-1)
+                curl_z = ld(1, j, dx=1) - ld(1, j, dx=-1) - dy[0][j]
+                if not flat:
+                    curl_x = curl_x + dy[2][j]
+                    curl_y = curl_y - (ld(2, j, dx=1) - ld(2, j, dx=-1))
+                for c, value in enumerate((curl_x, curl_y, curl_z)):
+                    bm[c, out, j, r : r + ROWS, :] = jnp.where(inside, value, 0.0)
+        return 0
+
+    lax.fori_loop(0, planes, plane, 0, unroll=4)
+
+
+def pushed(bm, x, r, rub, blocks):
+    def ld(c, j, dx=0, dz=0):
+        return bm[c, x + dx, j, r + dz : r + dz + ROWS, :]
+
+    dy = [y_diff([ld(c, j) for j in range(blocks)]) if c != 1 else None for c in range(3)]
+    weight = rub[r : r + ROWS]
+    for j in range(blocks):
+        field = [ld(c, j) for c in range(3)]
+        current = (
+            dy[2][j] - (ld(1, j, dz=1) - ld(1, j, dz=-1)),
+            (ld(0, j, dz=1) - ld(0, j, dz=-1)) - (ld(2, j, dx=1) - ld(2, j, dx=-1)),
+            (ld(1, j, dx=1) - ld(1, j, dx=-1)) - dy[0][j],
+        )
+        square = dot(field, field)
+        scale = weight * (0.0625 / jnp.maximum(0.25 * square, 1.0))
+        both = dot(current, field)
+        yield j, [scale * (field[c] * both - current[c] * square) for c in range(3)]
+
+
+def first_push(ap, bm, an, rub, planes, at_of, out_of, cz, blocks):
+    def plane(x, _):
+        halo = HALO - 2
+        for r in windows(BASE - halo, BASE + cz + halo):
+            for j, change in pushed(bm, at_of(x), r, rub, blocks):
+                for c in range(2):
+                    an[c, out_of(x), j, r : r + ROWS, :] = ap[c, x + 2, j, r : r + ROWS, :] + change[c]
+                an[2, out_of(x), j, r : r + ROWS, :] = change[2]
+        return 0
+
+    lax.fori_loop(0, planes, plane, 0, unroll=2)
+
+
+def last_push(an, bm, out, rub, planes, at_of, cz, blocks):
+    def plane(x, _):
+        for z in range(0, cz, ROWS):
+            for j, change in pushed(bm, at_of(x), BASE + z, rub, blocks):
+                cut = slice(j * LANES, (j + 1) * LANES)
+                for c in range(3):
+                    out[c, x, z : z + ROWS, cut] = an[c, x + 2, j, BASE + z : BASE + z + ROWS, :] + change[c]
+        return 0
+
+    lax.fori_loop(0, planes, plane, 0, unroll=2)
+
+
+def middle_kernel(
+    cells, core_b, core_f, sums0, friction, face_za, face_zb, above, relaxed, ap, bm, an, bn, inner, rub
 ):
     _, cx, cz, ny = core_b.shape
     blocks = ny // LANES
     rows = row_index()
-    x_first, x_all, z_first, z_all = own_place(cx, cz)
+    _, _, z_first, z_all = own_place(cx, cz)
     rate = half_rate(sums0, cells)
     top = BASE + cz
 
@@ -385,31 +513,6 @@
         height = rows + (r - BASE) + z_first
         inside = (height >= 0) & (height < z_all)
         rub[r : r + ROWS] = jnp.where(inside, time_step / rub[r : r + ROWS], 0.0)
-
-    def suffix(value):
-        for reach in (1, 2, 4):
-            value = value + jnp.where(rows < ROWS - reach, pltpu.roll(value, ROWS - reach, 0), 0.0)
-        return value
-
-    def prefix(value):
-        for reach in (1, 2, 4):
-            value = value + jnp.where(rows >= reach, pltpu.roll(value, reach, 0), 0.0)
-        return value
-
-    def column(c, plane, j, low, own, high, beyond):
-        sign = 1.0 if c == 0 else -1.0
-        out = 1 - c
-        ap[out, plane, j, top : top + HALO, :] = high
-        value = ap[out, plane, j, top : top + ROWS, :]
-        ap[out, plane, j, top : top + ROWS, :] = sign * (beyond - (prefix(value) - value))
-        carry = beyond
-        for z in reversed(range(0, cz, ROWS)):
-            value = suffix(own[z // ROWS]) + carry
-            ap[out, plane, j, BASE + z : BASE + z + ROWS, :] = sign * value
-            carry = value[0:1]
-        ap[out, plane, j, BASE - HALO : BASE, :] = low
-        value = suffix(ap[out, plane, j, 0:BASE, :]) + carry
-        ap[out, plane, j, 0:BASE, :] = jnp.where(z_first > 0, sign * value, 0.0)
 
     def own_plane(x, _):
         for j in range(blocks):
@@ -427,10 +530,26 @@
                     face[(2 + c) * cx + x, :, cut] + rate * face[c * cx + x, :, cut] for face in (face_za, face_zb)
                 ]
                 low, high = sorted_out("gz", a, b)
-                column(c, x + HALO, j, low, own, high, above[x, c : c + 1, cut])
+                column(ap, c, x, j, low, own, high, above[x, c : c + 1, cut], rows)
         return 0
 
     lax.fori_loop(0, cx, own_plane, 0, unroll=2)
+    matrix = dealing(ny, True)
+    relaxed[...] = dealt(relaxed[...].reshape(3 * cx * cz, ny), matrix).reshape(relaxed.shape)
+    induced(ap, bm, cx - 2, HALO - 1, lambda x: x + 1, lambda x: x, lambda x: x + 1, True, cx, cz, blocks, rows)
+    first_push(ap, bm, an, rub, cx - 4, lambda x: x + 1, lambda x: x, cz, blocks)
+    induced(an, bn, cx - 6, 1, lambda x: x + 1, lambda x: x, lambda x: x + 3, False, cx, cz, blocks, rows)
+    last_push(an, bn, inner, rub, cx - 8, lambda x: x + 1, cz, blocks)
+    inner[...] = dealt(inner[...].reshape(-1, ny), matrix).reshape(inner.shape)
+
+
+def ends_kernel(
+    cells, sums0, face_xa, face_xb, corner_a, corner_b, own_ap, own_bm, own_an, own_bn, inner, rub, potential, ap, bm, an, rim
+):
+    _, cx, cz, ny = potential.shape
+    blocks = ny // LANES
+    rows = row_index()
+    rate = half_rate(sums0, cells)
 
     def rim_plane(x, _):
         for j in range(blocks):
@@ -442,86 +561,38 @@
                     a, b = [face[2 + c, x, span, cut] + rate * face[c, x, span, cut] for face in (face_xa, face_xb)]
                     own.append(sorted_out("gx", a, b))
                 corners = sorted_out("gx", corner_a[c, x, :, cut], corner_b[c, x, :, cut])
-                for side, plane in enumerate((x, x + HALO + cx)):
+                for side, plane in enumerate((x, x + 2 * HALO)):
                     corner = corners[side]
                     high = jnp.concatenate([corner[1:4], corner[3:4]], 0)
-                    column(c, plane, j, corner[4:8], [pair[side] for pair in own], high, corner[0:1])
+                    column(ap, c, plane, j, corner[4:8], [pair[side] for pair in own], high, corner[0:1], rows)
         return 0
 
     lax.fori_loop(0, HALO, rim_plane, 0)
 
-    def induced(a_ref, ax0, halo, flat):
-        def plane(x, _):
-            at = x + (ax0 - halo - 1)
-            there = x_first + x - halo - 1
-            inside_x = (there >= 0) & (there < x_all)
-            for r in windows(BASE - halo - 1, top + halo + 1):
-                height = rows + (r - BASE) + z_first
-                inside = (height >= 0) & (height < z_all) & inside_x
-
-                def ld(c, j, dx=0, dz=0):
-                    return a_ref[c, at + dx, j, r + dz : r + dz + ROWS, :]
-
-                dy = {c: y_diff([ld(c, j) for j in range(blocks)]) for c in ((0,) if flat else (0, 2))}
-                for j in range(blocks):
-                    curl_x = ld(1, j, dz=-1) - ld(1, j, dz=1)
-                    curl_y = ld(0, j, dz=1) - ld(0, j, dz=-1)
-                    curl_z = ld(1, j, dx=1) - ld(1, j, dx=-1) - dy[0][j]
-                    if not flat:
-                        curl_x = curl_x + dy[2][j]
-                        curl_y = curl_y - (ld(2, j, dx=1) - ld(2, j, dx=-1))
-                    for c, value in enumerate((curl_x, curl_y, curl_z)):
-                        bm[c, x, j, r : r + ROWS, :] = jnp.where(inside, value, 0.0)
-            return 0
-
-        lax.fori_loop(0, cx + 2 * halo + 2, plane, 0, unroll=6)
-
-    def pushed(x, r):
-        def ld(c, j, dx=0, dz=0):
-            return bm[c, x + dx, j, r + dz : r + dz + ROWS, :]
-
-        dy = [y_diff([ld(c, j) for j in range(blocks)]) if c != 1 else None for c in range(3)]
-        weight = rub[r : r + ROWS]
-        for j in range(blocks):
-            field = [ld(c, j) for c in range(3)]
-            current = (
-                dy[2][j] - (ld(1, j, dz=1) - ld(1, j, dz=-1)),
-                (ld(0, j, dz=1) - ld(0, j, dz=-1)) - (ld(2, j, dx=1) - ld(2, j, dx=-1)),
-                (ld(1, j, dx=1) - ld(1, j, dx=-1)) - dy[0][j],
-            )
-            square = dot(field, field)
-            scale = weight * (0.0625 / jnp.maximum(0.25 * square, 1.0))
-            both = dot(current, field)
-            yield j, [scale * (field[c] * both - current[c] * square) for c in range(3)]
-
-    halo = HALO - 2
-    induced(ap, HALO, halo, True)
-
-    def first_step(x, _):
-        for r in windows(BASE - halo, top + halo):
-            for j, change in pushed(x + 1, r):
-                for c in range(2):
-                    an[c, x, j, r : r + ROWS, :] = ap[c, x + HALO - halo, j, r : r + ROWS, :] + change[c]
-                an[2, x, j, r : r + ROWS, :] = change[2]
-        return 0
-
-    lax.fori_loop(0, cx + 2 * halo, first_step, 0, unroll=2)
-    induced(an, halo, 0, False)
-
-    def last_step(x, _):
-        for z in range(0, cz, ROWS):
-            for j, change in pushed(x + 1, BASE + z):
-                cut = slice(j * LANES, (j + 1) * LANES)
-                for c in range(3):
-                    potential[c, x, z : z + ROWS, cut] = (
-                        an[c, x + halo, j, BASE + z : BASE + z + ROWS, :] + change[c]
-                    )
-        return 0
-
-    lax.fori_loop(0, cx, last_step, 0, unroll=2)
-    matrix = dealing(ny, True)
-    for out in (relaxed, potential):
-        out[...] = dealt(out[...].reshape(3 * cx * cz, ny), matrix).reshape(3, cx, cz, ny)
+    def borrow(into, source, low, high):
+        for k in range(2):
+            for c in range(source.shape[0]):
+                into[c, 4 + k] = source[c, low + k]
+                into[c, 6 + k] = source[c, high + k]
+
+    def at_of(x):
+        return x + 1 + jnp.where(x >= 4, 2, 0)
+
+    def out_of(x):
+        return x + jnp.where(x >= 4, 4, 0)
+
+    borrow(ap, own_ap, 0, cx - 2)
+    induced(ap, bm, 8, HALO - 1, at_of, out_of, lambda x: x - 3 + jnp.where(x >= 4, cx - 2, 0), True, cx, cz, blocks, rows)
+    borrow(bm, own_bm, 0, cx - 4)
+    first_push(ap, bm, an, rub, 8, at_of, out_of, cz, blocks)
+    borrow(an, own_an, 0, cx - 6)
+    induced(an, bm, 8, 1, at_of, out_of, lambda x: x - 1 + jnp.where(x >= 4, cx - 6, 0), False, cx, cz, blocks, rows)
+    borrow(bm, own_bn, 0, cx - 8)
+    last_push(an, bm, rim, rub, 8, at_of, cz, blocks)
+    ends = dealt(rim[...].reshape(-1, ny), dealing(ny, True)).reshape(rim.shape)
+    potential[:, :HALO] = ends[:, :HALO]
+    potential[:, cx - HALO :] = ends[:, HALO:]
+    potential[:, HALO : cx - HALO] = inner[...]
 
 
 def pack_kernel(cells, count, *refs):
@@ -578,8 +649,11 @@
     cells = cx * cz * ny * devices
     work = cx * cz * ny * 200
 
+    def planes_of(components, planes):
+        return (components, planes, blocks, height, LANES)
+
     def padded(components, layers):
-        return (components, cx + 2 * layers, blocks, height, LANES)
+        return planes_of(components, cx + 2 * layers)
 
     tiles = (devices, ROWS, LANES)
     core = (3, cx, cz, ny)
@@ -589,30 +663,39 @@
         entry_kernel,
         [core, *[(3, HALO, cz, ny)] * 2, *[(3, cx, HALO, ny)] * 2],
         magnetic,
-        scratch=[core, pltpu.SemaphoreType.DMA((3,))],
-        outside=1,
         cost=work,
-        limit=16,
+        limit=8,
     )
     faces_x = swapped(faces[:2], "gx")
     faces_z = swapped(faces[2:], "gz")
     corners = swapped(edges(jnp.concatenate(faces_z, axis=2), "gx", 1), "gx")
-    bp, fp, sums = call(
-        first_kernel,
-        [padded(3, HALO), padded(3, HALO - 2), tiles],
+    own_b, inner_f, part = call(
+        inner_kernel,
+        [padded(3, 0), padded(3, -2), (2, ROWS, LANES)],
         magnetic,
+        *faces_z,
+        scratch=[padded(11, -1)],
+        cost=work,
+        limit=13,
+    )
+    outer_b, outer_f, sums = call(
+        outer_kernel,
+        [planes_of(3, 4 * HALO), planes_of(3, 8), tiles],
+        own_b,
+        part,
         *faces_x,
-        *faces_z,
         *corners,
-        scratch=[padded(11, HALO - 1)],
-        cost=2 * work,
-        limit=18,
+        scratch=[planes_of(11, 12)],
+        cost=work,
+        limit=12,
     )
     core_b, core_f, *faces, sums = call(
         functools.partial(second_kernel, cells),
         [core, core, (4, HALO, cz, ny), (4, HALO, cz, ny), (5 * cx + 1, HALO, ny), (4 * cx + 1, HALO, ny), tiles],
-        bp,
-        fp,
+        own_b,
+        inner_f,
+        outer_b,
+        outer_f,
         shared(sums),
         rubbed,
         scratch=[padded(3, HALO - 2), padded(11, 1)],
@@ -639,23 +722,30 @@
         cost=work // 50,
     )
     corners = swapped(corners, "gx")
-    return tuple(
-        call(
-            functools.partial(third_kernel, cells),
-            [core, core],
-            core_b,
-            core_f,
-            sums,
-            rubbed,
-            *faces_x,
-            *faces_z,
-            above,
-            *corners,
-            scratch=[padded(2, HALO), padded(3, HALO - 1), padded(3, HALO - 2), (height, LANES)],
-            cost=work,
-            limit=16,
-        )
-    )
+    relaxed, *shares = call(
+        functools.partial(middle_kernel, cells),
+        [core, padded(2, 0), padded(3, -1), padded(3, -2), padded(3, -3), (3, cx - 2 * HALO, cz, ny), (height, LANES)],
+        core_b,
+        core_f,
+        sums,
+        rubbed,
+        *faces_z,
+        above,
+        cost=work,
+        limit=8,
+    )
+    (potential,) = call(
+        functools.partial(ends_kernel, cells),
+        [core],
+        sums,
+        *faces_x,
+        *corners,
+        *shares,
+        scratch=[planes_of(2, 12), planes_of(3, 12), planes_of(3, 12), (3, 2 * HALO, cz, ny)],
+        cost=work,
+        limit=14,
+    )
+    return relaxed, potential
 
 
 def solution(mesh):

time: 84.7 us -> 77.3 us (0.913)
  waiting for transfers between devices: 18.6 us -> 9.76 us
  Pallas kernels: 24.6 us -> 26.1 us
    ppermute x6, waiting for transfers between devices: 5.29 us -> 0.02 us  [swapped(): lax.ppermute(pair[0], AXES, first)]
    ppermute x6, waiting for transfers between devices: 13.3 us -> 9.74 us  [swapped(): lax.ppermute(pair[1], AXES, second)]
    pallas_call x5 -> x7, Pallas kernels: 24.6 us -> 26.1 us  [call(): pl.pallas_call(kernel, out_shape=shapes, in_specs=[pl.BlockSpec(memory_sp...]
  transfers between devices with their start and end apart: 13 -> 13, of which waited for: 7 -> 3; matrix products, arithmetic and copies ran while one was open for 0% -> 0% of each run, Pallas kernels for 1% -> 15%
where the time goes in v2:
time: 77.3 us; the launch traced here: 77 us
  Pallas kernels  26.1 us (34%)
  blocking collectives  25.8 us (33%)
  starting transfers between devices  13 us (17%)
  waiting for transfers between devices  9.76 us (13%)
  local copies, waits for them, and re-layouts  1.47 us (2%)
    pallas_call x7, Pallas kernels, call(): pl.pallas_call(kernel, out_shape=shapes, in_specs=[pl.BlockSpec(memory_sp...  26.1 us
    all_to_all x2, blocking collectives, shared(): return lax.all_to_all(tile_copies, ('gz', 'gx'), 0, 0)  25.8 us
    ppermute x6, waiting for transfers between devices, swapped(): lax.ppermute(pair[1], AXES, second)  9.74 us
    ppermute x6, starting transfers between devices, swapped(): lax.ppermute(pair[1], AXES, second)  8.12 us
    ppermute x6, starting transfers between devices, swapped(): lax.ppermute(pair[0], AXES, first)  3.36 us
    ppermute x1, starting transfers between devices, body(): lax.ppermute(group, 'gz', [(i, i ^ stride) for i in range(count_z)])  1.57 us
  transfers between devices with their start and end apart: 13, of which 3 were waited for; matrix products, arithmetic and copies ran while one was open for 0% of the time, Pallas kernels for 15%

profile of v2, /device:TPU:0, one launch (start us, length us, event | category | flops | bytes accessed | tf_op | source)
XLA Modules:
  0.0 77.0 jit_solution(17433624782235777295)
XLA Ops:
  0.6 0.0 copy-start
  0.6 1.4 %copy-done = f32[3,16,16,512]{3,2,1,0:T(8,128)S(1)} copy-done((f32[3,16,16,512]{3,2,1,0:T(8,128)S(1)}, f32[3,16,16,512]{3,2,1,0:T(8,128)}, u32[]{:S(2)}) %copy-start) | copy-done | bytes 1572888
  2.0 2.0 %shard_map.41 = (f32[3,16,16,512]{3,2,1,0:T(8,128)S(1)}, f32[3,4,16,512]{3,2,1,0:T(8,128)}, f32[3,4,16,512]{3,2,1,0:T(8,128)S(1)}, f32[3,16,4,512]{3,2,1,0:T(4,128)}, f32[3,16,4,512]{3,2,1,0:T(4,128)}) custom-call(f32[3,16,16,512]{3,2,1,0:T(8,128)S(1)} %copy-done), custom_call_target="tpu_custom_call" | custom-call | flops 26214400 | bytes 2621440 | tf_op jit(solution)/shard_map/pallas_call | solution.py:630
  4.1 0.5 collective-permute-start
  4.5 2.5 %collective-permute-start.1 = (f32[3,16,4,512]{3,2,1,0:T(4,128)}, f32[3,16,4,512]{3,2,1,0:T(4,128)S(1)}, u32[]{:S(2)}, u32[]{:S(2)}) collective-permute-start(f32[3,16,4,512]{3,2,1,0:T(4,128)} %get-tuple-element.32), channel_id=1, source_target_pairs={{0,16},{1,17},{2,18},{3,19},{4,8},{5,9},{6,10},{7,11},{8,4},{9,5},... | collective-permute-start | bytes 1179656 | tf_op jit(solution)/shard_map/ppermute | solution.py:63
  7.0 1.6 %collective-permute-start.2 = (f32[3,4,16,512]{3,2,1,0:T(8,128)}, f32[3,4,16,512]{3,2,1,0:T(8,128)S(1)}, u32[]{:S(2)}, u32[]{:S(2)}) collective-permute-start(f32[3,4,16,512]{3,2,1,0:T(8,128)} %get-tuple-element.36), channel_id=1, source_target_pairs={{0,1},{1,0},{2,3},{3,2},{4,5},{5,4},{6,7},{7,6},{8,9},{9,8},{10,11... | collective-permute-start | bytes 1179656 | tf_op jit(solution)/shard_map/ppermute | solution.py:63
  8.6 0.5 collective-permute-start.3
  9.1 0.0 collective-permute-done.face_za
  9.1 5.9 %collective-permute-done.1.face_zb = f32[3,16,4,512]{3,2,1,0:T(4,128)S(1)} collective-permute-done((f32[3,16,4,512]{3,2,1,0:T(4,128)}, f32[3,16,4,512]{3,2,1,0:T(4,128)S(1)}, u32[]{:S(2)}, u32[]{:S(2)}) %collective-permute-start.1) | collective-permute-done | bytes 393248 | tf_op jit(solution)/shard_map/ppermute | solution.py:63
  15.1 0.1 fusion
  15.2 2.4 %collective-permute-start.5 = (f32[3,4,8,512]{3,2,1,0:T(8,128)S(1)}, f32[3,4,8,512]{3,2,1,0:T(8,128)S(1)}, u32[]{:S(2)}, u32[]{:S(2)}) collective-permute-start(f32[3,4,8,512]{3,2,1,0:T(8,128)S(1)} %get-tuple-element.58), channel_id=1, source_target_pairs={{0,16},{1,2},{2,1},{3,19},{4,20},{5,6},{6,5},{7,23},{8,24},{9,10},... | collective-permute-start | bytes 589832 | tf_op jit(solution)/shard_map/ppermute | solution.py:63
  17.6 0.0 collective-permute-start.4
  17.6 4.2 %shard_map.42 = (f32[3,16,4,32,128]{4,3,2,1,0:T(8,128)S(1)}, f32[3,12,4,32,128]{4,3,2,1,0:T(8,128)S(1)}, f32[2,8,128]{2,1,0:T(8,128)S(1)}) custom-call(f32[3,16,16,512]{3,2,1,0:T(8,128)S(1)} %get-tuple-element.30.core, f32[3,16,4,512]{3,2,1,0:T(4,128)S(1)} %collective-permute-done.face_za, f32[3,16,4,512]{3,2,1,0:T(4,128)S(1)} %collective-permute-done.1.face_zb), custom_call_target="tpu_custom_call" | custom-call | flops 26214400 | bytes 2621440 | tf_op jit(solution)/shard_map/pallas_call | solution.py:630
  21.8 0.0 collective-permute-done.2.face_xa
  21.9 1.5 %collective-permute-done.3.face_xb = f32[3,4,16,512]{3,2,1,0:T(8,128)S(1)} collective-permute-done((f32[3,4,16,512]{3,2,1,0:T(8,128)S(1)}, f32[3,4,16,512]{3,2,1,0:T(8,128)S(1)}, u32[]{:S(2)}, u32[]{:S(2)}) %collective-permute-start.3) | collective-permute-done | bytes 393248 | tf_op jit(solution)/shard_map/ppermute | solution.py:63
  23.3 2.3 %collective-permute-done.5.corner_b = f32[3,4,8,512]{3,2,1,0:T(8,128)S(1)} collective-permute-done((f32[3,4,8,512]{3,2,1,0:T(8,128)S(1)}, f32[3,4,8,512]{3,2,1,0:T(8,128)S(1)}, u32[]{:S(2)}, u32[]{:S(2)}) %collective-permute-start.5) | collective-permute-done | bytes 196640 | tf_op jit(solution)/shard_map/ppermute | solution.py:63
  25.6 0.0 collective-permute-done.4.corner_a
  25.6 0.0 copy-start.1
  25.6 3.1 %shard_map.43 = (f32[3,16,4,32,128]{4,3,2,1,0:T(8,128)S(1)}, f32[3,8,4,32,128]{4,3,2,1,0:T(8,128)S(1)}, f32[16,8,128]{2,1,0:T(8,128)S(1)}) custom-call(f32[3,16,4,32,128]{4,3,2,1,0:T(8,128)S(1)} %get-tuple-element.33.own.own_b, f32[2,8,128]{2,1,0:T(8,128)S(1)} %get-tuple-element.35.part, f32[3,4,16,512]{3,2,1,0:T(8,128)S(1)} %collective-permute-done.2.face_xa, ...), custom_call_target="tpu_custom_call" | custom-call | flops 26214400 | bytes 2621440 | tf_op jit(solution)/shard_map/pallas_call | solution.py:630
  28.7 11.9 %all_to_all.10.sums0 = f32[16,8,128]{2,1,0:T(8,128)S(1)} all-to-all(f32[16,8,128]{2,1,0:T(8,128)S(1)} %get-tuple-element.40), channel_id=1, replica_groups=mesh['runs'=2,'gz'=4,'gx'=4] {'gz','gx'}, dimensions={0} | all-to-all | bytes 131072 | tf_op jit(solution)/shard_map/all_to_all | solution.py:75
  40.6 0.0 copy-done.1
  40.7 0.1 broadcast_in_dim.2.friction
  40.7 5.4 %shard_map.44 = (f32[3,16,16,512]{3,2,1,0:T(8,128)S(1)}, f32[3,16,16,512]{3,2,1,0:T(8,128)S(1)}, f32[4,4,16,512]{3,2,1,0:T(8,128)S(1)}, f32[4,4,16,512]{3,2,1,0:...) custom-call(f32[3,16,4,32,128]{4,3,2,1,0:T(8,128)S(1)} %get-tuple-element.33.own.own_b, ...), custom_call_target="tpu_custom_call" | custom-call | flops 26214400 | bytes 2621440 | tf_op jit(solution)/shard_map/pallas_call | solution.py:630
  46.1 0.2 collective-permute-start.6
  46.3 1.5 %collective-permute-start.7 = (f32[65,4,512]{2,1,0:T(4,128)S(1)}, f32[65,4,512]{2,1,0:T(4,128)S(1)}, u32[]{:S(2)}, u32[]{:S(2)}) collective-permute-start(f32[65,4,512]{2,1,0:T(4,128)S(1)} %get-tuple-element.45), channel_id=1, source_target_pairs={{0,16},{1,17},{2,18},{3,19},{4,8},{5,9},{6,10},{7,11},{8,4},{9,5},... | collective-permute-start | bytes 1597448 | tf_op jit(solution)/shard_map/ppermute | solution.py:63
  47.8 0.3 collective-permute-start.9
  48.1 0.5 collective-permute-start.10
  48.7 0.0 collective-permute-done.6.refs_2_.face_za
  48.7 1.6 %collective-permute-start.8 = (f32[16,4,512]{2,1,0:T(4,128)S(1)}, f32[16,4,512]{2,1,0:T(4,128)S(1)}, u32[]{:S(2)}, u32[]{:S(2)}) collective-permute-start(f32[16,4,512]{2,1,0:T(4,128)S(1)} %get-tuple-element.60), channel_id=1, source_target_pairs={{0,8},{4,12},{8,0},{12,4},{1,9},{5,13},{9,1},{13,5},{2,10},{6,14},... | collective-permute-start | bytes 393224 | tf_op jit(solution)/shard_map/ppermute | solution.py:712
  50.3 13.9 %all_to_all.11.refs_4_.sums0 = f32[16,8,128]{2,1,0:T(8,128)S(1)} all-to-all(f32[16,8,128]{2,1,0:T(8,128)S(1)} %get-tuple-element.43), channel_id=1, replica_groups=mesh['runs'=2,'gz'=4,'gx'=4] {'gz','gx'}, dimensions={0} | all-to-all | bytes 131072 | tf_op jit(solution)/shard_map/all_to_all | solution.py:75
  64.2 0.0 collective-permute-done.7.refs_3_.face_zb
  64.2 0.0 collective-permute-done.8.refs_1_
  64.2 0.8 %shard_map.45 = (f32[16,2,512]{2,1,0:T(2,128)S(1)}, f32[2,4,8,512]{3,2,1,0:T(8,128)S(1)}, f32[2,4,8,512]{3,2,1,0:T(8,128)S(1)}) custom-call(f32[16,4,512]{2,1,0:T(4,128)S(1)} %get-tuple-element.61.refs_0_, f32[16,4,512]{2,1,0:T(4,128)S(1)} %collective-permute-done.8.refs_1_, f32[81,4,512]{2,1,0:T(4,128)S(1)} %collective-permute-done.6.refs_2_.face_za, ...), custom_call_target="tpu_custom_call" | custom-call | flops 524288 | bytes 52428 | tf_op jit(solution)/shard_map/pallas_call | solution.py:630
  65.1 0.8 %collective-permute-start.11 = (f32[2,4,8,512]{3,2,1,0:T(8,128)S(1)}, f32[2,4,8,512]{3,2,1,0:T(8,128)S(1)}, u32[]{:S(2)}, u32[]{:S(2)}) collective-permute-start(f32[2,4,8,512]{3,2,1,0:T(8,128)S(1)} %get-tuple-element.50), channel_id=1, source_target_pairs={{0,1},{1,0},{2,3},{3,2},{4,5},{5,4},{6,7},{7,6},{8,9},{9,8},{10,11... | collective-permute-start | bytes 393224 | tf_op jit(solution)/shard_map/ppermute | solution.py:63
  65.9 0.6 collective-permute-start.12
  66.5 6.2 %shard_map.46 = (f32[3,16,16,512]{3,2,1,0:T(8,128)}, f32[2,16,4,32,128]{4,3,2,1,0:T(8,128)S(1)}, f32[3,14,4,32,128]{4,3,2,1,0:T(8,128)S(1)}, f32[3,12,4,32,128]{...) custom-call(f32[3,16,16,512]{3,2,1,0:T(8,128)S(1)} %get-tuple-elemen, ...), custom_call_target="tpu_custom_call" | custom-call | flops 26214400 | bytes 2621440 | tf_op jit(solution)/shard_map/pallas_call | solution.py:630
  72.7 0.0 collective-permute-done.9.face_xa
  72.7 0.0 collective-permute-done.10.face_xb
  72.7 0.0 collective-permute-done.11.corner_a
  72.7 0.0 collective-permute-done.12.corner_b
  72.7 4.3 %shard_map.47 = f32[3,16,16,512]{3,2,1,0:T(8,128)} custom-call(f32[16,8,128]{2,1,0:T(8,128)S(1)} %all_to_all.11.refs_4_.sums0, f32[4,4,16,512]{3,2,1,0:T(8,128)S(1)} %collective-permute-done.9.face_xa, f32[4,4,16,512]{3,2,1,0:T(8,128)S(1)} %collective-permute-done.10.face_xb, f32[2,4,8,512]{3,2,1,0:T(8,128)S(1)} %collective-permute-done.11.corner_a, ...), custom_call_target="tpu_custom_call" | custom-call | flops 26214400 | bytes 2621440 | tf_op jit(solution)/shard_map/pallas_call | solution.py:630
  (1 shorter events, 0.0 us)
Async XLA Ops:
  0.6 1.4 %copy-start = (f32[3,16,16,512]{3,2,1,0:T(8,128)S(1)}, f32[3,16,16,512]{3,2,1,0:T(8,128)}, u32[]{:S(2)}) copy-start(f32[3,16,16,512]{3,2,1,0:T(8,128)} %magnetic.1) | copy-start | bytes 4718596
  4.1 5.1 %collective-permute-start = (f32[3,16,4,512]{3,2,1,0:T(4,128)}, f32[3,16,4,512]{3,2,1,0:T(4,128)S(1)}, u32[]{:S(2)}, u32[]{:S(2)}) collective-permute-start(f32[3,16,4,512]{3,2,1,0:T(4,128)} %get-tuple-element.31), channel_id=1, source_target_pairs={{0,4},{1,5},{2,6},{3,7},{4,0},{5,1},{6,2},{7,3},{8,12},{9,13},{10,... | collective-permute-start | bytes 1179656 | tf_op jit(solution)/shard_map/ppermute | solution.py:63
  4.5 10.5 %collective-permute-start.1 = (f32[3,16,4,512]{3,2,1,0:T(4,128)}, f32[3,16,4,512]{3,2,1,0:T(4,128)S(1)}, u32[]{:S(2)}, u32[]{:S(2)}) collective-permute-start(f32[3,16,4,512]{3,2,1,0:T(4,128)} %get-tuple-element.32), channel_id=1, source_target_pairs={{0,16},{1,17},{2,18},{3,19},{4,8},{5,9},{6,10},{7,11},{8,4},{9,5},... | collective-permute-start | bytes 1179656 | tf_op jit(solution)/shard_map/ppermute | solution.py:63
  7.0 14.8 %collective-permute-start.2 = (f32[3,4,16,512]{3,2,1,0:T(8,128)}, f32[3,4,16,512]{3,2,1,0:T(8,128)S(1)}, u32[]{:S(2)}, u32[]{:S(2)}) collective-permute-start(f32[3,4,16,512]{3,2,1,0:T(8,128)} %get-tuple-element.36), channel_id=1, source_target_pairs={{0,1},{1,0},{2,3},{3,2},{4,5},{5,4},{6,7},{7,6},{8,9},{9,8},{10,11... | collective-permute-start | bytes 1179656 | tf_op jit(solution)/shard_map/ppermute | solution.py:63
  8.6 14.7 %collective-permute-start.3 = (f32[3,4,16,512]{3,2,1,0:T(8,128)S(1)}, f32[3,4,16,512]{3,2,1,0:T(8,128)S(1)}, u32[]{:S(2)}, u32[]{:S(2)}) collective-permute-start(f32[3,4,16,512]{3,2,1,0:T(8,128)S(1)} %get-tuple-element.37), channel_id=1, source_target_pairs={{0,16},{1,2},{2,1},{3,19},{4,20},{5,6},{6,5},{7,23},{8,24},{9,10},... | collective-permute-start | bytes 1179656 | tf_op jit(solution)/shard_map/ppermute | solution.py:63
  15.2 10.5 %collective-permute-start.5 = (f32[3,4,8,512]{3,2,1,0:T(8,128)S(1)}, f32[3,4,8,512]{3,2,1,0:T(8,128)S(1)}, u32[]{:S(2)}, u32[]{:S(2)}) collective-permute-start(f32[3,4,8,512]{3,2,1,0:T(8,128)S(1)} %get-tuple-element.58), channel_id=1, source_target_pairs={{0,16},{1,2},{2,1},{3,19},{4,20},{5,6},{6,5},{7,23},{8,24},{9,10},... | collective-permute-start | bytes 589832 | tf_op jit(solution)/shard_map/ppermute | solution.py:63
  17.6 8.0 %collective-permute-start.4 = (f32[3,4,8,512]{3,2,1,0:T(8,128)S(1)}, f32[3,4,8,512]{3,2,1,0:T(8,128)S(1)}, u32[]{:S(2)}, u32[]{:S(2)}) collective-permute-start(f32[3,4,8,512]{3,2,1,0:T(8,128)S(1)} %get-tuple-element.59), channel_id=1, source_target_pairs={{0,1},{1,0},{2,3},{3,2},{4,5},{5,4},{6,7},{7,6},{8,9},{9,8},{10,11... | collective-permute-start | bytes 589832 | tf_op jit(solution)/shard_map/ppermute | solution.py:63
  25.6 15.0 %copy-start.1 = (f32[16]{0:T(128)S(1)}, f32[16]{0:T(128)}, u32[]{:S(2)}) copy-start(f32[16]{0:T(128)} %param.3) | copy-start | bytes 196
  46.1 2.6 %collective-permute-start.6 = (f32[81,4,512]{2,1,0:T(4,128)S(1)}, f32[81,4,512]{2,1,0:T(4,128)S(1)}, u32[]{:S(2)}, u32[]{:S(2)}) collective-permute-start(f32[81,4,512]{2,1,0:T(4,128)S(1)} %get-tuple-element.44), channel_id=1, source_target_pairs={{0,4},{1,5},{2,6},{3,7},{4,0},{5,1},{6,2},{7,3},{8,12},{9,13},{10,... | collective-permute-start | bytes 1990664 | tf_op jit(solution)/shard_map/ppermute | solution.py:63
  46.3 17.9 %collective-permute-start.7 = (f32[65,4,512]{2,1,0:T(4,128)S(1)}, f32[65,4,512]{2,1,0:T(4,128)S(1)}, u32[]{:S(2)}, u32[]{:S(2)}) collective-permute-start(f32[65,4,512]{2,1,0:T(4,128)S(1)} %get-tuple-element.45), channel_id=1, source_target_pairs={{0,16},{1,17},{2,18},{3,19},{4,8},{5,9},{6,10},{7,11},{8,4},{9,5},... | collective-permute-start | bytes 1597448 | tf_op jit(solution)/shard_map/ppermute | solution.py:63
  47.8 24.9 %collective-permute-start.9 = (f32[4,4,16,512]{3,2,1,0:T(8,128)S(1)}, f32[4,4,16,512]{3,2,1,0:T(8,128)S(1)}, u32[]{:S(2)}, u32[]{:S(2)}) collective-permute-start(f32[4,4,16,512]{3,2,1,0:T(8,128)S(1)} %get-tuple-element.48), channel_id=1, source_target_pairs={{0,1},{1,0},{2,3},{3,2},{4,5},{5,4},{6,7},{7,6},{8,9},{9,8},{10,11... | collective-permute-start | bytes 1572872 | tf_op jit(solution)/shard_map/ppermute | solution.py:63
  48.1 24.5 %collective-permute-start.10 = (f32[4,4,16,512]{3,2,1,0:T(8,128)S(1)}, f32[4,4,16,512]{3,2,1,0:T(8,128)S(1)}, u32[]{:S(2)}, u32[]{:S(2)}) collective-permute-start(f32[4,4,16,512]{3,2,1,0:T(8,128)S(1)} %get-tuple-element.49), channel_id=1, source_target_pairs={{0,16},{1,2},{2,1},{3,19},{4,20},{5,6},{6,5},{7,23},{8,24},{9,10},... | collective-permute-start | bytes 1572872 | tf_op jit(solution)/shard_map/ppermute | solution.py:63
  48.7 15.5 %collective-permute-start.8 = (f32[16,4,512]{2,1,0:T(4,128)S(1)}, f32[16,4,512]{2,1,0:T(4,128)S(1)}, u32[]{:S(2)}, u32[]{:S(2)}) collective-permute-start(f32[16,4,512]{2,1,0:T(4,128)S(1)} %get-tuple-element.60), channel_id=1, source_target_pairs={{0,8},{4,12},{8,0},{12,4},{1,9},{5,13},{9,1},{13,5},{2,10},{6,14},... | collective-permute-start | bytes 393224 | tf_op jit(solution)/shard_map/ppermute | solution.py:712
  65.1 7.6 %collective-permute-start.11 = (f32[2,4,8,512]{3,2,1,0:T(8,128)S(1)}, f32[2,4,8,512]{3,2,1,0:T(8,128)S(1)}, u32[]{:S(2)}, u32[]{:S(2)}) collective-permute-start(f32[2,4,8,512]{3,2,1,0:T(8,128)S(1)} %get-tuple-element.50), channel_id=1, source_target_pairs={{0,1},{1,0},{2,3},{3,2},{4,5},{5,4},{6,7},{7,6},{8,9},{9,8},{10,11... | collective-permute-start | bytes 393224 | tf_op jit(solution)/shard_map/ppermute | solution.py:63
  65.9 6.8 %collective-permute-start.12 = (f32[2,4,8,512]{3,2,1,0:T(8,128)S(1)}, f32[2,4,8,512]{3,2,1,0:T(8,128)S(1)}, u32[]{:S(2)}, u32[]{:S(2)}) collective-permute-start(f32[2,4,8,512]{3,2,1,0:T(8,128)S(1)} %get-tuple-element.51), channel_id=1, source_target_pairs={{0,16},{1,2},{2,1},{3,19},{4,20},{5,6},{6,5},{7,23},{8,24},{9,10},... | collective-permute-start | bytes 393224 | tf_op jit(solution)/shard_map/ppermute | solution.py:63

commit v3 on v2

--- a/solution.py
+++ b/solution.py
@@ -41,21 +41,16 @@
         to = at + 1 if at % 2 else at - 1
         if 0 <= to < sizes[along]:
             second.append((flat(place), flat(moved(place, axis, to))))
-        elif sizes[0] % 2 == 0:
-            second.append((flat(place), flat(moved(place, "runs", place[0] ^ 1))))
+        else:
+            idle = "gz" if axis == "gx" else "runs"
+            at = place[AXES.index(idle)] ^ 1
+            if at < sizes[AXES.index(idle)]:
+                second.append((flat(place), flat(moved(place, idle, at))))
     return first, second
 
 
 def is_even(axis):
     return lax.axis_index(axis) % 2 == 0
-
-
-def edges(cells, axis, dim):
-    far = cells.shape[dim] - HALO
-    even = is_even(axis)
-    first = lax.dynamic_slice_in_dim(cells, jnp.where(even, far, 0), HALO, dim)
-    second = lax.dynamic_slice_in_dim(cells, jnp.where(even, 0, far), HALO, dim)
-    return first, second
 
 
 def swapped(pair, axis):
@@ -232,6 +227,36 @@
         return functional, slope
 
     return lax.fori_loop(0, planes, plane, sums, unroll=4)
+
+
+def corner_row(d):
+    return sum(HALO - k for k in range(1, d))
+
+
+def corner_rows(corner, first, d):
+    high, low = [corner[at : at + HALO - d] for at in (first + corner_row(d), first + corner_row(HALO) + corner_row(d))]
+    none = jnp.zeros((d, LANES), jnp.float32)
+    if d == HALO:
+        return none, none
+    return jnp.concatenate([high, none], 0), jnp.concatenate([none, low], 0)
+
+
+def corners_kernel(face_za, face_zb, corner_a, corner_b):
+    _, cx, _, ny = face_za.shape
+    even_x = is_even("gx")
+    for j in range(ny // LANES):
+        cut = slice(j * LANES, (j + 1) * LANES)
+        packed = []
+        for edge in (lambda d: d - 1, lambda d: cx - d):
+            pieces = []
+            for c in range(3):
+                rims = [sorted_out("gz", face_za[c, edge(d), :, cut], face_zb[c, edge(d), :, cut]) for d in range(1, HALO)]
+                pieces += [high[: HALO - d] for d, (_, high) in enumerate(rims, 1)]
+                pieces += [low[d:] for d, (low, _) in enumerate(rims, 1)]
+            pieces.append(jnp.zeros((corner_a.shape[0] - 6 * corner_row(HALO), LANES), jnp.float32))
+            packed.append(jnp.concatenate(pieces, axis=0))
+        corner_a[:, cut] = jnp.where(even_x, packed[1], packed[0])
+        corner_b[:, cut] = jnp.where(even_x, packed[0], packed[1])
 
 
 def z_halos(bp, c, plane, j, top, a, b):
@@ -280,25 +305,28 @@
     rows = row_index()
     top = BASE + cz
 
-    def rim(x, _):
+    def copied(x, _):
+        for c in range(3):
+            for j in range(blocks):
+                for r in range(0, top + BASE, ROWS):
+                    bp[c, x + HALO, j, r : r + ROWS, :] = own[c, x, j, r : r + ROWS, :]
+                    bp[c, x + 2 * HALO, j, r : r + ROWS, :] = own[c, x + cx - HALO, j, r : r + ROWS, :]
+        return 0
+
+    lax.fori_loop(0, HALO, copied, 0)
+    for d in range(1, HALO + 1):
         for c in range(3):
             for j in range(blocks):
                 cut = slice(j * LANES, (j + 1) * LANES)
-                planes = (x, x + 3 * HALO)
-                for r in range(0, top + BASE, ROWS):
-                    bp[c, x + HALO, j, r : r + ROWS, :] = own[c, x, j, r : r + ROWS, :]
-                    bp[c, x + 2 * HALO, j, r : r + ROWS, :] = own[c, x + cx - HALO, j, r : r + ROWS, :]
-                for z in range(0, cz, ROWS):
-                    span = slice(z, z + ROWS)
-                    both = sorted_out("gx", face_xa[c, x, span, cut], face_xb[c, x, span, cut])
-                    for plane, value in zip(planes, both):
+                corners = sorted_out("gx", corner_a[:, cut], corner_b[:, cut])
+                for side, (plane, k) in enumerate(((HALO - d, HALO - d), (3 * HALO + d - 1, d - 1))):
+                    for z in range(0, cz, ROWS):
+                        span = slice(z, z + ROWS)
+                        value = sorted_out("gx", face_xa[c, k, span, cut], face_xb[c, k, span, cut])[side]
                         bp[c, plane, j, BASE + z : BASE + z + ROWS, :] = value
-                both = sorted_out("gx", corner_a[c, x, :, cut], corner_b[c, x, :, cut])
-                for plane, value in zip(planes, both):
-                    z_halos(bp, c, plane, j, top, value[:HALO], value[HALO:])
-        return 0
-
-    lax.fori_loop(0, HALO, rim, 0)
+                    high, low = corner_rows(corners[side], 2 * c * corner_row(HALO), d)
+                    bp[c, plane, j, BASE - HALO : BASE, :] = low
+                    bp[c, plane, j, top : top + HALO, :] = high
     descent_stages(bp, lambda x: x + 1 + jnp.where(x >= 6, 2, 0), 12, halo, cz, blocks, omega_ref)
     functional, slope = first_forces(
         bp,
@@ -318,7 +346,7 @@
 
 
 def second_kernel(
-    cells, own_b, inner_f, outer_b, outer_f, sums0, friction, core_b, core_f, face_xa, face_xb, face_za, face_zb, sums_ref, bp, omega_ref
+    cells, own_b, inner_f, outer_b, outer_f, sums0, core_b, core_f, bp, sums_ref, omega_ref
 ):
     _, cx, cz, ny = core_b.shape
     blocks = ny // LANES
@@ -358,39 +386,61 @@
                 for c in range(3):
                     core_b[c, x, z : z + ROWS, cut] = field[c]
                     core_f[c, x, z : z + ROWS, cut] = force[c]
-        for j in range(blocks):
-            cut = slice(j * LANES, (j + 1) * LANES)
-            for k, (source, c) in enumerate(((core_f, 0), (core_f, 1), (core_b, 0), (core_b, 1))):
-                low, high = source[c, x, 0:HALO, cut], source[c, x, cz - HALO : cz, cut]
-                face_za[k * cx + x, :, cut] = jnp.where(even_z, high, low)
-                face_zb[k * cx + x, :, cut] = jnp.where(even_z, low, high)
-                column = source[c, x, 0:ROWS, cut]
-                for z in range(ROWS, cz, ROWS):
-                    column = column + source[c, x, z : z + ROWS, cut]
-                face_za[4 * cx + 1 + x, k : k + 1, cut] = jnp.sum(column, axis=0, keepdims=True)
         return functional, slope
 
     zero = jnp.zeros((ROWS, LANES), jnp.float32)
     functional, slope = lax.fori_loop(0, cx, plane, (zero, zero), unroll=4)
     store_sums(sums_ref, functional, slope, rows)
 
-    def faces(x, _):
+
+LAYERS = [(0, 0, d) for d in (1, 2, 3, 4)] + [(0, 1, d) for d in (1, 2, 3)] + [(1, 0, 3), (1, 0, 4), (1, 1, 3)]
+
+
+def faces_kernel(core_b, core_f, friction, face_xa, face_xb, face_za, face_zb):
+    _, cx, cz, ny = core_b.shape
+    blocks = ny // LANES
+    even_x, even_z = is_even("gx"), is_even("gz")
+
+    def plane(x, _):
         for j in range(blocks):
             cut = slice(j * LANES, (j + 1) * LANES)
+            for c in range(2):
+                low, high = core_f[c, x, 0:HALO, cut], core_f[c, x, cz - HALO : cz, cut]
+                face_za[c * cx + x, :, cut] = jnp.where(even_z, high, low)
+                face_zb[c * cx + x, :, cut] = jnp.where(even_z, low, high)
+                low, high = core_b[c, x, 2:4, cut], core_b[c, x, cz - 4 : cz - 2, cut]
+                face_za[2 * cx + x, 2 * c : 2 * c + 2, cut] = jnp.where(even_z, high, low)
+                face_zb[2 * cx + x, 2 * c : 2 * c + 2, cut] = jnp.where(even_z, low, high)
             for k, (source, c) in enumerate(((core_f, 0), (core_f, 1), (core_b, 0), (core_b, 1))):
-                for z in range(0, cz, ROWS):
-                    low = source[c, x, z : z + ROWS, cut]
-                    high = source[c, x + cx - HALO, z : z + ROWS, cut]
-                    face_xa[k, x, z : z + ROWS, cut] = jnp.where(even_x, high, low)
-                    face_xb[k, x, z : z + ROWS, cut] = jnp.where(even_x, low, high)
-        return 0
-
-    lax.fori_loop(0, HALO, faces, 0)
+                value = source[c, x, 0:ROWS, cut]
+                for z in range(ROWS, cz, ROWS):
+                    value = value + source[c, x, z : z + ROWS, cut]
+                face_za[3 * cx + 1 + x, k : k + 1, cut] = jnp.sum(value, axis=0, keepdims=True)
+        return 0
+
+    lax.fori_loop(0, cx, plane, 0, unroll=4)
     for j in range(blocks):
         cut = slice(j * LANES, (j + 1) * LANES)
+        for k, (which, c, d) in enumerate(LAYERS):
+            source = (core_f, core_b)[which]
+            for z in range(0, cz, ROWS):
+                low, high = source[c, d - 1, z : z + ROWS, cut], source[c, cx - d, z : z + ROWS, cut]
+                face_xa[k, z : z + ROWS, cut] = jnp.where(even_x, high, low)
+                face_xb[k, z : z + ROWS, cut] = jnp.where(even_x, low, high)
         low, high = friction[0:HALO], friction[cz - HALO : cz]
-        face_za[4 * cx, :, cut] = jnp.where(even_z, high, low)
-        face_zb[4 * cx, :, cut] = jnp.where(even_z, low, high)
+        face_za[3 * cx, :, cut] = jnp.where(even_z, high, low)
+        face_zb[3 * cx, :, cut] = jnp.where(even_z, low, high)
+
+
+def z_rims(face_za, face_zb, bp, rate, cx, cz, c, x, j):
+    cut = slice(j * LANES, (j + 1) * LANES)
+    top = BASE + cz
+    force = sorted_out("gz", face_za[c * cx + x, :, cut], face_zb[c * cx + x, :, cut])
+    span = slice(2 * c, 2 * c + 2)
+    far = sorted_out("gz", face_za[2 * cx + x, span, cut], face_zb[2 * cx + x, span, cut])
+    low = jnp.concatenate([far[0], bp[c, x + 2, j, BASE - 2 : BASE, :]], axis=0)
+    high = jnp.concatenate([bp[c, x + 2, j, top : top + 2, :], far[1]], axis=0)
+    return low + rate * force[0], high + rate * force[1]
 
 
 def suffix(value, rows):
@@ -496,7 +546,7 @@
 
 
 def middle_kernel(
-    cells, core_b, core_f, sums0, friction, face_za, face_zb, above, relaxed, ap, bm, an, bn, inner, rub
+    cells, core_b, core_f, bp, sums0, friction, face_za, face_zb, above, relaxed, ap, bm, an, bn, inner, rub
 ):
     _, cx, cz, ny = core_b.shape
     blocks = ny // LANES
@@ -506,7 +556,7 @@
     top = BASE + cz
 
     rub[BASE:top] = friction[...]
-    low, high = sorted_out("gz", face_za[4 * cx, :, :LANES], face_zb[4 * cx, :, :LANES])
+    low, high = sorted_out("gz", face_za[3 * cx, :, :LANES], face_zb[3 * cx, :, :LANES])
     rub[BASE - HALO : BASE] = low
     rub[top : top + HALO] = high
     for r in range(0, cz + 2 * BASE, ROWS):
@@ -526,10 +576,7 @@
                     relaxed[c, x, z : z + ROWS, cut] = own[z // ROWS]
                 if c == 2:
                     continue
-                a, b = [
-                    face[(2 + c) * cx + x, :, cut] + rate * face[c * cx + x, :, cut] for face in (face_za, face_zb)
-                ]
-                low, high = sorted_out("gz", a, b)
+                low, high = z_rims(face_za, face_zb, bp, rate, cx, cz, c, x, j)
                 column(ap, c, x, j, low, own, high, above[x, c : c + 1, cut], rows)
         return 0
 
@@ -544,30 +591,38 @@
 
 
 def ends_kernel(
-    cells, sums0, face_xa, face_xb, corner_a, corner_b, own_ap, own_bm, own_an, own_bn, inner, rub, potential, ap, bm, an, rim
+    cells, bp, sums0, face_xa, face_xb, corner_a, corner_b, own_ap, own_bm, own_an, own_bn, inner, rub, potential, ap, bm, an, rim
 ):
     _, cx, cz, ny = potential.shape
     blocks = ny // LANES
     rows = row_index()
     rate = half_rate(sums0, cells)
 
-    def rim_plane(x, _):
-        for j in range(blocks):
-            cut = slice(j * LANES, (j + 1) * LANES)
-            for c in range(2):
-                own = []
+    for d in range(1, HALO + 1):
+        for c in range(2):
+            if (0, c, d) not in LAYERS:
+                continue
+            for j in range(blocks):
+                cut = slice(j * LANES, (j + 1) * LANES)
+
+                def layer(which, span):
+                    k = LAYERS.index((which, c, d))
+                    return sorted_out("gx", face_xa[k, span, cut], face_xb[k, span, cut])
+
+                own = ([], [])
                 for z in range(0, cz, ROWS):
-                    span = slice(z, z + ROWS)
-                    a, b = [face[2 + c, x, span, cut] + rate * face[c, x, span, cut] for face in (face_xa, face_xb)]
-                    own.append(sorted_out("gx", a, b))
-                corners = sorted_out("gx", corner_a[c, x, :, cut], corner_b[c, x, :, cut])
-                for side, plane in enumerate((x, x + 2 * HALO)):
+                    force = layer(0, slice(z, z + ROWS))
+                    if d <= 2:
+                        field = [bp[c, at, j, BASE + z : BASE + z + ROWS, :] for at in (2 - d, cx + 1 + d)]
+                    else:
+                        field = layer(1, slice(z, z + ROWS))
+                    for side in range(2):
+                        own[side].append(field[side] + rate * force[side])
+                corners = sorted_out("gx", corner_a[c, :, cut], corner_b[c, :, cut])
+                for side, plane in enumerate((HALO - d, 2 * HALO + d - 1)):
                     corner = corners[side]
-                    high = jnp.concatenate([corner[1:4], corner[3:4]], 0)
-                    column(ap, c, plane, j, corner[4:8], [pair[side] for pair in own], high, corner[0:1], rows)
-        return 0
-
-    lax.fori_loop(0, HALO, rim_plane, 0)
+                    high, low = corner_rows(corner, HALO, d)
+                    column(ap, c, plane, j, low, own[side], high, corner[d - 1 : d], rows)
 
     def borrow(into, source, low, high):
         for k in range(2):
@@ -596,8 +651,9 @@
 
 
 def pack_kernel(cells, count, *refs):
-    columns, (face_za, face_zb, sums0, above, corner_a, corner_b) = refs[:count], refs[count:]
-    cx = above.shape[0]
+    columns, (face_za, face_zb, bp, sums0, above, corner_a, corner_b) = refs[:count], refs[count:]
+    cx, _, ny = above.shape
+    cz = bp.shape[3] - 2 * BASE
     even_x = is_even("gx")
     place = lax.axis_index("gz")
     rate = half_rate(sums0, cells)
@@ -609,20 +665,19 @@
         above[x] = column[2:4] + rate * column[0:2]
         return 0
 
-    lax.fori_loop(0, cx, total, 0)
-
-    def plane(x, _):
-        for c in range(2):
+    lax.fori_loop(0, cx, total, 0, unroll=4)
+    for c in range(2):
+        for j in range(ny // LANES):
+            cut = slice(j * LANES, (j + 1) * LANES)
             packed = []
-            for at in (x, x + cx - HALO):
-                a, b = [face[(2 + c) * cx + at] + rate * face[c * cx + at] for face in (face_za, face_zb)]
-                low, high = sorted_out("gz", a, b)
-                packed.append(jnp.concatenate([above[at, c : c + 1], high[0 : HALO - 1], low], axis=0))
-            corner_a[c, x] = jnp.where(even_x, packed[1], packed[0])
-            corner_b[c, x] = jnp.where(even_x, packed[0], packed[1])
-        return 0
-
-    lax.fori_loop(0, HALO, plane, 0)
+            for edge in (lambda d: d - 1, lambda d: cx - d):
+                rims = [z_rims(face_za, face_zb, bp, rate, cx, cz, c, edge(d), j) for d in range(1, HALO)]
+                pieces = [above[edge(d), c : c + 1, cut] for d in range(1, HALO + 1)]
+                pieces += [high[: HALO - d] for d, (_, high) in enumerate(rims, 1)]
+                pieces += [low[d:] for d, (low, _) in enumerate(rims, 1)]
+                packed.append(jnp.concatenate(pieces, axis=0))
+            corner_a[c, :, cut] = jnp.where(even_x, packed[1], packed[0])
+            corner_b[c, :, cut] = jnp.where(even_x, packed[0], packed[1])
 
 
 def call(kernel, outs, *args, scratch=(), cost=0, limit=8, outside=0):
@@ -668,7 +723,13 @@
     )
     faces_x = swapped(faces[:2], "gx")
     faces_z = swapped(faces[2:], "gz")
-    corners = swapped(edges(jnp.concatenate(faces_z, axis=2), "gx", 1), "gx")
+    corners = call(
+        corners_kernel,
+        [(-(-6 * corner_row(HALO) // ROWS) * ROWS, ny)] * 2,
+        *faces_z,
+        cost=work // 50,
+    )
+    corners = swapped(corners, "gx")
     own_b, inner_f, part = call(
         inner_kernel,
         [padded(3, 0), padded(3, -2), (2, ROWS, LANES)],
@@ -689,24 +750,31 @@
         cost=work,
         limit=12,
     )
-    core_b, core_f, *faces, sums = call(
+    core_b, core_f, bp, sums = call(
         functools.partial(second_kernel, cells),
-        [core, core, (4, HALO, cz, ny), (4, HALO, cz, ny), (5 * cx + 1, HALO, ny), (4 * cx + 1, HALO, ny), tiles],
+        [core, core, padded(3, HALO - 2), tiles],
         own_b,
         inner_f,
         outer_b,
         outer_f,
         shared(sums),
+        scratch=[padded(11, 1)],
+        cost=work,
+        limit=15,
+    )
+    faces = call(
+        faces_kernel,
+        [*[(len(LAYERS), cz, ny)] * 2, (4 * cx + 1, HALO, ny), (3 * cx + 1, HALO, ny)],
+        core_b,
+        core_f,
         rubbed,
-        scratch=[padded(3, HALO - 2), padded(11, 1)],
         cost=work,
-        limit=19,
     )
     faces_z = swapped(faces[2:], "gz")
     faces_x = swapped(faces[:2], "gx")
     sums = shared(sums)
-    columns = [faces_z[0][4 * cx + 1 :]]
-    group = faces[2][4 * cx + 1 :] + columns[0]
+    columns = [faces_z[0][3 * cx + 1 :]]
+    group = faces[2][3 * cx + 1 :] + columns[0]
     stride = 2
     while stride < count_z:
         columns.append(lax.ppermute(group, "gz", [(i, i ^ stride) for i in range(count_z)]))
@@ -715,9 +783,10 @@
             group = group + columns[-1]
     above, *corners = call(
         functools.partial(pack_kernel, cells, len(columns)),
-        [(cx, 2, ny), (2, HALO, 2 * HALO, ny), (2, HALO, 2 * HALO, ny)],
+        [(cx, 2, ny), *[(2, HALO + 2 * corner_row(HALO), ny)] * 2],
         *columns,
         *faces_z,
+        bp,
         sums,
         cost=work // 50,
     )
@@ -727,6 +796,7 @@
         [core, padded(2, 0), padded(3, -1), padded(3, -2), padded(3, -3), (3, cx - 2 * HALO, cz, ny), (height, LANES)],
         core_b,
         core_f,
+        bp,
         sums,
         rubbed,
         *faces_z,
@@ -737,6 +807,7 @@
     (potential,) = call(
         functools.partial(ends_kernel, cells),
         [core],
+        bp,
         sums,
         *faces_x,
         *corners,

time: 77.3 us -> 65.4 us (0.85)
  waiting for transfers between devices: 9.76 us -> 5.77 us
  starting transfers between devices: 13 us -> 9.16 us
  blocking collectives: 25.8 us -> 23.5 us
  Pallas kernels: 26.1 us -> 24.5 us
    ppermute x6, waiting for transfers between devices: 9.74 us -> 4.19 us  [swapped(): lax.ppermute(pair[1], AXES, second)]
    ppermute x6, starting transfers between devices: 8.12 us -> 3.19 us  [swapped(): lax.ppermute(pair[1], AXES, second)]
    all_to_all x2, blocking collectives: 25.8 us -> 23.5 us  [shared(): return lax.all_to_all(tile_copies, ('gz', 'gx'), 0, 0)]
    ppermute x6, starting transfers between devices: 3.36 us -> 5.17 us  [swapped(): lax.ppermute(pair[0], AXES, first)]
    pallas_call x7 -> x9, Pallas kernels: 26.1 us -> 24.5 us  [call(): pl.pallas_call(kernel, out_shape=shapes, in_specs=[pl.BlockSpec(memory_sp...]
    ppermute x6, waiting for transfers between devices: 0.02 us -> 1.58 us  [swapped(): lax.ppermute(pair[0], AXES, first)]
  transfers between devices with their start and end apart: 13 -> 13, of which waited for: 3 -> 3; matrix products, arithmetic and copies ran while one was open for 0% -> 0% of each run, Pallas kernels for 15% -> 17%
where the time goes in v3:
time: 65.4 us; the launch traced here: 65.1 us
  Pallas kernels  24.5 us (37%)
  blocking collectives  23.5 us (36%)
  starting transfers between devices  9.16 us (14%)
  waiting for transfers between devices  5.77 us (9%)
  local copies, waits for them, and re-layouts  1.48 us (2%)
  between operations  0.73 us (1%)
    pallas_call x9, Pallas kernels, call(): pl.pallas_call(kernel, out_shape=shapes, in_specs=[pl.BlockSpec(memory_sp...  24.5 us
    all_to_all x2, blocking collectives, shared(): return lax.all_to_all(tile_copies, ('gz', 'gx'), 0, 0)  23.5 us
    ppermute x6, starting transfers between devices, swapped(): lax.ppermute(pair[0], AXES, first)  5.17 us
    ppermute x6, waiting for transfers between devices, swapped(): lax.ppermute(pair[1], AXES, second)  4.19 us
    ppermute x6, starting transfers between devices, swapped(): lax.ppermute(pair[1], AXES, second)  3.19 us
    ppermute x6, waiting for transfers between devices, swapped(): lax.ppermute(pair[0], AXES, first)  1.58 us
    unnamed x4, local copies, waits for them, and re-layouts  1.4 us
  transfers between devices with their start and end apart: 13, of which 3 were waited for; matrix products, arithmetic and copies ran while one was open for 0% of the time, Pallas kernels for 17%

profile of v3, /device:TPU:0, one launch (start us, length us, event | category | flops | bytes accessed | tf_op | source)
XLA Modules:
  0.0 65.1 jit_solution(7028481086930279704)
XLA Ops:
  0.6 0.0 copy-start
  0.6 1.4 %copy-done = f32[3,16,16,512]{3,2,1,0:T(8,128)S(1)} copy-done((f32[3,16,16,512]{3,2,1,0:T(8,128)S(1)}, f32[3,16,16,512]{3,2,1,0:T(8,128)}, u32[]{:S(2)}) %copy-start) | copy-done | bytes 1572888
  2.0 1.0 %shard_map.41 = (f32[3,16,16,512]{3,2,1,0:T(8,128)S(1)}, f32[3,4,16,512]{3,2,1,0:T(8,128)S(1)}, f32[3,4,16,512]{3,2,1,0:T(8,128)S(1)}, f32[3,16,4,512]{3,2,1,0:T(4,128)S(1)}, f32[3,16,4,512]{3,2,1,0:T(4,128)S(1)}) custom-call(f32[3,16,16,512]{3,2,1,0:T(8,128)S(1)} %copy-done), custom_call_target="tpu_custom_call" | custom-call | flops 26214400 | bytes 2621440 | tf_op jit(solution)/shard_map/pallas_call | solution.py:685
  3.1 0.5 collective-permute-start
  3.6 2.6 %collective-permute-start.1 = (f32[3,16,4,512]{3,2,1,0:T(4,128)S(1)}, f32[3,16,4,512]{3,2,1,0:T(4,128)S(1)}, u32[]{:S(2)}, u32[]{:S(2)}) collective-permute-start(f32[3,16,4,512]{3,2,1,0:T(4,128)S(1)} %get-tuple-element.35), channel_id=1, source_target_pairs={{0,16},{1,17},{2,18},{3,19},{4,8},{5,9},{6,10},{7,11},{8,4},{9,5},... | collective-permute-start | bytes 1179656 | tf_op jit(solution)/shard_map/ppermute | solution.py:58
  6.2 1.6 %collective-permute-start.2 = (f32[3,4,16,512]{3,2,1,0:T(8,128)S(1)}, f32[3,4,16,512]{3,2,1,0:T(8,128)S(1)}, u32[]{:S(2)}, u32[]{:S(2)}) collective-permute-start(f32[3,4,16,512]{3,2,1,0:T(8,128)S(1)} %get-tuple-element.39), channel_id=1, source_target_pairs={{0,1},{1,0},{2,3},{3,2},{4,5},{5,4},{6,7},{7,6},{8,9},{9,8},{10,11... | collective-permute-start | bytes 1179656 | tf_op jit(solution)/shard_map/ppermute | solution.py:58
  7.7 0.0 collective-permute-start.3
  7.7 0.0 collective-permute-done.face_za
  7.7 4.2 %collective-permute-done.1.face_zb = f32[3,16,4,512]{3,2,1,0:T(4,128)S(1)} collective-permute-done((f32[3,16,4,512]{3,2,1,0:T(4,128)S(1)}, f32[3,16,4,512]{3,2,1,0:T(4,128)S(1)}, u32[]{:S(2)}, u32[]{:S(2)}) %collective-permute-start.1) | collective-permute-done | bytes 393248 | tf_op jit(solution)/shard_map/ppermute | solution.py:58
  11.9 0.1 shard_map.43
  12.0 2.1 %collective-permute-start.4 = (f32[40,512]{1,0:T(8,128)S(1)}, f32[40,512]{1,0:T(8,128)S(1)}, u32[]{:S(2)}, u32[]{:S(2)}) collective-permute-start(f32[40,512]{1,0:T(8,128)S(1)} %get-tuple-element.41), channel_id=1, source_target_pairs={{0,1},{1,0},{2,3},{3,2},{4,5},{5,4},{6,7},{7,6},{8,9},{9,8},{10,11... | collective-permute-start | bytes 245768 | tf_op jit(solution)/shard_map/ppermute | solution.py:58
  14.2 0.0 collective-permute-start.5
  14.2 4.1 %shard_map.42 = (f32[3,16,4,32,128]{4,3,2,1,0:T(8,128)S(1)}, f32[3,12,4,32,128]{4,3,2,1,0:T(8,128)S(1)}, f32[2,8,128]{2,1,0:T(8,128)S(1)}) custom-call(f32[3,16,16,512]{3,2,1,0:T(8,128)S(1)} %get-tuple-element.33.core, f32[3,16,4,512]{3,2,1,0:T(4,128)S(1)} %collective-permute-done.face_za, f32[3,16,4,512]{3,2,1,0:T(4,128)S(1)} %collective-permute-done.1.face_zb), custom_call_target="tpu_custom_call" | custom-call | flops 26214400 | bytes 2621440 | tf_op jit(solution)/shard_map/pallas_call | solution.py:685
  18.3 0.0 collective-permute-done.2.face_xa
  18.3 0.0 collective-permute-done.3.face_xb
  18.3 0.7 %collective-permute-done.4.corner_a = f32[40,512]{1,0:T(8,128)S(1)} collective-permute-done((f32[40,512]{1,0:T(8,128)S(1)}, f32[40,512]{1,0:T(8,128)S(1)}, u32[]{:S(2)}, u32[]{:S(2)}) %collective-permute-start.4) | collective-permute-done | bytes 81952 | tf_op jit(solution)/shard_map/ppermute | solution.py:58
  19.0 0.0 collective-permute-done.5.corner_b
  19.0 3.1 %shard_map.44 = (f32[3,16,4,32,128]{4,3,2,1,0:T(8,128)S(1)}, f32[3,8,4,32,128]{4,3,2,1,0:T(8,128)S(1)}, f32[16,8,128]{2,1,0:T(8,128)S(1)}) custom-call(f32[3,16,4,32,128]{4,3,2,1,0:T(8,128)S(1)} %get-tuple-element.36.own.own_b, f32[2,8,128]{2,1,0:T(8,128)S(1)} %get-tuple-element.38.part, f32[3,4,16,512]{3,2,1,0:T(8,128)S(1)} %collective-permute-done.2.face_xa, ...), custom_call_target="tpu_custom_call" | custom-call | flops 26214400 | bytes 2621440 | tf_op jit(solution)/shard_map/pallas_call | solution.py:685
  22.1 12.7 %all_to_all.10.sums0 = f32[16,8,128]{2,1,0:T(8,128)S(1)} all-to-all(f32[16,8,128]{2,1,0:T(8,128)S(1)} %get-tuple-element.45), channel_id=1, replica_groups=mesh['runs'=2,'gz'=4,'gx'=4] {'gz','gx'}, dimensions={0} | all-to-all | bytes 131072 | tf_op jit(solution)/shard_map/all_to_all | solution.py:70
  34.8 0.0 copy-start.1
  34.8 4.8 %shard_map.45 = (f32[3,16,16,512]{3,2,1,0:T(8,128)S(1)}, f32[3,16,16,512]{3,2,1,0:T(8,128)S(1)}, f32[3,20,4,32,128]{4,3,2,1,0:T(8,128)S(1)}, f32[16,8,128]{2,1,0:T(8,128)S(1)}) custom-call(f32[3,16,4,32,128]{4,3,2,1,0:T(8,128)S(1)} %get-tuple-element.36.own.own_b, f32[3,12,4,32,128]{4,3,2,1,0:T(8,128)S(1)} %get-tuple-element.37.inner_f, ...), custom_call_target="tpu_custom_call" | custom-call | flops 26214400 | bytes 2621440 | tf_op jit(solution)/shard_map/pallas_call | solution.py:685
  39.6 0.0 copy-done.1
  39.6 0.1 broadcast_in_dim.2.friction
  39.7 0.5 shard_map.46
  40.2 0.2 collective-permute-start.6
  40.4 0.5 collective-permute-start.7
  40.9 0.3 collective-permute-start.9
  41.3 0.1 collective-permute-start.10
  41.3 0.9 %collective-permute-done.6.refs_2_.face_za = f32[65,4,512]{2,1,0:T(4,128)S(1)} collective-permute-done((f32[65,4,512]{2,1,0:T(4,128)S(1)}, f32[65,4,512]{2,1,0:T(4,128)S(1)}, u32[]{:S(2)}, u32[]{:S(2)}) %collective-permute-start.6) | collective-permute-done | bytes 532512 | tf_op jit(solution)/shard_map/ppermute | solution.py:58
  42.2 0.8 %collective-permute-start.8 = (f32[16,4,512]{2,1,0:T(4,128)S(1)}, f32[16,4,512]{2,1,0:T(4,128)S(1)}, u32[]{:S(2)}, u32[]{:S(2)}) collective-permute-start(f32[16,4,512]{2,1,0:T(4,128)S(1)} %get-tuple-element.64), channel_id=1, source_target_pairs={{0,8},{4,12},{8,0},{12,4},{1,9},{5,13},{9,1},{13,5},{2,10},{6,14},... | collective-permute-start | bytes 393224 | tf_op jit(solution)/shard_map/ppermute | solution.py:780
  43.0 10.8 %all_to_all.11.refs_5_.sums0 = f32[16,8,128]{2,1,0:T(8,128)S(1)} all-to-all(f32[16,8,128]{2,1,0:T(8,128)S(1)} %get-tuple-element.49), channel_id=1, replica_groups=mesh['runs'=2,'gz'=4,'gx'=4] {'gz','gx'}, dimensions={0} | all-to-all | bytes 131072 | tf_op jit(solution)/shard_map/all_to_all | solution.py:70
  53.8 0.0 collective-permute-done.7.refs_3_.face_zb
  53.8 0.0 collective-permute-done.8.refs_1_
  53.8 0.4 shard_map.47
  54.2 0.4 collective-permute-start.11
  54.7 0.0 collective-permute-start.12
  54.7 6.3 %shard_map.48 = (f32[3,16,16,512]{3,2,1,0:T(8,128)}, f32[2,16,4,32,128]{4,3,2,1,0:T(8,128)S(1)}, f32[3,14,4,32,128]{4,3,2,1,0:T(8,128)S(1)}, f32[3,12,4,32,128]{...) custom-call(f32[3,16,16,512]{3,2,1,0:T(8,128)S(1)} %get-tuple-elemen, ...), custom_call_target="tpu_custom_call" | custom-call | flops 26214400 | bytes 2621440 | tf_op jit(solution)/shard_map/pallas_call | solution.py:685
  60.9 0.0 collective-permute-done.9.face_xa
  60.9 0.0 collective-permute-done.10.face_xb
  60.9 0.0 collective-permute-done.11.corner_a
  60.9 0.0 collective-permute-done.12.corner_b
  60.9 4.2 %shard_map.49 = f32[3,16,16,512]{3,2,1,0:T(8,128)} custom-call(f32[3,20,4,32,128]{4,3,2,1,0:T(8,128)S(1)} %get-tuple-element.48.refs_4_.bp, f32[16,8,128]{2,1,0:T(8,128)S(1)} %all_to_all.11.refs_5_.sums0, f32[10,16,512]{2,1,0:T(8,128)S(1)} %collective-permute-done.9.face_xa, f32[10,16,512]{2,1,0:T(8,128)S(1)} %collective-permute-done.10.face_xb, ...), custom_call_target="tpu_custom_call" | custom-call | flops 26214400 | bytes 2621440 | tf_op jit(solution)/shard_map/pallas_call | solution.py:685
  (1 shorter events, 0.0 us)
Async XLA Ops:
  0.6 1.4 %copy-start = (f32[3,16,16,512]{3,2,1,0:T(8,128)S(1)}, f32[3,16,16,512]{3,2,1,0:T(8,128)}, u32[]{:S(2)}) copy-start(f32[3,16,16,512]{3,2,1,0:T(8,128)} %magnetic.1) | copy-start | bytes 4718596
  3.1 4.7 %collective-permute-start = (f32[3,16,4,512]{3,2,1,0:T(4,128)S(1)}, f32[3,16,4,512]{3,2,1,0:T(4,128)S(1)}, u32[]{:S(2)}, u32[]{:S(2)}) collective-permute-start(f32[3,16,4,512]{3,2,1,0:T(4,128)S(1)} %get-tuple-element.34), channel_id=1, source_target_pairs={{0,4},{1,5},{2,6},{3,7},{4,0},{5,1},{6,2},{7,3},{8,12},{9,13},{10,... | collective-permute-start | bytes 1179656 | tf_op jit(solution)/shard_map/ppermute | solution.py:58
  3.6 8.3 %collective-permute-start.1 = (f32[3,16,4,512]{3,2,1,0:T(4,128)S(1)}, f32[3,16,4,512]{3,2,1,0:T(4,128)S(1)}, u32[]{:S(2)}, u32[]{:S(2)}) collective-permute-start(f32[3,16,4,512]{3,2,1,0:T(4,128)S(1)} %get-tuple-element.35), channel_id=1, source_target_pairs={{0,16},{1,17},{2,18},{3,19},{4,8},{5,9},{6,10},{7,11},{8,4},{9,5},... | collective-permute-start | bytes 1179656 | tf_op jit(solution)/shard_map/ppermute | solution.py:58
  6.2 12.2 %collective-permute-start.2 = (f32[3,4,16,512]{3,2,1,0:T(8,128)S(1)}, f32[3,4,16,512]{3,2,1,0:T(8,128)S(1)}, u32[]{:S(2)}, u32[]{:S(2)}) collective-permute-start(f32[3,4,16,512]{3,2,1,0:T(8,128)S(1)} %get-tuple-element.39), channel_id=1, source_target_pairs={{0,1},{1,0},{2,3},{3,2},{4,5},{5,4},{6,7},{7,6},{8,9},{9,8},{10,11... | collective-permute-start | bytes 1179656 | tf_op jit(solution)/shard_map/ppermute | solution.py:58
  7.7 10.6 %collective-permute-start.3 = (f32[3,4,16,512]{3,2,1,0:T(8,128)S(1)}, f32[3,4,16,512]{3,2,1,0:T(8,128)S(1)}, u32[]{:S(2)}, u32[]{:S(2)}) collective-permute-start(f32[3,4,16,512]{3,2,1,0:T(8,128)S(1)} %get-tuple-element.40), channel_id=1, source_target_pairs={{0,4},{1,2},{2,1},{3,7},{4,0},{5,6},{6,5},{7,3},{8,12},{9,10},{10,... | collective-permute-start | bytes 1179656 | tf_op jit(solution)/shard_map/ppermute | solution.py:58
  12.0 7.0 %collective-permute-start.4 = (f32[40,512]{1,0:T(8,128)S(1)}, f32[40,512]{1,0:T(8,128)S(1)}, u32[]{:S(2)}, u32[]{:S(2)}) collective-permute-start(f32[40,512]{1,0:T(8,128)S(1)} %get-tuple-element.41), channel_id=1, source_target_pairs={{0,1},{1,0},{2,3},{3,2},{4,5},{5,4},{6,7},{7,6},{8,9},{9,8},{10,11... | collective-permute-start | bytes 245768 | tf_op jit(solution)/shard_map/ppermute | solution.py:58
  14.2 4.9 %collective-permute-start.5 = (f32[40,512]{1,0:T(8,128)S(1)}, f32[40,512]{1,0:T(8,128)S(1)}, u32[]{:S(2)}, u32[]{:S(2)}) collective-permute-start(f32[40,512]{1,0:T(8,128)S(1)} %get-tuple-element.42), channel_id=1, source_target_pairs={{0,4},{1,2},{2,1},{3,7},{4,0},{5,6},{6,5},{7,3},{8,12},{9,10},{10,... | collective-permute-start | bytes 245768 | tf_op jit(solution)/shard_map/ppermute | solution.py:58
  34.8 4.8 %copy-start.1 = (f32[16]{0:T(128)S(1)}, f32[16]{0:T(128)}, u32[]{:S(2)}) copy-start(f32[16]{0:T(128)} %param.3) | copy-start | bytes 196
  40.2 2.0 %collective-permute-start.6 = (f32[65,4,512]{2,1,0:T(4,128)S(1)}, f32[65,4,512]{2,1,0:T(4,128)S(1)}, u32[]{:S(2)}, u32[]{:S(2)}) collective-permute-start(f32[65,4,512]{2,1,0:T(4,128)S(1)} %get-tuple-element.50), channel_id=1, source_target_pairs={{0,4},{1,5},{2,6},{3,7},{4,0},{5,1},{6,2},{7,3},{8,12},{9,13},{10,... | collective-permute-start | bytes 1597448 | tf_op jit(solution)/shard_map/ppermute | solution.py:58
  40.4 13.4 %collective-permute-start.7 = (f32[49,4,512]{2,1,0:T(4,128)S(1)}, f32[49,4,512]{2,1,0:T(4,128)S(1)}, u32[]{:S(2)}, u32[]{:S(2)}) collective-permute-start(f32[49,4,512]{2,1,0:T(4,128)S(1)} %get-tuple-element.51), channel_id=1, source_target_pairs={{0,16},{1,17},{2,18},{3,19},{4,8},{5,9},{6,10},{7,11},{8,4},{9,5},... | collective-permute-start | bytes 1204232 | tf_op jit(solution)/shard_map/ppermute | solution.py:58
  40.9 20.0 %collective-permute-start.9 = (f32[10,16,512]{2,1,0:T(8,128)S(1)}, f32[10,16,512]{2,1,0:T(8,128)S(1)}, u32[]{:S(2)}, u32[]{:S(2)}) collective-permute-start(f32[10,16,512]{2,1,0:T(8,128)S(1)} %get-tuple-element.54), channel_id=1, source_target_pairs={{0,1},{1,0},{2,3},{3,2},{4,5},{5,4},{6,7},{7,6},{8,9},{9,8},{10,11... | collective-permute-start | bytes 983048 | tf_op jit(solution)/shard_map/ppermute | solution.py:58
  41.3 19.7 %collective-permute-start.10 = (f32[10,16,512]{2,1,0:T(8,128)S(1)}, f32[10,16,512]{2,1,0:T(8,128)S(1)}, u32[]{:S(2)}, u32[]{:S(2)}) collective-permute-start(f32[10,16,512]{2,1,0:T(8,128)S(1)} %get-tuple-element.55), channel_id=1, source_target_pairs={{0,4},{1,2},{2,1},{3,7},{4,0},{5,6},{6,5},{7,3},{8,12},{9,10},{10,... | collective-permute-start | bytes 983048 | tf_op jit(solution)/shard_map/ppermute | solution.py:58
  42.2 11.6 %collective-permute-start.8 = (f32[16,4,512]{2,1,0:T(4,128)S(1)}, f32[16,4,512]{2,1,0:T(4,128)S(1)}, u32[]{:S(2)}, u32[]{:S(2)}) collective-permute-start(f32[16,4,512]{2,1,0:T(4,128)S(1)} %get-tuple-element.64), channel_id=1, source_target_pairs={{0,8},{4,12},{8,0},{12,4},{1,9},{5,13},{9,1},{13,5},{2,10},{6,14},... | collective-permute-start | bytes 393224 | tf_op jit(solution)/shard_map/ppermute | solution.py:780
  54.2 6.7 %collective-permute-start.11 = (f32[2,16,512]{2,1,0:T(8,128)S(1)}, f32[2,16,512]{2,1,0:T(8,128)S(1)}, u32[]{:S(2)}, u32[]{:S(2)}) collective-permute-start(f32[2,16,512]{2,1,0:T(8,128)S(1)} %get-tuple-element.56), channel_id=1, source_target_pairs={{0,1},{1,0},{2,3},{3,2},{4,5},{5,4},{6,7},{7,6},{8,9},{9,8},{10,11... | collective-permute-start | bytes 196616 | tf_op jit(solution)/shard_map/ppermute | solution.py:58
  54.7 6.3 %collective-permute-start.12 = (f32[2,16,512]{2,1,0:T(8,128)S(1)}, f32[2,16,512]{2,1,0:T(8,128)S(1)}, u32[]{:S(2)}, u32[]{:S(2)}) collective-permute-start(f32[2,16,512]{2,1,0:T(8,128)S(1)} %get-tuple-element.57), channel_id=1, source_target_pairs={{0,4},{1,2},{2,1},{3,7},{4,0},{5,6},{6,5},{7,3},{8,12},{9,10},{10,... | collective-permute-start | bytes 196616 | tf_op jit(solution)/shard_map/ppermute | solution.py:58

commit v4 on v3

--- a/solution.py
+++ b/solution.py
@@ -92,10 +92,6 @@
     return both[:rows] + both[rows:]
 
 
-def cross(a, b):
-    return (a[1] * b[2] - a[2] * b[1], a[2] * b[0] - a[0] * b[2], a[0] * b[1] - a[1] * b[0])
-
-
 def dot(a, b):
     return a[0] * b[0] + a[1] * b[1] + a[2] * b[2]
 
@@ -117,10 +113,24 @@
     )
 
 
-def descent_stages(bp, plane_of, planes, halo, cz, blocks, omega_ref):
-    def plane(x, _):
+def row_mask(rows, r, cz):
+    height = rows + (r - BASE)
+    return None if BASE <= r and r + ROWS <= BASE + cz else (height >= 0) & (height < cz)
+
+
+def masked(value, *conditions):
+    for condition in conditions:
+        if condition is not None:
+            value = jnp.where(condition, value, 0.0)
+    return value
+
+
+def descent_stages(bp, plane_of, planes, halo, cz, blocks, parts_ref, counted, functional, rows):
+    def plane(x, functional):
         at = plane_of(x)
         for r in windows(BASE - halo - 1, BASE + cz + halo + 1):
+            own = row_mask(rows, r, cz)
+
             def ld(c, j, dx=0, dz=0):
                 return bp[c, at + dx, j, r + dz : r + dz + ROWS, :]
 
@@ -131,29 +141,31 @@
                 dz = [ld(c, j, dz=1) - ld(c, j, dz=-1) for c in range(3)]
                 current = (dy[2][j] - dz[1], dz[0] - dx[2], dx[1] - dy[0][j])
                 spread = dx[0] + dy[1][j] + dz[2]
-                square = jnp.maximum(dot(field, field), 1.0)
-                inverse = 0.5 / square
-                lorentz = cross(current, field)
-                omega = [(lorentz[c] - spread * field[c]) * inverse for c in range(3)]
-                twist = cross(omega, field)
-                along = dot(omega, field)
-                for k, value in enumerate([*twist, along, *omega, *current, spread]):
-                    omega_ref[k, x, j, r : r + ROWS, :] = value
-        return 0
-
-    lax.fori_loop(0, planes, plane, 0, unroll=2)
-
-
-def doubled_force(bp, bat, omega_ref, at, r, blocks):
+                square = dot(field, field)
+                inverse = 1.0 / jnp.maximum(square, 1.0)
+                capped = jnp.minimum(square, 1.0)
+                along = dot(current, field)
+                ratio = along * inverse
+                bulk = dot(current, current)
+                spread_square = spread * spread
+                pull = (bulk + spread_square) * inverse * (1.0 - capped) + ratio * ratio
+                density = bulk * capped - ratio * along + spread_square
+                functional = functional + masked(density, own, None if counted is None else counted(x))
+                twist = [ratio * field[c] - capped * current[c] for c in range(3)]
+                local = [ratio * current[c] - pull * field[c] for c in range(3)]
+                for k, value in enumerate([*twist, capped * spread, *local]):
+                    parts_ref[k, x, j, r : r + ROWS, :] = value
+        return functional
+
+    return lax.fori_loop(0, planes, plane, functional, unroll=2)
+
+
+def forces(parts_ref, at, r, blocks):
     def ld(k, j, dx=0, dz=0):
-        return omega_ref[k, at + dx, j, r + dz : r + dz + ROWS, :]
+        return parts_ref[k, at + dx, j, r + dz : r + dz + ROWS, :]
 
     dy = {k: y_diff([ld(k, j) for j in range(blocks)]) for k in (0, 2, 3)}
     for j in range(blocks):
-        field = [bp[c, bat, j, r : r + ROWS, :] for c in range(3)]
-        omega = [ld(4 + c, j) for c in range(3)]
-        current = [ld(7 + c, j) for c in range(3)]
-        spread = ld(10, j)
 
         def dx(k):
             return ld(k, j, dx=1) - ld(k, j, dx=-1)
@@ -161,17 +173,11 @@
         def dz(k):
             return ld(k, j, dz=1) - ld(k, j, dz=-1)
 
-        curled = (dy[2][j] - dz(1) - dx(3), dz(0) - dx(2) - dy[3][j], dx(1) - dy[0][j] - dz(3))
-        bent = cross(omega, current)
-        size = dot(omega, omega)
-        twice = size + size
-        force = [curled[c] - bent[c] + omega[c] * spread + twice * field[c] for c in range(3)]
-        yield j, force, field, size, spread
-
-
-def density_of(field, size, spread):
-    square = dot(field, field)
-    return size * jnp.maximum(square, 1.0) + 0.25 * (spread * spread) * jnp.maximum(1.0 - square, 0.0)
+        yield j, [
+            (dy[2][j] - dz(1)) + (dx(3) + ld(4, j)),
+            (dz(0) - dx(2)) + (dy[3][j] + ld(5, j)),
+            (dx(1) - dy[0][j]) + (dz(3) + ld(6, j)),
+        ]
 
 
 def store_sums(sums_ref, functional, slope, rows):
@@ -182,13 +188,13 @@
         sums_ref[k] = tile
 
 
-def half_rate(sums_ref, cells):
+def rate_of(sums_ref, cells):
     total = sums_ref[0]
     for k in range(1, sums_ref.shape[0]):
         total = total + sums_ref[k]
-    functional = jnp.sum(total[0:1], axis=1, keepdims=True) / cells
-    slope = jnp.sum(total[1:2], axis=1, keepdims=True) * 0.25 / cells
-    return (0.5 * step_scale) * functional / (slope + 1e-6)
+    functional = jnp.sum(total[0:1], axis=1, keepdims=True) * 0.25 / cells
+    slope = jnp.sum(total[1:2], axis=1, keepdims=True) * 0.0625 / cells
+    return (0.25 * step_scale) * functional / (slope + 1e-6)
 
 
 def entry_kernel(magnetic, core, face_xa, face_xb, face_za, face_zb):
@@ -206,27 +212,33 @@
         face_zb[c] = jnp.where(even_z, low, high)
 
 
-def first_forces(bp, plane_of, omega_ref, omega_of, fp, planes, x_of, cx, cz, blocks, rows, sums):
+def first_forces(parts_ref, parts_of, fp, planes, x_of, cx, cz, blocks, rows, slope):
     halo = HALO - 2
     x_first, x_all, z_first, z_all = own_place(cx, cz)
 
-    def plane(x, sums):
-        functional, slope = sums
-        own = x_of(x)
-        own_x = (own >= 0) & (own < cx)
-        inside_x = (own + x_first >= 0) & (own + x_first < x_all)
+    def plane(x, slope):
+        own_x = inside_x = None
+        if x_of is not None:
+            own = x_of(x)
+            own_x = (own >= 0) & (own < cx)
+            inside_x = (own + x_first >= 0) & (own + x_first < x_all)
         for r in windows(BASE - halo, BASE + cz + halo):
-            height = rows + (r - BASE)
-            owned = (height >= 0) & (height < cz) & own_x
-            inside = (height + z_first >= 0) & (height + z_first < z_all) & inside_x
-            for j, force, field, size, spread in doubled_force(bp, plane_of(x), omega_ref, omega_of(x), r, blocks):
-                functional = functional + jnp.where(owned, density_of(field, size, spread), 0.0)
-                slope = slope + jnp.where(owned, dot(force, force), 0.0)
+            own_z = row_mask(rows, r, cz)
+            height = rows + (r - BASE) + z_first
+            inside_z = None if own_z is None else (height >= 0) & (height < z_all)
+            for j, force in forces(parts_ref, parts_of(x), r, blocks):
+                slope = slope + masked(dot(force, force), own_z, own_x)
                 for c in range(3):
-                    fp[c, x, j, r : r + ROWS, :] = jnp.where(inside, force[c], 0.0)
-        return functional, slope
-
-    return lax.fori_loop(0, planes, plane, sums, unroll=4)
+                    fp[c, x, j, r : r + ROWS, :] = masked(force[c], inside_z, inside_x)
+        return slope
+
+    return lax.fori_loop(0, planes, plane, slope, unroll=4)
+
+
+def z_halos(bp, c, plane, j, top, a, b):
+    low, high = sorted_out("gz", a, b)
+    bp[c, plane, j, BASE - HALO : BASE, :] = low
+    bp[c, plane, j, top : top + HALO, :] = high
 
 
 def corner_row(d):
@@ -265,7 +277,7 @@
     bp[c, plane, j, top : top + HALO, :] = high
 
 
-def inner_kernel(core, face_za, face_zb, bp, fp, sums_ref, omega_ref):
+def inner_kernel(core, face_za, face_zb, bp, fp, sums_ref, parts_ref):
     _, cx, cz, ny = core.shape
     blocks = ny // LANES
     halo = HALO - 2
@@ -280,25 +292,13 @@
         return 0
 
     lax.fori_loop(0, cx, own, 0)
-    descent_stages(bp, lambda x: x + 1, cx - 2, halo, cz, blocks, omega_ref)
+    rows = row_index()
     zero = jnp.zeros((ROWS, LANES), jnp.float32)
-    sums_ref[0], sums_ref[1] = first_forces(
-        bp,
-        lambda x: x + 2,
-        omega_ref,
-        lambda x: x + 1,
-        fp,
-        cx - 4,
-        lambda x: x + 2,
-        cx,
-        cz,
-        blocks,
-        row_index(),
-        (zero, zero),
-    )
-
-
-def outer_kernel(own, part, face_xa, face_xb, corner_a, corner_b, bp, fp, sums_ref, omega_ref):
+    sums_ref[0] = descent_stages(bp, lambda x: x + 1, cx - 2, halo, cz, blocks, parts_ref, None, zero, rows)
+    sums_ref[1] = first_forces(parts_ref, lambda x: x + 1, fp, cx - 4, None, cx, cz, blocks, rows, zero)
+
+
+def outer_kernel(own, part, face_xa, face_xb, corner_a, corner_b, bp, fp, sums_ref, parts_ref):
     _, cx, blocks, _, _ = own.shape
     cz = face_xa.shape[2]
     halo = HALO - 2
@@ -327,11 +327,20 @@
                     high, low = corner_rows(corners[side], 2 * c * corner_row(HALO), d)
                     bp[c, plane, j, BASE - HALO : BASE, :] = low
                     bp[c, plane, j, top : top + HALO, :] = high
-    descent_stages(bp, lambda x: x + 1 + jnp.where(x >= 6, 2, 0), 12, halo, cz, blocks, omega_ref)
-    functional, slope = first_forces(
+    functional = descent_stages(
         bp,
-        lambda x: x + 2 + jnp.where(x >= 4, 4, 0),
-        omega_ref,
+        lambda x: x + 1 + jnp.where(x >= 6, 2, 0),
+        12,
+        halo,
+        cz,
+        blocks,
+        parts_ref,
+        lambda x: (x == 3) | (x == 8),
+        part[0],
+        rows,
+    )
+    slope = first_forces(
+        parts_ref,
         lambda x: x + 1 + jnp.where(x >= 4, 2, 0),
         fp,
         8,
@@ -340,19 +349,19 @@
         cz,
         blocks,
         rows,
-        (part[0], part[1]),
+        part[1],
     )
     store_sums(sums_ref, functional, slope, rows)
 
 
 def second_kernel(
-    cells, own_b, inner_f, outer_b, outer_f, sums0, core_b, core_f, bp, sums_ref, omega_ref
+    cells, own_b, inner_f, outer_b, outer_f, sums0, core_b, core_f, bp, sums_ref, parts_ref
 ):
     _, cx, cz, ny = core_b.shape
     blocks = ny // LANES
     rows = row_index()
     even_x, even_z = is_even("gx"), is_even("gz")
-    rate = half_rate(sums0, cells)
+    rate = rate_of(sums0, cells)
     halo = HALO - 2
 
     def step(x, field, at, force, there):
@@ -373,23 +382,32 @@
         step(k + 2, own_b, k, outer_f, k + 2)
         step(k + cx, own_b, k + cx - 2, outer_f, k + 4)
         step(k + cx + 2, outer_b, k + 12, outer_f, k + 6)
-    descent_stages(bp, lambda x: x + 1, cx + 2, 0, cz, blocks, omega_ref)
-
-    def plane(x, sums):
-        functional, slope = sums
+    zero = jnp.zeros((ROWS, LANES), jnp.float32)
+    functional = descent_stages(
+        bp,
+        lambda x: x + 1,
+        cx + 2,
+        0,
+        cz,
+        blocks,
+        parts_ref,
+        lambda x: (x >= 1) & (x <= cx),
+        zero,
+        rows,
+    )
+
+    def plane(x, slope):
         for z in range(0, cz, ROWS):
             r = BASE + z
-            for j, force, field, size, spread in doubled_force(bp, x + halo, omega_ref, x + 1, r, blocks):
+            for j, force in forces(parts_ref, x + 1, r, blocks):
                 cut = slice(j * LANES, (j + 1) * LANES)
-                functional = functional + density_of(field, size, spread)
                 slope = slope + dot(force, force)
                 for c in range(3):
-                    core_b[c, x, z : z + ROWS, cut] = field[c]
+                    core_b[c, x, z : z + ROWS, cut] = bp[c, x + halo, j, r : r + ROWS, :]
                     core_f[c, x, z : z + ROWS, cut] = force[c]
-        return functional, slope
-
-    zero = jnp.zeros((ROWS, LANES), jnp.float32)
-    functional, slope = lax.fori_loop(0, cx, plane, (zero, zero), unroll=4)
+        return slope
+
+    slope = lax.fori_loop(0, cx, plane, zero, unroll=4)
     store_sums(sums_ref, functional, slope, rows)
 
 
@@ -477,11 +495,13 @@
 
     def plane(x, _):
         at, out = at_of(x), out_of(x)
-        there = x_first + own_of(x)
-        inside_x = (there >= 0) & (there < x_all)
+        inside_x = None
+        if own_of is not None:
+            there = x_first + own_of(x)
+            inside_x = (there >= 0) & (there < x_all)
         for r in windows(BASE - halo, BASE + cz + halo):
             height = rows + (r - BASE) + z_first
-            inside = (height >= 0) & (height < z_all) & inside_x
+            inside_z = None if row_mask(rows, r, cz) is None else (height >= 0) & (height < z_all)
 
             def ld(c, j, dx=0, dz=0):
                 return a_ref[c, at + dx, j, r + dz : r + dz + ROWS, :]
@@ -495,7 +515,7 @@
                     curl_x = curl_x + dy[2][j]
                     curl_y = curl_y - (ld(2, j, dx=1) - ld(2, j, dx=-1))
                 for c, value in enumerate((curl_x, curl_y, curl_z)):
-                    bm[c, out, j, r : r + ROWS, :] = jnp.where(inside, value, 0.0)
+                    bm[c, out, j, r : r + ROWS, :] = masked(value, inside_z, inside_x)
         return 0
 
     lax.fori_loop(0, planes, plane, 0, unroll=4)
@@ -546,13 +566,13 @@
 
 
 def middle_kernel(
-    cells, core_b, core_f, bp, sums0, friction, face_za, face_zb, above, relaxed, ap, bm, an, bn, inner, rub
+    cells, core_b, core_f, bp, sums0, friction, face_za, face_zb, above, out, ap, bm, an, bn, inner, rub, relaxed, sent
 ):
     _, cx, cz, ny = core_b.shape
     blocks = ny // LANES
     rows = row_index()
     _, _, z_first, z_all = own_place(cx, cz)
-    rate = half_rate(sums0, cells)
+    rate = rate_of(sums0, cells)
     top = BASE + cz
 
     rub[BASE:top] = friction[...]
@@ -583,20 +603,25 @@
     lax.fori_loop(0, cx, own_plane, 0, unroll=2)
     matrix = dealing(ny, True)
     relaxed[...] = dealt(relaxed[...].reshape(3 * cx * cz, ny), matrix).reshape(relaxed.shape)
-    induced(ap, bm, cx - 2, HALO - 1, lambda x: x + 1, lambda x: x, lambda x: x + 1, True, cx, cz, blocks, rows)
+    copy = pltpu.make_async_copy(relaxed, out, sent)
+    copy.start()
+    induced(ap, bm, cx - 2, HALO - 1, lambda x: x + 1, lambda x: x, None, True, cx, cz, blocks, rows)
     first_push(ap, bm, an, rub, cx - 4, lambda x: x + 1, lambda x: x, cz, blocks)
-    induced(an, bn, cx - 6, 1, lambda x: x + 1, lambda x: x, lambda x: x + 3, False, cx, cz, blocks, rows)
+    induced(an, bn, cx - 6, 1, lambda x: x + 1, lambda x: x, None, False, cx, cz, blocks, rows)
     last_push(an, bn, inner, rub, cx - 8, lambda x: x + 1, cz, blocks)
     inner[...] = dealt(inner[...].reshape(-1, ny), matrix).reshape(inner.shape)
+    copy.wait()
 
 
 def ends_kernel(
-    cells, bp, sums0, face_xa, face_xb, corner_a, corner_b, own_ap, own_bm, own_an, own_bn, inner, rub, potential, ap, bm, an, rim
+    cells, bp, sums0, face_xa, face_xb, corner_a, corner_b, own_ap, own_bm, own_an, own_bn, inner, rub, potential, ap, bm, an, rim, sent
 ):
     _, cx, cz, ny = potential.shape
     blocks = ny // LANES
     rows = row_index()
-    rate = half_rate(sums0, cells)
+    copies = [pltpu.make_async_copy(inner, potential.at[:, HALO : cx - HALO], sent.at[0])]
+    copies[0].start()
+    rate = rate_of(sums0, cells)
 
     for d in range(1, HALO + 1):
         for c in range(2):
@@ -644,10 +669,13 @@
     induced(an, bm, 8, 1, at_of, out_of, lambda x: x - 1 + jnp.where(x >= 4, cx - 6, 0), False, cx, cz, blocks, rows)
     borrow(bm, own_bn, 0, cx - 8)
     last_push(an, bm, rim, rub, 8, at_of, cz, blocks)
-    ends = dealt(rim[...].reshape(-1, ny), dealing(ny, True)).reshape(rim.shape)
-    potential[:, :HALO] = ends[:, :HALO]
-    potential[:, cx - HALO :] = ends[:, HALO:]
-    potential[:, HALO : cx - HALO] = inner[...]
+    rim[...] = dealt(rim[...].reshape(-1, ny), dealing(ny, True)).reshape(rim.shape)
+    copies.append(pltpu.make_async_copy(rim.at[:, :HALO], potential.at[:, :HALO], sent.at[1]))
+    copies.append(pltpu.make_async_copy(rim.at[:, HALO:], potential.at[:, cx - HALO :], sent.at[2]))
+    for copy in copies[1:]:
+        copy.start()
+    for copy in copies:
+        copy.wait()
 
 
 def pack_kernel(cells, count, *refs):
@@ -656,7 +684,7 @@
     cz = bp.shape[3] - 2 * BASE
     even_x = is_even("gx")
     place = lax.axis_index("gz")
-    rate = half_rate(sums0, cells)
+    rate = rate_of(sums0, cells)
 
     def total(x, _):
         column = jnp.zeros(columns[0].shape[1:], jnp.float32)
@@ -680,15 +708,13 @@
             corner_b[c, :, cut] = jnp.where(even_x, packed[0], packed[1])
 
 
-def call(kernel, outs, *args, scratch=(), cost=0, limit=8, outside=0):
+def call(kernel, outs, *args, scratch=(), cost=0, limit=8, outside_out=0):
     shapes = [jax.ShapeDtypeStruct(shape, jnp.float32) for shape in outs]
     return pl.pallas_call(
         kernel,
         out_shape=shapes,
-        in_specs=[
-            pl.BlockSpec(memory_space=pltpu.HBM if k < outside else pltpu.VMEM) for k in range(len(args))
-        ],
-        out_specs=[pl.BlockSpec(memory_space=pltpu.VMEM)] * len(outs),
+        in_specs=[pl.BlockSpec(memory_space=pltpu.VMEM)] * len(args),
+        out_specs=[pl.BlockSpec(memory_space=pl.ANY if k < outside_out else pltpu.VMEM) for k in range(len(outs))],
         scratch_shapes=[pltpu.VMEM(item, jnp.float32) if isinstance(item, tuple) else item for item in scratch],
         compiler_params=pltpu.CompilerParams(vmem_limit_bytes=limit * 1024 * 1024),
         cost_estimate=pl.CostEstimate(flops=cost, bytes_accessed=cost // 10, transcendentals=0),
@@ -735,9 +761,9 @@
         [padded(3, 0), padded(3, -2), (2, ROWS, LANES)],
         magnetic,
         *faces_z,
-        scratch=[padded(11, -1)],
+        scratch=[padded(7, -1)],
         cost=work,
-        limit=13,
+        limit=9,
     )
     outer_b, outer_f, sums = call(
         outer_kernel,
@@ -746,9 +772,9 @@
         part,
         *faces_x,
         *corners,
-        scratch=[planes_of(11, 12)],
+        scratch=[planes_of(7, 12)],
         cost=work,
-        limit=12,
+        limit=9,
     )
     core_b, core_f, bp, sums = call(
         functools.partial(second_kernel, cells),
@@ -758,9 +784,9 @@
         outer_b,
         outer_f,
         shared(sums),
-        scratch=[padded(11, 1)],
+        scratch=[padded(7, 1)],
         cost=work,
-        limit=15,
+        limit=11,
     )
     faces = call(
         faces_kernel,
@@ -801,6 +827,8 @@
         rubbed,
         *faces_z,
         above,
+        scratch=[core, pltpu.SemaphoreType.DMA],
+        outside_out=1,
         cost=work,
         limit=8,
     )
@@ -812,7 +840,8 @@
         *faces_x,
         *corners,
         *shares,
-        scratch=[planes_of(2, 12), planes_of(3, 12), planes_of(3, 12), (3, 2 * HALO, cz, ny)],
+        scratch=[planes_of(2, 12), planes_of(3, 12), planes_of(3, 12), (3, 2 * HALO, cz, ny), pltpu.SemaphoreType.DMA((3,))],
+        outside_out=1,
         cost=work,
         limit=14,
     )

time: 65.4 us -> 63.3 us (0.968)
  Pallas kernels: 24.5 us -> 21.3 us
  waiting for transfers between devices: 5.77 us -> 6.83 us
    pallas_call x9, Pallas kernels: 24.5 us -> 21.3 us  [call(): pl.pallas_call(kernel, out_shape=shapes, in_specs=[pl.BlockSpec(memory_sp...]
    ppermute x6, waiting for transfers between devices: 1.58 us -> 2.64 us  [swapped(): lax.ppermute(pair[0], AXES, first)]
  transfers between devices with their start and end apart: 13 -> 13, of which waited for: 3 -> 4; matrix products, arithmetic and copies ran while one was open for 0% -> 0% of each run, Pallas kernels for 17% -> 15%
where the time goes in v4:
time: 63.3 us; the launch traced here: 63 us
  blocking collectives  23.5 us (37%)
  Pallas kernels  21.3 us (34%)
  starting transfers between devices  9.16 us (14%)
  waiting for transfers between devices  6.83 us (11%)
  local copies, waits for them, and re-layouts  1.48 us (2%)
  between operations  0.75 us (1%)
    all_to_all x2, blocking collectives, shared(): return lax.all_to_all(tile_copies, ('gz', 'gx'), 0, 0)  23.5 us
    pallas_call x9, Pallas kernels, call(): pl.pallas_call(kernel, out_shape=shapes, in_specs=[pl.BlockSpec(memory_sp...  21.3 us
    ppermute x6, starting transfers between devices, swapped(): lax.ppermute(pair[0], AXES, first)  5.17 us
    ppermute x6, waiting for transfers between devices, swapped(): lax.ppermute(pair[1], AXES, second)  4.19 us
    ppermute x6, starting transfers between devices, swapped(): lax.ppermute(pair[1], AXES, second)  3.19 us
    ppermute x6, waiting for transfers between devices, swapped(): lax.ppermute(pair[0], AXES, first)  2.64 us
    unnamed x4, local copies, waits for them, and re-layouts  1.4 us
  transfers between devices with their start and end apart: 13, of which 4 were waited for; matrix products, arithmetic and copies ran while one was open for 0% of the time, Pallas kernels for 15%

profile of v4, /device:TPU:0, one launch (start us, length us, event | category | flops | bytes accessed | tf_op | source)
XLA Modules:
  0.0 63.0 jit_solution(16777624647090021271)
XLA Ops:
  0.6 0.0 copy-start
  0.6 1.4 %copy-done = f32[3,16,16,512]{3,2,1,0:T(8,128)S(1)} copy-done((f32[3,16,16,512]{3,2,1,0:T(8,128)S(1)}, f32[3,16,16,512]{3,2,1,0:T(8,128)}, u32[]{:S(2)}) %copy-start) | copy-done | bytes 1572888
  2.0 1.0 %shard_map.41 = (f32[3,16,16,512]{3,2,1,0:T(8,128)S(1)}, f32[3,4,16,512]{3,2,1,0:T(8,128)S(1)}, f32[3,4,16,512]{3,2,1,0:T(8,128)S(1)}, f32[3,16,4,512]{3,2,1,0:T(4,128)S(1)}, f32[3,16,4,512]{3,2,1,0:T(4,128)S(1)}) custom-call(f32[3,16,16,512]{3,2,1,0:T(8,128)S(1)} %copy-done), custom_call_target="tpu_custom_call" | custom-call | flops 26214400 | bytes 2621440 | tf_op jit(solution)/shard_map/pallas_call | solution.py:713
  3.1 0.5 collective-permute-start
  3.6 2.6 %collective-permute-start.1 = (f32[3,16,4,512]{3,2,1,0:T(4,128)S(1)}, f32[3,16,4,512]{3,2,1,0:T(4,128)S(1)}, u32[]{:S(2)}, u32[]{:S(2)}) collective-permute-start(f32[3,16,4,512]{3,2,1,0:T(4,128)S(1)} %get-tuple-element.35), channel_id=1, source_target_pairs={{0,16},{1,17},{2,18},{3,19},{4,8},{5,9},{6,10},{7,11},{8,4},{9,5},... | collective-permute-start | bytes 1179656 | tf_op jit(solution)/shard_map/ppermute | solution.py:58
  6.2 1.6 %collective-permute-start.2 = (f32[3,4,16,512]{3,2,1,0:T(8,128)S(1)}, f32[3,4,16,512]{3,2,1,0:T(8,128)S(1)}, u32[]{:S(2)}, u32[]{:S(2)}) collective-permute-start(f32[3,4,16,512]{3,2,1,0:T(8,128)S(1)} %get-tuple-element.39), channel_id=1, source_target_pairs={{0,1},{1,0},{2,3},{3,2},{4,5},{5,4},{6,7},{7,6},{8,9},{9,8},{10,11... | collective-permute-start | bytes 1179656 | tf_op jit(solution)/shard_map/ppermute | solution.py:58
  7.7 0.0 collective-permute-start.3
  7.7 0.0 collective-permute-done.face_za
  7.7 4.2 %collective-permute-done.1.face_zb = f32[3,16,4,512]{3,2,1,0:T(4,128)S(1)} collective-permute-done((f32[3,16,4,512]{3,2,1,0:T(4,128)S(1)}, f32[3,16,4,512]{3,2,1,0:T(4,128)S(1)}, u32[]{:S(2)}, u32[]{:S(2)}) %collective-permute-start.1) | collective-permute-done | bytes 393248 | tf_op jit(solution)/shard_map/ppermute | solution.py:58
  11.9 0.1 shard_map.43
  12.0 2.1 %collective-permute-start.4 = (f32[40,512]{1,0:T(8,128)S(1)}, f32[40,512]{1,0:T(8,128)S(1)}, u32[]{:S(2)}, u32[]{:S(2)}) collective-permute-start(f32[40,512]{1,0:T(8,128)S(1)} %get-tuple-element.41), channel_id=1, source_target_pairs={{0,1},{1,0},{2,3},{3,2},{4,5},{5,4},{6,7},{7,6},{8,9},{9,8},{10,11... | collective-permute-start | bytes 245768 | tf_op jit(solution)/shard_map/ppermute | solution.py:58
  14.2 0.0 collective-permute-start.5
  14.2 3.1 %shard_map.42 = (f32[3,16,4,32,128]{4,3,2,1,0:T(8,128)S(1)}, f32[3,12,4,32,128]{4,3,2,1,0:T(8,128)S(1)}, f32[2,8,128]{2,1,0:T(8,128)S(1)}) custom-call(f32[3,16,16,512]{3,2,1,0:T(8,128)S(1)} %get-tuple-element.33.core, f32[3,16,4,512]{3,2,1,0:T(4,128)S(1)} %collective-permute-done.face_za, f32[3,16,4,512]{3,2,1,0:T(4,128)S(1)} %collective-permute-done.1.face_zb), custom_call_target="tpu_custom_call" | custom-call | flops 26214400 | bytes 2621440 | tf_op jit(solution)/shard_map/pallas_call | solution.py:713
  17.3 0.9 %collective-permute-done.2.face_xa = f32[3,4,16,512]{3,2,1,0:T(8,128)S(1)} collective-permute-done((f32[3,4,16,512]{3,2,1,0:T(8,128)S(1)}, f32[3,4,16,512]{3,2,1,0:T(8,128)S(1)}, u32[]{:S(2)}, u32[]{:S(2)}) %collective-permute-start.2) | collective-permute-done | bytes 393248 | tf_op jit(solution)/shard_map/ppermute | solution.py:58
  18.1 0.0 collective-permute-done.3.face_xb
  18.1 0.9 %collective-permute-done.4.corner_a = f32[40,512]{1,0:T(8,128)S(1)} collective-permute-done((f32[40,512]{1,0:T(8,128)S(1)}, f32[40,512]{1,0:T(8,128)S(1)}, u32[]{:S(2)}, u32[]{:S(2)}) %collective-permute-start.4) | collective-permute-done | bytes 81952 | tf_op jit(solution)/shard_map/ppermute | solution.py:58
  19.0 0.0 collective-permute-done.5.corner_b
  19.0 2.4 %shard_map.44 = (f32[3,16,4,32,128]{4,3,2,1,0:T(8,128)S(1)}, f32[3,8,4,32,128]{4,3,2,1,0:T(8,128)S(1)}, f32[16,8,128]{2,1,0:T(8,128)S(1)}) custom-call(f32[3,16,4,32,128]{4,3,2,1,0:T(8,128)S(1)} %get-tuple-element.36.own.own_b, f32[2,8,128]{2,1,0:T(8,128)S(1)} %get-tuple-element.38.part, f32[3,4,16,512]{3,2,1,0:T(8,128)S(1)} %collective-permute-done.2.face_xa, ...), custom_call_target="tpu_custom_call" | custom-call | flops 26214400 | bytes 2621440 | tf_op jit(solution)/shard_map/pallas_call | solution.py:713
  21.5 12.7 %all_to_all.10.sums0 = f32[16,8,128]{2,1,0:T(8,128)S(1)} all-to-all(f32[16,8,128]{2,1,0:T(8,128)S(1)} %get-tuple-element.45), channel_id=1, replica_groups=mesh['runs'=2,'gz'=4,'gx'=4] {'gz','gx'}, dimensions={0} | all-to-all | bytes 131072 | tf_op jit(solution)/shard_map/all_to_all | solution.py:70
  34.2 0.0 copy-start.1
  34.2 4.0 %shard_map.45 = (f32[3,16,16,512]{3,2,1,0:T(8,128)S(1)}, f32[3,16,16,512]{3,2,1,0:T(8,128)S(1)}, f32[3,20,4,32,128]{4,3,2,1,0:T(8,128)S(1)}, f32[16,8,128]{2,1,0:T(8,128)S(1)}) custom-call(f32[3,16,4,32,128]{4,3,2,1,0:T(8,128)S(1)} %get-tuple-element.36.own.own_b, f32[3,12,4,32,128]{4,3,2,1,0:T(8,128)S(1)} %get-tuple-element.37.inner_f, ...), custom_call_target="tpu_custom_call" | custom-call | flops 26214400 | bytes 2621440 | tf_op jit(solution)/shard_map/pallas_call | solution.py:713
  38.2 0.0 copy-done.1
  38.2 0.1 broadcast_in_dim.2.friction
  38.3 0.5 shard_map.46
  38.8 0.2 collective-permute-start.6
  39.0 0.5 collective-permute-start.7
  39.5 0.3 collective-permute-start.9
  39.9 0.1 collective-permute-start.10
  39.9 0.9 %collective-permute-done.6.refs_2_.face_za = f32[65,4,512]{2,1,0:T(4,128)S(1)} collective-permute-done((f32[65,4,512]{2,1,0:T(4,128)S(1)}, f32[65,4,512]{2,1,0:T(4,128)S(1)}, u32[]{:S(2)}, u32[]{:S(2)}) %collective-permute-start.6) | collective-permute-done | bytes 532512 | tf_op jit(solution)/shard_map/ppermute | solution.py:58
  40.9 0.8 %collective-permute-start.8 = (f32[16,4,512]{2,1,0:T(4,128)S(1)}, f32[16,4,512]{2,1,0:T(4,128)S(1)}, u32[]{:S(2)}, u32[]{:S(2)}) collective-permute-start(f32[16,4,512]{2,1,0:T(4,128)S(1)} %get-tuple-element.64), channel_id=1, source_target_pairs={{0,8},{4,12},{8,0},{12,4},{1,9},{5,13},{9,1},{13,5},{2,10},{6,14},... | collective-permute-start | bytes 393224 | tf_op jit(solution)/shard_map/ppermute | solution.py:806
  41.7 10.8 %all_to_all.11.refs_5_.sums0 = f32[16,8,128]{2,1,0:T(8,128)S(1)} all-to-all(f32[16,8,128]{2,1,0:T(8,128)S(1)} %get-tuple-element.49), channel_id=1, replica_groups=mesh['runs'=2,'gz'=4,'gx'=4] {'gz','gx'}, dimensions={0} | all-to-all | bytes 131072 | tf_op jit(solution)/shard_map/all_to_all | solution.py:70
  52.4 0.0 collective-permute-done.7.refs_3_.face_zb
  52.4 0.0 collective-permute-done.8.refs_1_
  52.4 0.4 shard_map.47
  52.9 0.4 collective-permute-start.11
  53.3 0.0 collective-permute-start.12
  53.3 5.8 %shard_map.48 = (f32[3,16,16,512]{3,2,1,0:T(8,128)}, f32[2,16,4,32,128]{4,3,2,1,0:T(8,128)S(1)}, f32[3,14,4,32,128]{4,3,2,1,0:T(8,128)S(1)}, f32[3,12,4,32,128]{...) custom-call(f32[3,16,16,512]{3,2,1,0:T(8,128)S(1)} %get-tuple-elemen, ...), custom_call_target="tpu_custom_call" | custom-call | flops 26214400 | bytes 2621440 | tf_op jit(solution)/shard_map/pallas_call | solution.py:713
  59.1 0.0 collective-permute-done.9.face_xa
  59.1 0.0 collective-permute-done.10.face_xb
  59.1 0.0 collective-permute-done.11.corner_a
  59.1 0.0 collective-permute-done.12.corner_b
  59.1 3.9 %shard_map.49 = f32[3,16,16,512]{3,2,1,0:T(8,128)} custom-call(f32[3,20,4,32,128]{4,3,2,1,0:T(8,128)S(1)} %get-tuple-element.48.refs_4_.bp, f32[16,8,128]{2,1,0:T(8,128)S(1)} %all_to_all.11.refs_5_.sums0, f32[10,16,512]{2,1,0:T(8,128)S(1)} %collective-permute-done.9.face_xa, f32[10,16,512]{2,1,0:T(8,128)S(1)} %collective-permute-done.10.face_xb, ...), custom_call_target="tpu_custom_call" | custom-call | flops 26214400 | bytes 2621440 | tf_op jit(solution)/shard_map/pallas_call | solution.py:713
  (1 shorter events, 0.0 us)
Async XLA Ops:
  0.6 1.4 %copy-start = (f32[3,16,16,512]{3,2,1,0:T(8,128)S(1)}, f32[3,16,16,512]{3,2,1,0:T(8,128)}, u32[]{:S(2)}) copy-start(f32[3,16,16,512]{3,2,1,0:T(8,128)} %magnetic.1) | copy-start | bytes 4718596
  3.1 4.7 %collective-permute-start = (f32[3,16,4,512]{3,2,1,0:T(4,128)S(1)}, f32[3,16,4,512]{3,2,1,0:T(4,128)S(1)}, u32[]{:S(2)}, u32[]{:S(2)}) collective-permute-start(f32[3,16,4,512]{3,2,1,0:T(4,128)S(1)} %get-tuple-element.34), channel_id=1, source_target_pairs={{0,4},{1,5},{2,6},{3,7},{4,0},{5,1},{6,2},{7,3},{8,12},{9,13},{10,... | collective-permute-start | bytes 1179656 | tf_op jit(solution)/shard_map/ppermute | solution.py:58
  3.6 8.3 %collective-permute-start.1 = (f32[3,16,4,512]{3,2,1,0:T(4,128)S(1)}, f32[3,16,4,512]{3,2,1,0:T(4,128)S(1)}, u32[]{:S(2)}, u32[]{:S(2)}) collective-permute-start(f32[3,16,4,512]{3,2,1,0:T(4,128)S(1)} %get-tuple-element.35), channel_id=1, source_target_pairs={{0,16},{1,17},{2,18},{3,19},{4,8},{5,9},{6,10},{7,11},{8,4},{9,5},... | collective-permute-start | bytes 1179656 | tf_op jit(solution)/shard_map/ppermute | solution.py:58
  6.2 12.0 %collective-permute-start.2 = (f32[3,4,16,512]{3,2,1,0:T(8,128)S(1)}, f32[3,4,16,512]{3,2,1,0:T(8,128)S(1)}, u32[]{:S(2)}, u32[]{:S(2)}) collective-permute-start(f32[3,4,16,512]{3,2,1,0:T(8,128)S(1)} %get-tuple-element.39), channel_id=1, source_target_pairs={{0,1},{1,0},{2,3},{3,2},{4,5},{5,4},{6,7},{7,6},{8,9},{9,8},{10,11... | collective-permute-start | bytes 1179656 | tf_op jit(solution)/shard_map/ppermute | solution.py:58
  7.7 10.4 %collective-permute-start.3 = (f32[3,4,16,512]{3,2,1,0:T(8,128)S(1)}, f32[3,4,16,512]{3,2,1,0:T(8,128)S(1)}, u32[]{:S(2)}, u32[]{:S(2)}) collective-permute-start(f32[3,4,16,512]{3,2,1,0:T(8,128)S(1)} %get-tuple-element.40), channel_id=1, source_target_pairs={{0,4},{1,2},{2,1},{3,7},{4,0},{5,6},{6,5},{7,3},{8,12},{9,10},{10,... | collective-permute-start | bytes 1179656 | tf_op jit(solution)/shard_map/ppermute | solution.py:58
  12.0 7.0 %collective-permute-start.4 = (f32[40,512]{1,0:T(8,128)S(1)}, f32[40,512]{1,0:T(8,128)S(1)}, u32[]{:S(2)}, u32[]{:S(2)}) collective-permute-start(f32[40,512]{1,0:T(8,128)S(1)} %get-tuple-element.41), channel_id=1, source_target_pairs={{0,1},{1,0},{2,3},{3,2},{4,5},{5,4},{6,7},{7,6},{8,9},{9,8},{10,11... | collective-permute-start | bytes 245768 | tf_op jit(solution)/shard_map/ppermute | solution.py:58
  14.2 4.9 %collective-permute-start.5 = (f32[40,512]{1,0:T(8,128)S(1)}, f32[40,512]{1,0:T(8,128)S(1)}, u32[]{:S(2)}, u32[]{:S(2)}) collective-permute-start(f32[40,512]{1,0:T(8,128)S(1)} %get-tuple-element.42), channel_id=1, source_target_pairs={{0,4},{1,2},{2,1},{3,7},{4,0},{5,6},{6,5},{7,3},{8,12},{9,10},{10,... | collective-permute-start | bytes 245768 | tf_op jit(solution)/shard_map/ppermute | solution.py:58
  34.2 4.1 %copy-start.1 = (f32[16]{0:T(128)S(1)}, f32[16]{0:T(128)}, u32[]{:S(2)}) copy-start(f32[16]{0:T(128)} %param.3) | copy-start | bytes 196
  38.8 2.0 %collective-permute-start.6 = (f32[65,4,512]{2,1,0:T(4,128)S(1)}, f32[65,4,512]{2,1,0:T(4,128)S(1)}, u32[]{:S(2)}, u32[]{:S(2)}) collective-permute-start(f32[65,4,512]{2,1,0:T(4,128)S(1)} %get-tuple-element.50), channel_id=1, source_target_pairs={{0,4},{1,5},{2,6},{3,7},{4,0},{5,1},{6,2},{7,3},{8,12},{9,13},{10,... | collective-permute-start | bytes 1597448 | tf_op jit(solution)/shard_map/ppermute | solution.py:58
  39.0 13.4 %collective-permute-start.7 = (f32[49,4,512]{2,1,0:T(4,128)S(1)}, f32[49,4,512]{2,1,0:T(4,128)S(1)}, u32[]{:S(2)}, u32[]{:S(2)}) collective-permute-start(f32[49,4,512]{2,1,0:T(4,128)S(1)} %get-tuple-element.51), channel_id=1, source_target_pairs={{0,16},{1,17},{2,18},{3,19},{4,8},{5,9},{6,10},{7,11},{8,4},{9,5},... | collective-permute-start | bytes 1204232 | tf_op jit(solution)/shard_map/ppermute | solution.py:58
  39.5 19.5 %collective-permute-start.9 = (f32[10,16,512]{2,1,0:T(8,128)S(1)}, f32[10,16,512]{2,1,0:T(8,128)S(1)}, u32[]{:S(2)}, u32[]{:S(2)}) collective-permute-start(f32[10,16,512]{2,1,0:T(8,128)S(1)} %get-tuple-element.54), channel_id=1, source_target_pairs={{0,1},{1,0},{2,3},{3,2},{4,5},{5,4},{6,7},{7,6},{8,9},{9,8},{10,11... | collective-permute-start | bytes 983048 | tf_op jit(solution)/shard_map/ppermute | solution.py:58
  39.9 19.2 %collective-permute-start.10 = (f32[10,16,512]{2,1,0:T(8,128)S(1)}, f32[10,16,512]{2,1,0:T(8,128)S(1)}, u32[]{:S(2)}, u32[]{:S(2)}) collective-permute-start(f32[10,16,512]{2,1,0:T(8,128)S(1)} %get-tuple-element.55), channel_id=1, source_target_pairs={{0,4},{1,2},{2,1},{3,7},{4,0},{5,6},{6,5},{7,3},{8,12},{9,10},{10,... | collective-permute-start | bytes 983048 | tf_op jit(solution)/shard_map/ppermute | solution.py:58
  40.9 11.6 %collective-permute-start.8 = (f32[16,4,512]{2,1,0:T(4,128)S(1)}, f32[16,4,512]{2,1,0:T(4,128)S(1)}, u32[]{:S(2)}, u32[]{:S(2)}) collective-permute-start(f32[16,4,512]{2,1,0:T(4,128)S(1)} %get-tuple-element.64), channel_id=1, source_target_pairs={{0,8},{4,12},{8,0},{12,4},{1,9},{5,13},{9,1},{13,5},{2,10},{6,14},... | collective-permute-start | bytes 393224 | tf_op jit(solution)/shard_map/ppermute | solution.py:806
  52.9 6.2 %collective-permute-start.11 = (f32[2,16,512]{2,1,0:T(8,128)S(1)}, f32[2,16,512]{2,1,0:T(8,128)S(1)}, u32[]{:S(2)}, u32[]{:S(2)}) collective-permute-start(f32[2,16,512]{2,1,0:T(8,128)S(1)} %get-tuple-element.56), channel_id=1, source_target_pairs={{0,1},{1,0},{2,3},{3,2},{4,5},{5,4},{6,7},{7,6},{8,9},{9,8},{10,11... | collective-permute-start | bytes 196616 | tf_op jit(solution)/shard_map/ppermute | solution.py:58
  53.3 5.8 %collective-permute-start.12 = (f32[2,16,512]{2,1,0:T(8,128)S(1)}, f32[2,16,512]{2,1,0:T(8,128)S(1)}, u32[]{:S(2)}, u32[]{:S(2)}) collective-permute-start(f32[2,16,512]{2,1,0:T(8,128)S(1)} %get-tuple-element.57), channel_id=1, source_target_pairs={{0,4},{1,2},{2,1},{3,7},{4,0},{5,6},{6,5},{7,3},{8,12},{9,10},{10,... | collective-permute-start | bytes 196616 | tf_op jit(solution)/shard_map/ppermute | solution.py:58

commit v5 on v4

--- a/solution.py
+++ b/solution.py
@@ -16,6 +16,7 @@
 LANES = 128
 ROWS = 8
 HALO = 4
+NEAR = HALO // 2
 BASE = 8
 
 
@@ -204,7 +205,7 @@
     for c in range(3):
         value = dealt(magnetic[c].reshape(cx * cz, ny), matrix).reshape(cx, cz, ny)
         core[c] = value
-        low, high = value[:HALO], value[cx - HALO :]
+        low, high = value[:NEAR], value[cx - NEAR :]
         face_xa[c] = jnp.where(even_x, high, low)
         face_xb[c] = jnp.where(even_x, low, high)
         low, high = value[:, :HALO], value[:, cz - HALO :]
@@ -212,24 +213,19 @@
         face_zb[c] = jnp.where(even_z, low, high)
 
 
-def first_forces(parts_ref, parts_of, fp, planes, x_of, cx, cz, blocks, rows, slope):
+def first_forces(parts_ref, parts_of, fp, planes, cz, blocks, rows, slope):
     halo = HALO - 2
-    x_first, x_all, z_first, z_all = own_place(cx, cz)
+    z_first, z_all = lax.axis_index("gz") * cz, lax.axis_size("gz") * cz
 
     def plane(x, slope):
-        own_x = inside_x = None
-        if x_of is not None:
-            own = x_of(x)
-            own_x = (own >= 0) & (own < cx)
-            inside_x = (own + x_first >= 0) & (own + x_first < x_all)
         for r in windows(BASE - halo, BASE + cz + halo):
-            own_z = row_mask(rows, r, cz)
+            own = row_mask(rows, r, cz)
             height = rows + (r - BASE) + z_first
-            inside_z = None if own_z is None else (height >= 0) & (height < z_all)
+            inside = None if own is None else (height >= 0) & (height < z_all)
             for j, force in forces(parts_ref, parts_of(x), r, blocks):
-                slope = slope + masked(dot(force, force), own_z, own_x)
+                slope = slope + masked(dot(force, force), own)
                 for c in range(3):
-                    fp[c, x, j, r : r + ROWS, :] = masked(force[c], inside_z, inside_x)
+                    fp[c, x, j, r : r + ROWS, :] = masked(force[c], inside)
         return slope
 
     return lax.fori_loop(0, planes, plane, slope, unroll=4)
@@ -245,11 +241,11 @@
     return sum(HALO - k for k in range(1, d))
 
 
-def corner_rows(corner, first, d):
-    high, low = [corner[at : at + HALO - d] for at in (first + corner_row(d), first + corner_row(HALO) + corner_row(d))]
+def corner_rows(corner, first, d, reach):
     none = jnp.zeros((d, LANES), jnp.float32)
     if d == HALO:
         return none, none
+    high, low = [corner[at : at + HALO - d] for at in (first + corner_row(d), first + corner_row(reach + 1) + corner_row(d))]
     return jnp.concatenate([high, none], 0), jnp.concatenate([none, low], 0)
 
 
@@ -262,10 +258,10 @@
         for edge in (lambda d: d - 1, lambda d: cx - d):
             pieces = []
             for c in range(3):
-                rims = [sorted_out("gz", face_za[c, edge(d), :, cut], face_zb[c, edge(d), :, cut]) for d in range(1, HALO)]
+                rims = [sorted_out("gz", face_za[c, edge(d), :, cut], face_zb[c, edge(d), :, cut]) for d in range(1, NEAR + 1)]
                 pieces += [high[: HALO - d] for d, (_, high) in enumerate(rims, 1)]
                 pieces += [low[d:] for d, (low, _) in enumerate(rims, 1)]
-            pieces.append(jnp.zeros((corner_a.shape[0] - 6 * corner_row(HALO), LANES), jnp.float32))
+            pieces.append(jnp.zeros((corner_a.shape[0] - 6 * corner_row(NEAR + 1), LANES), jnp.float32))
             packed.append(jnp.concatenate(pieces, axis=0))
         corner_a[:, cut] = jnp.where(even_x, packed[1], packed[0])
         corner_b[:, cut] = jnp.where(even_x, packed[0], packed[1])
@@ -295,67 +291,73 @@
     rows = row_index()
     zero = jnp.zeros((ROWS, LANES), jnp.float32)
     sums_ref[0] = descent_stages(bp, lambda x: x + 1, cx - 2, halo, cz, blocks, parts_ref, None, zero, rows)
-    sums_ref[1] = first_forces(parts_ref, lambda x: x + 1, fp, cx - 4, None, cx, cz, blocks, rows, zero)
-
-
-def outer_kernel(own, part, face_xa, face_xb, corner_a, corner_b, bp, fp, sums_ref, parts_ref):
+    sums_ref[1] = first_forces(parts_ref, lambda x: x + 1, fp, cx - 4, cz, blocks, rows, zero)
+
+
+def outer_kernel(own, part, face_xa, face_xb, corner_a, corner_b, bp, fp, sums_ref, rim_a, rim_b, parts_ref):
     _, cx, blocks, _, _ = own.shape
     cz = face_xa.shape[2]
     halo = HALO - 2
     rows = row_index()
     top = BASE + cz
+    end = NEAR + HALO
 
     def copied(x, _):
         for c in range(3):
             for j in range(blocks):
                 for r in range(0, top + BASE, ROWS):
-                    bp[c, x + HALO, j, r : r + ROWS, :] = own[c, x, j, r : r + ROWS, :]
-                    bp[c, x + 2 * HALO, j, r : r + ROWS, :] = own[c, x + cx - HALO, j, r : r + ROWS, :]
+                    bp[c, x + NEAR, j, r : r + ROWS, :] = own[c, x, j, r : r + ROWS, :]
+                    bp[c, x + end, j, r : r + ROWS, :] = own[c, x + cx - HALO, j, r : r + ROWS, :]
         return 0
 
     lax.fori_loop(0, HALO, copied, 0)
-    for d in range(1, HALO + 1):
+    for d in range(1, NEAR + 1):
         for c in range(3):
             for j in range(blocks):
                 cut = slice(j * LANES, (j + 1) * LANES)
                 corners = sorted_out("gx", corner_a[:, cut], corner_b[:, cut])
-                for side, (plane, k) in enumerate(((HALO - d, HALO - d), (3 * HALO + d - 1, d - 1))):
+                for side, (plane, k) in enumerate(((NEAR - d, NEAR - d), (end + HALO + d - 1, d - 1))):
                     for z in range(0, cz, ROWS):
                         span = slice(z, z + ROWS)
                         value = sorted_out("gx", face_xa[c, k, span, cut], face_xb[c, k, span, cut])[side]
                         bp[c, plane, j, BASE + z : BASE + z + ROWS, :] = value
-                    high, low = corner_rows(corners[side], 2 * c * corner_row(HALO), d)
+                    high, low = corner_rows(corners[side], 2 * c * corner_row(NEAR + 1), d, NEAR)
                     bp[c, plane, j, BASE - HALO : BASE, :] = low
                     bp[c, plane, j, top : top + HALO, :] = high
     functional = descent_stages(
         bp,
-        lambda x: x + 1 + jnp.where(x >= 6, 2, 0),
-        12,
+        lambda x: x + 1 + jnp.where(x >= 4, 2, 0),
+        8,
         halo,
         cz,
         blocks,
         parts_ref,
-        lambda x: (x == 3) | (x == 8),
+        lambda x: (x == 1) | (x == 6),
         part[0],
         rows,
     )
-    slope = first_forces(
-        parts_ref,
-        lambda x: x + 1 + jnp.where(x >= 4, 2, 0),
-        fp,
-        8,
-        lambda x: x - 2 + jnp.where(x >= 4, cx - 4, 0),
-        cx,
-        cz,
-        blocks,
-        rows,
-        part[1],
-    )
+    slope = first_forces(parts_ref, lambda x: x + 1 + jnp.where(x >= 2, 2, 0), fp, 4, cz, blocks, rows, part[1])
     store_sums(sums_ref, functional, slope, rows)
+    even = is_even("gx")
+    for c in range(3):
+        for j in range(blocks):
+            cut = slice(j * LANES, (j + 1) * LANES)
+
+            def send(at, count, low, high):
+                rim_a[at : at + count, cut] = jnp.where(even, high, low)
+                rim_b[at : at + count, cut] = jnp.where(even, low, high)
+
+            for d in range(1, NEAR + 1):
+                for z in range(0, cz, ROWS):
+                    span = slice(BASE + z, BASE + z + ROWS)
+                    send((c * NEAR + d - 1) * cz + z, ROWS, fp[c, d - 1, j, span, :], fp[c, 2 * NEAR - d, j, span, :])
+            for k, r in enumerate((BASE - 1, top)):
+                row = slice(r, r + 1)
+                send(3 * NEAR * cz + 2 * c + k, 1, fp[c, 0, j, row, :], fp[c, 2 * NEAR - 1, j, row, :])
 
 
 def second_kernel(
-    cells, own_b, inner_f, outer_b, outer_f, sums0, core_b, core_f, bp, sums_ref, parts_ref
+    cells, own_b, inner_f, outer_b, outer_f, rim_a, rim_b, sums0, core_b, core_f, bp, sums_ref, parts_ref
 ):
     _, cx, cz, ny = core_b.shape
     blocks = ny // LANES
@@ -377,11 +379,27 @@
         return 0
 
     lax.fori_loop(0, cx - 4, inner_step, 0, unroll=2)
-    for k in range(2):
-        step(k, outer_b, k + 2, outer_f, k)
-        step(k + 2, own_b, k, outer_f, k + 2)
-        step(k + cx, own_b, k + cx - 2, outer_f, k + 4)
-        step(k + cx + 2, outer_b, k + 12, outer_f, k + 6)
+    for k in range(NEAR):
+        step(k + halo, own_b, k, outer_f, k)
+        step(k + cx, own_b, k + cx - NEAR, outer_f, k + NEAR)
+    top = BASE + cz
+    for d in range(1, NEAR + 1):
+        for c in range(3):
+            for j in range(blocks):
+                cut = slice(j * LANES, (j + 1) * LANES)
+                for side, (x, at) in enumerate(((halo - d, NEAR - d), (halo + cx + d - 1, 2 * HALO + NEAR + d - 1))):
+                    for r in (0, top):
+                        bp[c, x, j, r : r + ROWS, :] = outer_b[c, at, j, r : r + ROWS, :]
+                    for z in range(0, cz, ROWS):
+                        r, k = BASE + z, (c * NEAR + d - 1) * cz + z
+                        force = sorted_out("gx", rim_a[k : k + ROWS, cut], rim_b[k : k + ROWS, cut])[side]
+                        bp[c, x, j, r : r + ROWS, :] = outer_b[c, at, j, r : r + ROWS, :] + rate * force
+                    if d > 1:
+                        continue
+                    for n, r in enumerate((BASE - 1, top)):
+                        k = 3 * NEAR * cz + 2 * c + n
+                        force = sorted_out("gx", rim_a[k : k + 1, cut], rim_b[k : k + 1, cut])[side]
+                        bp[c, x, j, r : r + 1, :] = outer_b[c, at, j, r : r + 1, :] + rate * force
     zero = jnp.zeros((ROWS, LANES), jnp.float32)
     functional = descent_stages(
         bp,
@@ -646,7 +664,7 @@
                 corners = sorted_out("gx", corner_a[c, :, cut], corner_b[c, :, cut])
                 for side, plane in enumerate((HALO - d, 2 * HALO + d - 1)):
                     corner = corners[side]
-                    high, low = corner_rows(corner, HALO, d)
+                    high, low = corner_rows(corner, HALO, d, HALO - 1)
                     column(ap, c, plane, j, low, own[side], high, corner[d - 1 : d], rows)
 
     def borrow(into, source, low, high):
@@ -742,7 +760,7 @@
 
     magnetic, *faces = call(
         entry_kernel,
-        [core, *[(3, HALO, cz, ny)] * 2, *[(3, cx, HALO, ny)] * 2],
+        [core, *[(3, NEAR, cz, ny)] * 2, *[(3, cx, HALO, ny)] * 2],
         magnetic,
         cost=work,
         limit=8,
@@ -751,7 +769,7 @@
     faces_z = swapped(faces[2:], "gz")
     corners = call(
         corners_kernel,
-        [(-(-6 * corner_row(HALO) // ROWS) * ROWS, ny)] * 2,
+        [(-(-6 * corner_row(NEAR + 1) // ROWS) * ROWS, ny)] * 2,
         *faces_z,
         cost=work // 50,
     )
@@ -765,17 +783,18 @@
         cost=work,
         limit=9,
     )
-    outer_b, outer_f, sums = call(
+    outer_b, outer_f, sums, *rims = call(
         outer_kernel,
-        [planes_of(3, 4 * HALO), planes_of(3, 8), tiles],
+        [planes_of(3, 2 * (NEAR + HALO)), planes_of(3, 2 * NEAR), tiles, *[(3 * NEAR * cz + ROWS, ny)] * 2],
         own_b,
         part,
         *faces_x,
         *corners,
-        scratch=[planes_of(7, 12)],
+        scratch=[planes_of(7, 8)],
         cost=work,
         limit=9,
     )
+    rims = swapped(rims, "gx")
     core_b, core_f, bp, sums = call(
         functools.partial(second_kernel, cells),
         [core, core, padded(3, HALO - 2), tiles],
@@ -783,6 +802,7 @@
         inner_f,
         outer_b,
         outer_f,
+        *rims,
         shared(sums),
         scratch=[padded(7, 1)],
         cost=work,

time: 63.3 us -> 62.5 us (0.987)
  starting transfers between devices: 9.16 us -> 13.2 us
  waiting for transfers between devices: 6.83 us -> 4.21 us
  blocking collectives: 23.5 us -> 22 us
  Pallas kernels: 21.3 us -> 20.5 us
    ppermute x6 -> x7, starting transfers between devices: 5.17 us -> 8.38 us  [swapped(): lax.ppermute(pair[0], AXES, first)]
    ppermute x6 -> x7, waiting for transfers between devices: 2.64 us -> 0.02 us  [swapped(): lax.ppermute(pair[0], AXES, first)]
    all_to_all x2, blocking collectives: 23.5 us -> 22 us  [shared(): return lax.all_to_all(tile_copies, ('gz', 'gx'), 0, 0)]
    ppermute x6 -> x7, starting transfers between devices: 3.19 us -> 4.13 us  [swapped(): lax.ppermute(pair[1], AXES, second)]
    pallas_call x9, Pallas kernels: 21.3 us -> 20.5 us  [call(): pl.pallas_call(kernel, out_shape=shapes, in_specs=[pl.BlockSpec(memory_sp...]
    ppermute x6 -> x7, waiting for transfers between devices: 4.19 us -> 4.19 us  [swapped(): lax.ppermute(pair[1], AXES, second)]
  transfers between devices with their start and end apart: 13 -> 15, of which waited for: 4 -> 1; matrix products, arithmetic and copies ran while one was open for 0% -> 0% of each run, Pallas kernels for 15% -> 15%
where the time goes in v5:
time: 62.5 us; the launch traced here: 62.3 us
  blocking collectives  22 us (35%)
  Pallas kernels  20.5 us (33%)
  starting transfers between devices  13.2 us (21%)
  waiting for transfers between devices  4.21 us (7%)
  local copies, waits for them, and re-layouts  1.48 us (2%)
  between operations  0.78 us (1%)
    all_to_all x2, blocking collectives, shared(): return lax.all_to_all(tile_copies, ('gz', 'gx'), 0, 0)  22 us
    pallas_call x9, Pallas kernels, call(): pl.pallas_call(kernel, out_shape=shapes, in_specs=[pl.BlockSpec(memory_sp...  20.5 us
    ppermute x7, starting transfers between devices, swapped(): lax.ppermute(pair[0], AXES, first)  8.38 us
    ppermute x7, waiting for transfers between devices, swapped(): lax.ppermute(pair[1], AXES, second)  4.19 us
    ppermute x7, starting transfers between devices, swapped(): lax.ppermute(pair[1], AXES, second)  4.13 us
    unnamed x4, local copies, waits for them, and re-layouts  1.4 us
  transfers between devices with their start and end apart: 15, of which 1 were waited for; matrix products, arithmetic and copies ran while one was open for 0% of the time, Pallas kernels for 15%

profile of v5, /device:TPU:0, one launch (start us, length us, event | category | flops | bytes accessed | tf_op | source)
XLA Modules:
  0.0 62.3 jit_solution(11839703934919797314)
XLA Ops:
  0.6 0.0 copy-start
  0.6 1.4 %copy-done = f32[3,16,16,512]{3,2,1,0:T(8,128)S(1)} copy-done((f32[3,16,16,512]{3,2,1,0:T(8,128)S(1)}, f32[3,16,16,512]{3,2,1,0:T(8,128)}, u32[]{:S(2)}) %copy-start) | copy-done | bytes 1572888
  2.0 1.0 %shard_map.41 = (f32[3,16,16,512]{3,2,1,0:T(8,128)S(1)}, f32[3,2,16,512]{3,2,1,0:T(8,128)S(1)}, f32[3,2,16,512]{3,2,1,0:T(8,128)S(1)}, f32[3,16,4,512]{3,2,1,0:T(4,128)S(1)}, f32[3,16,4,512]{3,2,1,0:T(4,128)S(1)}) custom-call(f32[3,16,16,512]{3,2,1,0:T(8,128)S(1)} %copy-done), custom_call_target="tpu_custom_call" | custom-call | flops 26214400 | bytes 2621440 | tf_op jit(solution)/shard_map/pallas_call | solution.py:731
  3.0 0.5 collective-permute-start
  3.6 2.6 %collective-permute-start.1 = (f32[3,16,4,512]{3,2,1,0:T(4,128)S(1)}, f32[3,16,4,512]{3,2,1,0:T(4,128)S(1)}, u32[]{:S(2)}, u32[]{:S(2)}) collective-permute-start(f32[3,16,4,512]{3,2,1,0:T(4,128)S(1)} %get-tuple-element.37), channel_id=1, source_target_pairs={{0,16},{1,17},{2,18},{3,19},{4,8},{5,9},{6,10},{7,11},{8,4},{9,5},... | collective-permute-start | bytes 1179656 | tf_op jit(solution)/shard_map/ppermute | solution.py:59
  6.2 1.6 %collective-permute-start.2 = (f32[3,2,16,512]{3,2,1,0:T(8,128)S(1)}, f32[3,2,16,512]{3,2,1,0:T(8,128)S(1)}, u32[]{:S(2)}, u32[]{:S(2)}) collective-permute-start(f32[3,2,16,512]{3,2,1,0:T(8,128)S(1)} %get-tuple-element.41), channel_id=1, source_target_pairs={{0,1},{1,0},{2,3},{3,2},{4,5},{5,4},{6,7},{7,6},{8,9},{9,8},{10,11... | collective-permute-start | bytes 589832 | tf_op jit(solution)/shard_map/ppermute | solution.py:59
  7.7 0.0 collective-permute-start.3
  7.7 0.0 collective-permute-done.face_za
  7.7 4.2 %collective-permute-done.1.face_zb = f32[3,16,4,512]{3,2,1,0:T(4,128)S(1)} collective-permute-done((f32[3,16,4,512]{3,2,1,0:T(4,128)S(1)}, f32[3,16,4,512]{3,2,1,0:T(4,128)S(1)}, u32[]{:S(2)}, u32[]{:S(2)}) %collective-permute-start.1) | collective-permute-done | bytes 393248 | tf_op jit(solution)/shard_map/ppermute | solution.py:59
  11.9 0.1 shard_map.43
  12.0 2.1 %collective-permute-start.4 = (f32[32,512]{1,0:T(8,128)S(1)}, f32[32,512]{1,0:T(8,128)S(1)}, u32[]{:S(2)}, u32[]{:S(2)}) collective-permute-start(f32[32,512]{1,0:T(8,128)S(1)} %get-tuple-element.43), channel_id=1, source_target_pairs={{0,1},{1,0},{2,3},{3,2},{4,5},{5,4},{6,7},{7,6},{8,9},{9,8},{10,11... | collective-permute-start | bytes 196616 | tf_op jit(solution)/shard_map/ppermute | solution.py:59
  14.1 0.0 collective-permute-start.5
  14.1 3.1 %shard_map.42 = (f32[3,16,4,32,128]{4,3,2,1,0:T(8,128)S(1)}, f32[3,12,4,32,128]{4,3,2,1,0:T(8,128)S(1)}, f32[2,8,128]{2,1,0:T(8,128)S(1)}) custom-call(f32[3,16,16,512]{3,2,1,0:T(8,128)S(1)} %get-tuple-element.35.core, f32[3,16,4,512]{3,2,1,0:T(4,128)S(1)} %collective-permute-done.face_za, f32[3,16,4,512]{3,2,1,0:T(4,128)S(1)} %collective-permute-done.1.face_zb), custom_call_target="tpu_custom_call" | custom-call | flops 26214400 | bytes 2621440 | tf_op jit(solution)/shard_map/pallas_call | solution.py:731
  17.2 0.0 collective-permute-done.2.face_xa
  17.2 0.0 collective-permute-done.3.face_xb
  17.3 0.0 collective-permute-done.4.corner_a
  17.3 0.0 collective-permute-done.5.corner_b
  17.3 1.7 %shard_map.44 = (f32[3,12,4,32,128]{4,3,2,1,0:T(8,128)S(1)}, f32[3,4,4,32,128]{4,3,2,1,0:T(8,128)S(1)}, f32[16,8,128]{2,1,0:T(8,128)S(1)}, f32[104,512]{1,0:T(8,128)S(1)}, f32[104,512]{1,0:T(8,128)S(1)}) custom-call(f32[3,16,4,32,128]{4,3,2,1,0:T(8,128)S(1)} %get-tuple-element.38.own.own_b, f32[2,8,128]{2,1,0:T(8,128)S(1)} %get-tuple-element.40.part, ...), custom_call_target="tpu_custom_call" | custom-call | flops 26214400 | bytes 2621440 | tf_op jit(solution)/shard_map/pallas_call | solution.py:731
  19.0 3.2 %collective-permute-start.6 = (f32[104,512]{1,0:T(8,128)S(1)}, f32[104,512]{1,0:T(8,128)S(1)}, u32[]{:S(2)}, u32[]{:S(2)}) collective-permute-start(f32[104,512]{1,0:T(8,128)S(1)} %get-tuple-element.47), channel_id=1, source_target_pairs={{0,1},{1,0},{2,3},{3,2},{4,5},{5,4},{6,7},{7,6},{8,9},{9,8},{10,11... | collective-permute-start | bytes 638984 | tf_op jit(solution)/shard_map/ppermute | solution.py:59
  22.2 0.0 collective-permute-start.7
  22.2 10.3 %all_to_all.10.sums0 = f32[16,8,128]{2,1,0:T(8,128)S(1)} all-to-all(f32[16,8,128]{2,1,0:T(8,128)S(1)} %get-tuple-element.49), channel_id=1, replica_groups=mesh['runs'=2,'gz'=4,'gx'=4] {'gz','gx'}, dimensions={0} | all-to-all | bytes 131072 | tf_op jit(solution)/shard_map/all_to_all | solution.py:71
  32.5 0.0 collective-permute-done.6.rim_a
  32.5 0.0 collective-permute-done.7.rim_b
  32.5 0.0 copy-start.1
  32.5 4.0 %shard_map.45 = (f32[3,16,16,512]{3,2,1,0:T(8,128)S(1)}, f32[3,16,16,512]{3,2,1,0:T(8,128)S(1)}, f32[3,20,4,32,128]{4,3,2,1,0:T(8,128)S(1)}, f32[16,8,128]{2,1,0:T(8,128)S(1)}) custom-call(f32[3,16,4,32,128]{4,3,2,1,0:T(8,128)S(1)} %get-tuple-element.38.own.own_b, f32[3,12,4,32,128]{4,3,2,1,0:T(8,128)S(1)} %get-tuple-element.39.inner_f, ...), custom_call_target="tpu_custom_call" | custom-call | flops 26214400 | bytes 2621440 | tf_op jit(solution)/shard_map/pallas_call | solution.py:731
  36.5 0.0 copy-done.1
  36.5 0.1 broadcast_in_dim.2.friction
  36.6 0.5 shard_map.46
  37.1 0.2 collective-permute-start.8
  37.3 1.5 %collective-permute-start.9 = (f32[49,4,512]{2,1,0:T(4,128)S(1)}, f32[49,4,512]{2,1,0:T(4,128)S(1)}, u32[]{:S(2)}, u32[]{:S(2)}) collective-permute-start(f32[49,4,512]{2,1,0:T(4,128)S(1)} %get-tuple-element.55), channel_id=1, source_target_pairs={{0,16},{1,17},{2,18},{3,19},{4,8},{5,9},{6,10},{7,11},{8,4},{9,5},... | collective-permute-start | bytes 1204232 | tf_op jit(solution)/shard_map/ppermute | solution.py:59
  38.8 0.3 collective-permute-start.11
  39.1 0.0 collective-permute-start.12
  39.1 0.0 collective-permute-done.8.refs_2_.face_za
  39.2 0.7 %collective-permute-start.10 = (f32[16,4,512]{2,1,0:T(4,128)S(1)}, f32[16,4,512]{2,1,0:T(4,128)S(1)}, u32[]{:S(2)}, u32[]{:S(2)}) collective-permute-start(f32[16,4,512]{2,1,0:T(4,128)S(1)} %get-tuple-element.68), channel_id=1, source_target_pairs={{0,8},{4,12},{8,0},{12,4},{1,9},{5,13},{9,1},{13,5},{2,10},{6,14},... | collective-permute-start | bytes 393224 | tf_op jit(solution)/shard_map/ppermute | solution.py:826
  39.9 11.7 %all_to_all.11.refs_5_.sums0 = f32[16,8,128]{2,1,0:T(8,128)S(1)} all-to-all(f32[16,8,128]{2,1,0:T(8,128)S(1)} %get-tuple-element.53), channel_id=1, replica_groups=mesh['runs'=2,'gz'=4,'gx'=4] {'gz','gx'}, dimensions={0} | all-to-all | bytes 131072 | tf_op jit(solution)/shard_map/all_to_all | solution.py:71
  51.7 0.0 collective-permute-done.9.refs_3_.face_zb
  51.7 0.0 collective-permute-done.10.refs_1_
  51.7 0.4 shard_map.47
  52.1 0.4 collective-permute-start.13
  52.5 0.0 collective-permute-start.14
  52.5 5.8 %shard_map.48 = (f32[3,16,16,512]{3,2,1,0:T(8,128)}, f32[2,16,4,32,128]{4,3,2,1,0:T(8,128)S(1)}, f32[3,14,4,32,128]{4,3,2,1,0:T(8,128)S(1)}, f32[3,12,4,32,128]{...) custom-call(f32[3,16,16,512]{3,2,1,0:T(8,128)S(1)} %get-tuple-elemen, ...), custom_call_target="tpu_custom_call" | custom-call | flops 26214400 | bytes 2621440 | tf_op jit(solution)/shard_map/pallas_call | solution.py:731
  58.3 0.0 collective-permute-done.11.face_xa
  58.3 0.0 collective-permute-done.12.face_xb
  58.3 0.0 collective-permute-done.13.corner_a
  58.3 0.0 collective-permute-done.14.corner_b
  58.3 3.9 %shard_map.49 = f32[3,16,16,512]{3,2,1,0:T(8,128)} custom-call(f32[3,20,4,32,128]{4,3,2,1,0:T(8,128)S(1)} %get-tuple-element.52.refs_4_.bp, f32[16,8,128]{2,1,0:T(8,128)S(1)} %all_to_all.11.refs_5_.sums0, f32[10,16,512]{2,1,0:T(8,128)S(1)} %collective-permute-done.11.face_xa, f32[10,16,512]{2,1,0:T(8,128)S(1)} %collective-permute-done.12.face_xb, ...), custom_call_target="tpu_custom_call" | custom-call | flops 26214400 | bytes 2621440 | tf_op jit(solution)/shard_map/pallas_call | solution.py:731
  (1 shorter events, 0.0 us)
Async XLA Ops:
  0.6 1.4 %copy-start = (f32[3,16,16,512]{3,2,1,0:T(8,128)S(1)}, f32[3,16,16,512]{3,2,1,0:T(8,128)}, u32[]{:S(2)}) copy-start(f32[3,16,16,512]{3,2,1,0:T(8,128)} %magnetic.1) | copy-start | bytes 4718596
  3.0 4.7 %collective-permute-start = (f32[3,16,4,512]{3,2,1,0:T(4,128)S(1)}, f32[3,16,4,512]{3,2,1,0:T(4,128)S(1)}, u32[]{:S(2)}, u32[]{:S(2)}) collective-permute-start(f32[3,16,4,512]{3,2,1,0:T(4,128)S(1)} %get-tuple-element.36), channel_id=1, source_target_pairs={{0,4},{1,5},{2,6},{3,7},{4,0},{5,1},{6,2},{7,3},{8,12},{9,13},{10,... | collective-permute-start | bytes 1179656 | tf_op jit(solution)/shard_map/ppermute | solution.py:59
  3.6 8.3 %collective-permute-start.1 = (f32[3,16,4,512]{3,2,1,0:T(4,128)S(1)}, f32[3,16,4,512]{3,2,1,0:T(4,128)S(1)}, u32[]{:S(2)}, u32[]{:S(2)}) collective-permute-start(f32[3,16,4,512]{3,2,1,0:T(4,128)S(1)} %get-tuple-element.37), channel_id=1, source_target_pairs={{0,16},{1,17},{2,18},{3,19},{4,8},{5,9},{6,10},{7,11},{8,4},{9,5},... | collective-permute-start | bytes 1179656 | tf_op jit(solution)/shard_map/ppermute | solution.py:59
  6.2 11.1 %collective-permute-start.2 = (f32[3,2,16,512]{3,2,1,0:T(8,128)S(1)}, f32[3,2,16,512]{3,2,1,0:T(8,128)S(1)}, u32[]{:S(2)}, u32[]{:S(2)}) collective-permute-start(f32[3,2,16,512]{3,2,1,0:T(8,128)S(1)} %get-tuple-element.41), channel_id=1, source_target_pairs={{0,1},{1,0},{2,3},{3,2},{4,5},{5,4},{6,7},{7,6},{8,9},{9,8},{10,11... | collective-permute-start | bytes 589832 | tf_op jit(solution)/shard_map/ppermute | solution.py:59
  7.7 9.5 %collective-permute-start.3 = (f32[3,2,16,512]{3,2,1,0:T(8,128)S(1)}, f32[3,2,16,512]{3,2,1,0:T(8,128)S(1)}, u32[]{:S(2)}, u32[]{:S(2)}) collective-permute-start(f32[3,2,16,512]{3,2,1,0:T(8,128)S(1)} %get-tuple-element.42), channel_id=1, source_target_pairs={{0,4},{1,2},{2,1},{3,7},{4,0},{5,6},{6,5},{7,3},{8,12},{9,10},{10,... | collective-permute-start | bytes 589832 | tf_op jit(solution)/shard_map/ppermute | solution.py:59
  12.0 5.3 %collective-permute-start.4 = (f32[32,512]{1,0:T(8,128)S(1)}, f32[32,512]{1,0:T(8,128)S(1)}, u32[]{:S(2)}, u32[]{:S(2)}) collective-permute-start(f32[32,512]{1,0:T(8,128)S(1)} %get-tuple-element.43), channel_id=1, source_target_pairs={{0,1},{1,0},{2,3},{3,2},{4,5},{5,4},{6,7},{7,6},{8,9},{9,8},{10,11... | collective-permute-start | bytes 196616 | tf_op jit(solution)/shard_map/ppermute | solution.py:59
  14.1 3.1 %collective-permute-start.5 = (f32[32,512]{1,0:T(8,128)S(1)}, f32[32,512]{1,0:T(8,128)S(1)}, u32[]{:S(2)}, u32[]{:S(2)}) collective-permute-start(f32[32,512]{1,0:T(8,128)S(1)} %get-tuple-element.44), channel_id=1, source_target_pairs={{0,4},{1,2},{2,1},{3,7},{4,0},{5,6},{6,5},{7,3},{8,12},{9,10},{10,... | collective-permute-start | bytes 196616 | tf_op jit(solution)/shard_map/ppermute | solution.py:59
  19.0 13.5 %collective-permute-start.6 = (f32[104,512]{1,0:T(8,128)S(1)}, f32[104,512]{1,0:T(8,128)S(1)}, u32[]{:S(2)}, u32[]{:S(2)}) collective-permute-start(f32[104,512]{1,0:T(8,128)S(1)} %get-tuple-element.47), channel_id=1, source_target_pairs={{0,1},{1,0},{2,3},{3,2},{4,5},{5,4},{6,7},{7,6},{8,9},{9,8},{10,11... | collective-permute-start | bytes 638984 | tf_op jit(solution)/shard_map/ppermute | solution.py:59
  22.2 10.3 %collective-permute-start.7 = (f32[104,512]{1,0:T(8,128)S(1)}, f32[104,512]{1,0:T(8,128)S(1)}, u32[]{:S(2)}, u32[]{:S(2)}) collective-permute-start(f32[104,512]{1,0:T(8,128)S(1)} %get-tuple-element.48), channel_id=1, source_target_pairs={{0,4},{1,2},{2,1},{3,7},{4,0},{5,6},{6,5},{7,3},{8,12},{9,10},{10,... | collective-permute-start | bytes 638984 | tf_op jit(solution)/shard_map/ppermute | solution.py:59
  32.5 4.0 %copy-start.1 = (f32[16]{0:T(128)S(1)}, f32[16]{0:T(128)}, u32[]{:S(2)}) copy-start(f32[16]{0:T(128)} %param.3) | copy-start | bytes 196
  37.1 2.1 %collective-permute-start.8 = (f32[65,4,512]{2,1,0:T(4,128)S(1)}, f32[65,4,512]{2,1,0:T(4,128)S(1)}, u32[]{:S(2)}, u32[]{:S(2)}) collective-permute-start(f32[65,4,512]{2,1,0:T(4,128)S(1)} %get-tuple-element.54), channel_id=1, source_target_pairs={{0,4},{1,5},{2,6},{3,7},{4,0},{5,1},{6,2},{7,3},{8,12},{9,13},{10,... | collective-permute-start | bytes 1597448 | tf_op jit(solution)/shard_map/ppermute | solution.py:59
  37.3 14.4 %collective-permute-start.9 = (f32[49,4,512]{2,1,0:T(4,128)S(1)}, f32[49,4,512]{2,1,0:T(4,128)S(1)}, u32[]{:S(2)}, u32[]{:S(2)}) collective-permute-start(f32[49,4,512]{2,1,0:T(4,128)S(1)} %get-tuple-element.55), channel_id=1, source_target_pairs={{0,16},{1,17},{2,18},{3,19},{4,8},{5,9},{6,10},{7,11},{8,4},{9,5},... | collective-permute-start | bytes 1204232 | tf_op jit(solution)/shard_map/ppermute | solution.py:59
  38.8 19.5 %collective-permute-start.11 = (f32[10,16,512]{2,1,0:T(8,128)S(1)}, f32[10,16,512]{2,1,0:T(8,128)S(1)}, u32[]{:S(2)}, u32[]{:S(2)}) collective-permute-start(f32[10,16,512]{2,1,0:T(8,128)S(1)} %get-tuple-element.58), channel_id=1, source_target_pairs={{0,1},{1,0},{2,3},{3,2},{4,5},{5,4},{6,7},{7,6},{8,9},{9,8},{10,11... | collective-permute-start | bytes 983048 | tf_op jit(solution)/shard_map/ppermute | solution.py:59
  39.1 19.2 %collective-permute-start.12 = (f32[10,16,512]{2,1,0:T(8,128)S(1)}, f32[10,16,512]{2,1,0:T(8,128)S(1)}, u32[]{:S(2)}, u32[]{:S(2)}) collective-permute-start(f32[10,16,512]{2,1,0:T(8,128)S(1)} %get-tuple-element.59), channel_id=1, source_target_pairs={{0,4},{1,2},{2,1},{3,7},{4,0},{5,6},{6,5},{7,3},{8,12},{9,10},{10,... | collective-permute-start | bytes 983048 | tf_op jit(solution)/shard_map/ppermute | solution.py:59
  39.2 12.5 %collective-permute-start.10 = (f32[16,4,512]{2,1,0:T(4,128)S(1)}, f32[16,4,512]{2,1,0:T(4,128)S(1)}, u32[]{:S(2)}, u32[]{:S(2)}) collective-permute-start(f32[16,4,512]{2,1,0:T(4,128)S(1)} %get-tuple-element.68), channel_id=1, source_target_pairs={{0,8},{4,12},{8,0},{12,4},{1,9},{5,13},{9,1},{13,5},{2,10},{6,14},... | collective-permute-start | bytes 393224 | tf_op jit(solution)/shard_map/ppermute | solution.py:826
  52.1 6.2 %collective-permute-start.13 = (f32[2,16,512]{2,1,0:T(8,128)S(1)}, f32[2,16,512]{2,1,0:T(8,128)S(1)}, u32[]{:S(2)}, u32[]{:S(2)}) collective-permute-start(f32[2,16,512]{2,1,0:T(8,128)S(1)} %get-tuple-element.60), channel_id=1, source_target_pairs={{0,1},{1,0},{2,3},{3,2},{4,5},{5,4},{6,7},{7,6},{8,9},{9,8},{10,11... | collective-permute-start | bytes 196616 | tf_op jit(solution)/shard_map/ppermute | solution.py:59
  52.5 5.8 %collective-permute-start.14 = (f32[2,16,512]{2,1,0:T(8,128)S(1)}, f32[2,16,512]{2,1,0:T(8,128)S(1)}, u32[]{:S(2)}, u32[]{:S(2)}) collective-permute-start(f32[2,16,512]{2,1,0:T(8,128)S(1)} %get-tuple-element.61), channel_id=1, source_target_pairs={{0,4},{1,2},{2,1},{3,7},{4,0},{5,6},{6,5},{7,3},{8,12},{9,10},{10,... | collective-permute-start | bytes 196616 | tf_op jit(solution)/shard_map/ppermute | solution.py:59

commit v6 on v5

--- a/solution.py
+++ b/solution.py
@@ -198,9 +198,9 @@
     return (0.25 * step_scale) * functional / (slope + 1e-6)
 
 
-def entry_kernel(magnetic, core, face_xa, face_xb, face_za, face_zb):
+def entry_kernel(magnetic, core, face_xa, face_xb):
     _, cx, cz, ny = magnetic.shape
-    even_x, even_z = is_even("gx"), is_even("gz")
+    even_x = is_even("gx")
     matrix = dealing(ny, False)
     for c in range(3):
         value = dealt(magnetic[c].reshape(cx * cz, ny), matrix).reshape(cx, cz, ny)
@@ -208,9 +208,6 @@
         low, high = value[:NEAR], value[cx - NEAR :]
         face_xa[c] = jnp.where(even_x, high, low)
         face_xb[c] = jnp.where(even_x, low, high)
-        low, high = value[:, :HALO], value[:, cz - HALO :]
-        face_za[c] = jnp.where(even_z, high, low)
-        face_zb[c] = jnp.where(even_z, low, high)
 
 
 def first_forces(parts_ref, parts_of, fp, planes, cz, blocks, rows, slope):
@@ -273,10 +270,13 @@
     bp[c, plane, j, top : top + HALO, :] = high
 
 
-def inner_kernel(core, face_za, face_zb, bp, fp, sums_ref, parts_ref):
+def inner_kernel(core, face_za, face_zb, bp, fp, sums_ref, parts_ref, faces):
     _, cx, cz, ny = core.shape
     blocks = ny // LANES
     halo = HALO - 2
+
+    both = jnp.concatenate([face_za[...], face_zb[...]], axis=2)
+    faces[...] = dealt(both.reshape(-1, ny), dealing(ny, False)).reshape(faces.shape)
 
     def own(x, _):
         for c in range(3):
@@ -284,7 +284,7 @@
                 cut = slice(j * LANES, (j + 1) * LANES)
                 for z in range(0, cz, ROWS):
                     bp[c, x, j, BASE + z : BASE + z + ROWS, :] = core[c, x, z : z + ROWS, cut]
-                z_halos(bp, c, x, j, BASE + cz, face_za[c, x, :, cut], face_zb[c, x, :, cut])
+                z_halos(bp, c, x, j, BASE + cz, faces[c, x, :HALO, cut], faces[c, x, HALO:, cut])
         return 0
 
     lax.fori_loop(0, cx, own, 0)
@@ -294,7 +294,7 @@
     sums_ref[1] = first_forces(parts_ref, lambda x: x + 1, fp, cx - 4, cz, blocks, rows, zero)
 
 
-def outer_kernel(own, part, face_xa, face_xb, corner_a, corner_b, bp, fp, sums_ref, rim_a, rim_b, parts_ref):
+def outer_kernel(own, part, face_xa, face_xb, corner_a, corner_b, bp, fp, sums_ref, rim_a, rim_b, parts_ref, corner):
     _, cx, blocks, _, _ = own.shape
     cz = face_xa.shape[2]
     halo = HALO - 2
@@ -311,11 +311,14 @@
         return 0
 
     lax.fori_loop(0, HALO, copied, 0)
+    ny = corner_a.shape[1]
+    corner[...] = dealt(jnp.concatenate([corner_a[...], corner_b[...]], axis=0), dealing(ny, False))
+    count = corner_a.shape[0]
     for d in range(1, NEAR + 1):
         for c in range(3):
             for j in range(blocks):
                 cut = slice(j * LANES, (j + 1) * LANES)
-                corners = sorted_out("gx", corner_a[:, cut], corner_b[:, cut])
+                corners = sorted_out("gx", corner[:count, cut], corner[count:, cut])
                 for side, (plane, k) in enumerate(((NEAR - d, NEAR - d), (end + HALO + d - 1, d - 1))):
                     for z in range(0, cz, ROWS):
                         span = slice(z, z + ROWS)
@@ -758,30 +761,30 @@
     core = (3, cx, cz, ny)
     rubbed = jnp.broadcast_to(friction[:, None], (cz, LANES))
 
-    magnetic, *faces = call(
+    even, far = is_even("gz"), cz - HALO
+    faces_z = [
+        lax.dynamic_slice_in_dim(magnetic, jnp.where(even == first, far, 0), HALO, 2) for first in (True, False)
+    ]
+    faces_z = swapped(faces_z, "gz")
+    magnetic, *faces_x = call(
         entry_kernel,
-        [core, *[(3, NEAR, cz, ny)] * 2, *[(3, cx, HALO, ny)] * 2],
+        [core, *[(3, NEAR, cz, ny)] * 2],
         magnetic,
         cost=work,
         limit=8,
     )
-    faces_x = swapped(faces[:2], "gx")
-    faces_z = swapped(faces[2:], "gz")
-    corners = call(
-        corners_kernel,
-        [(-(-6 * corner_row(NEAR + 1) // ROWS) * ROWS, ny)] * 2,
-        *faces_z,
-        cost=work // 50,
-    )
+    faces_x = swapped(faces_x, "gx")
+    corner = (-(-6 * corner_row(NEAR + 1) // ROWS) * ROWS, ny)
+    corners = call(corners_kernel, [corner] * 2, *faces_z, cost=work // 50)
     corners = swapped(corners, "gx")
     own_b, inner_f, part = call(
         inner_kernel,
         [padded(3, 0), padded(3, -2), (2, ROWS, LANES)],
         magnetic,
         *faces_z,
-        scratch=[padded(7, -1)],
+        scratch=[padded(7, -1), (3, cx, 2 * HALO, ny)],
         cost=work,
-        limit=9,
+        limit=13,
     )
     outer_b, outer_f, sums, *rims = call(
         outer_kernel,
@@ -790,7 +793,7 @@
         part,
         *faces_x,
         *corners,
-        scratch=[planes_of(7, 8)],
+        scratch=[planes_of(7, 8), (2 * corner[0], ny)],
         cost=work,
         limit=9,
     )

time: 62.5 us -> 61.9 us (level)
  waiting for transfers between devices: 4.21 us -> 2.9 us
  Pallas kernels: 20.5 us -> 21.3 us
    dynamic_slice x0 -> x1, local copies, waits for them, and re-layouts: none -> 1.67 us  [body(): lax.dynamic_slice_in_dim(magnetic, jnp.where(even == first, far, 0), HALO...]
    unnamed x4, local copies, waits for them, and re-layouts: 1.4 us -> 0.01 us
    ppermute x7, waiting for transfers between devices: 4.19 us -> 2.88 us  [swapped(): lax.ppermute(pair[1], AXES, second)]
    pallas_call x9, Pallas kernels: 20.5 us -> 21.3 us  [call(): pl.pallas_call(kernel, out_shape=shapes, in_specs=[pl.BlockSpec(memory_sp...]
  transfers between devices with their start and end apart: 15 -> 15, of which waited for: 1 -> 1; matrix products, arithmetic and copies ran while one was open for 0% -> 0% of each run, Pallas kernels for 15% -> 18%
where the time goes in v6:
time: 61.9 us; the launch traced here: 61.7 us
  blocking collectives  21.4 us (35%)
  Pallas kernels  21.3 us (34%)
  starting transfers between devices  13.5 us (22%)
  waiting for transfers between devices  2.9 us (5%)
  local copies, waits for them, and re-layouts  1.75 us (3%)
  between operations  0.8 us (1%)
    all_to_all x2, blocking collectives, shared(): return lax.all_to_all(tile_copies, ('gz', 'gx'), 0, 0)  21.4 us
    pallas_call x9, Pallas kernels, call(): pl.pallas_call(kernel, out_shape=shapes, in_specs=[pl.BlockSpec(memory_sp...  21.3 us
    ppermute x7, starting transfers between devices, swapped(): lax.ppermute(pair[0], AXES, first)  8.02 us
    ppermute x7, starting transfers between devices, swapped(): lax.ppermute(pair[1], AXES, second)  4.72 us
    ppermute x7, waiting for transfers between devices, swapped(): lax.ppermute(pair[1], AXES, second)  2.88 us
    dynamic_slice x1, local copies, waits for them, and re-layouts, body(): lax.dynamic_slice_in_dim(magnetic, jnp.where(even == first, far, 0), HALO...  1.67 us
  transfers between devices with their start and end apart: 15, of which 1 were waited for; matrix products, arithmetic and copies ran while one was open for 0% of the time, Pallas kernels for 18%

profile of v6, /device:TPU:0, one launch (start us, length us, event | category | flops | bytes accessed | tf_op | source)
XLA Modules:
  0.0 61.7 jit_solution(18083104757350363353)
XLA Ops:
  0.6 0.0 copy-start
  0.7 1.7 %constant_dynamic-slice_fusion = (f32[3,16,4,512]{3,2,1,0:T(4,128)S(1)}, f32[3,16,4,512]{3,2,1,0:T(4,128)S(1)}) fusion(f32[3,16,16,512]{3,2,1,0:T(8,128)} %magnetic.1, s32[]{:T(128)S(6)} %select_n.18, s32[]{:T(128)S(6)} %select_n.17), kind=kLoop, calls=%fused_computation.1 | loop fusion | bytes 1572872 | tf_op jit(solution)/shard_map/dynamic_slice | solution.py:766
  2.3 3.0 %collective-permute-start.1 = (f32[3,16,4,512]{3,2,1,0:T(4,128)S(1)}, f32[3,16,4,512]{3,2,1,0:T(4,128)S(1)}, u32[]{:S(2)}, u32[]{:S(2)}) collective-permute-start(f32[3,16,4,512]{3,2,1,0:T(4,128)S(1)} %get-tuple-element.64), channel_id=1, source_target_pairs={{0,16},{1,17},{2,18},{3,19},{4,8},{5,9},{6,10},{7,11},{8,4},{9,5},... | collective-permute-start | bytes 1179656 | tf_op jit(solution)/shard_map/ppermute | solution.py:59
  5.4 0.1 collective-permute-start
  5.5 0.0 copy-done
  5.5 1.0 %shard_map.41 = (f32[3,16,16,512]{3,2,1,0:T(8,128)S(1)}, f32[3,2,16,512]{3,2,1,0:T(8,128)S(1)}, f32[3,2,16,512]{3,2,1,0:T(8,128)S(1)}) custom-call(f32[3,16,16,512]{3,2,1,0:T(8,128)S(1)} %copy-done), custom_call_target="tpu_custom_call" | custom-call | flops 26214400 | bytes 2621440 | tf_op jit(solution)/shard_map/pallas_call | solution.py:734
  6.5 1.6 %collective-permute-start.2 = (f32[3,2,16,512]{3,2,1,0:T(8,128)S(1)}, f32[3,2,16,512]{3,2,1,0:T(8,128)S(1)}, u32[]{:S(2)}, u32[]{:S(2)}) collective-permute-start(f32[3,2,16,512]{3,2,1,0:T(8,128)S(1)} %get-tuple-element.37), channel_id=1, source_target_pairs={{0,1},{1,0},{2,3},{3,2},{4,5},{5,4},{6,7},{7,6},{8,9},{9,8},{10,11... | collective-permute-start | bytes 589832 | tf_op jit(solution)/shard_map/ppermute | solution.py:59
  8.1 0.2 collective-permute-start.3
  8.3 2.9 %collective-permute-done.1.face_zb = f32[3,16,4,512]{3,2,1,0:T(4,128)S(1)} collective-permute-done((f32[3,16,4,512]{3,2,1,0:T(4,128)S(1)}, f32[3,16,4,512]{3,2,1,0:T(4,128)S(1)}, u32[]{:S(2)}, u32[]{:S(2)}) %collective-permute-start.1) | collective-permute-done | bytes 393248 | tf_op jit(solution)/shard_map/ppermute | solution.py:59
  11.1 0.0 collective-permute-done.face_za
  11.1 0.1 shard_map.43
  11.2 2.1 %collective-permute-start.4 = (f32[32,512]{1,0:T(8,128)S(1)}, f32[32,512]{1,0:T(8,128)S(1)}, u32[]{:S(2)}, u32[]{:S(2)}) collective-permute-start(f32[32,512]{1,0:T(8,128)S(1)} %get-tuple-element.39), channel_id=1, source_target_pairs={{0,1},{1,0},{2,3},{3,2},{4,5},{5,4},{6,7},{7,6},{8,9},{9,8},{10,11... | collective-permute-start | bytes 196616 | tf_op jit(solution)/shard_map/ppermute | solution.py:59
  13.3 0.0 collective-permute-start.5
  13.3 3.7 %shard_map.42 = (f32[3,16,4,32,128]{4,3,2,1,0:T(8,128)S(1)}, f32[3,12,4,32,128]{4,3,2,1,0:T(8,128)S(1)}, f32[2,8,128]{2,1,0:T(8,128)S(1)}) custom-call(f32[3,16,16,512]{3,2,1,0:T(8,128)S(1)} %get-tuple-element.33.core, f32[3,16,4,512]{3,2,1,0:T(4,128)S(1)} %collective-permute-done.face_za, f32[3,16,4,512]{3,2,1,0:T(4,128)S(1)} %collective-permute-done.1.face_zb), custom_call_target="tpu_custom_call" | custom-call | flops 26214400 | bytes 2621440 | tf_op jit(solution)/shard_map/pallas_call | solution.py:734
  17.0 0.0 collective-permute-done.2.face_xa
  17.1 0.0 collective-permute-done.3.face_xb
  17.1 0.0 collective-permute-done.4.corner_a
  17.1 0.0 collective-permute-done.5.corner_b
  17.1 1.9 %shard_map.44 = (f32[3,12,4,32,128]{4,3,2,1,0:T(8,128)S(1)}, f32[3,4,4,32,128]{4,3,2,1,0:T(8,128)S(1)}, f32[16,8,128]{2,1,0:T(8,128)S(1)}, f32[104,512]{1,0:T(8,128)S(1)}, f32[104,512]{1,0:T(8,128)S(1)}) custom-call(f32[3,16,4,32,128]{4,3,2,1,0:T(8,128)S(1)} %get-tuple-element.34.own.own_b, f32[2,8,128]{2,1,0:T(8,128)S(1)} %get-tuple-element.36.part, ...), custom_call_target="tpu_custom_call" | custom-call | flops 26214400 | bytes 2621440 | tf_op jit(solution)/shard_map/pallas_call | solution.py:734
  19.0 3.2 %collective-permute-start.6 = (f32[104,512]{1,0:T(8,128)S(1)}, f32[104,512]{1,0:T(8,128)S(1)}, u32[]{:S(2)}, u32[]{:S(2)}) collective-permute-start(f32[104,512]{1,0:T(8,128)S(1)} %get-tuple-element.43), channel_id=1, source_target_pairs={{0,1},{1,0},{2,3},{3,2},{4,5},{5,4},{6,7},{7,6},{8,9},{9,8},{10,11... | collective-permute-start | bytes 638984 | tf_op jit(solution)/shard_map/ppermute | solution.py:59
  22.2 0.0 collective-permute-start.7
  22.2 9.7 %all_to_all.10.sums0 = f32[16,8,128]{2,1,0:T(8,128)S(1)} all-to-all(f32[16,8,128]{2,1,0:T(8,128)S(1)} %get-tuple-element.45), channel_id=1, replica_groups=mesh['runs'=2,'gz'=4,'gx'=4] {'gz','gx'}, dimensions={0} | all-to-all | bytes 131072 | tf_op jit(solution)/shard_map/all_to_all | solution.py:71
  31.9 0.0 collective-permute-done.6.rim_a
  31.9 0.0 collective-permute-done.7.rim_b
  31.9 0.0 copy-start.1
  31.9 4.0 %shard_map.45 = (f32[3,16,16,512]{3,2,1,0:T(8,128)S(1)}, f32[3,16,16,512]{3,2,1,0:T(8,128)S(1)}, f32[3,20,4,32,128]{4,3,2,1,0:T(8,128)S(1)}, f32[16,8,128]{2,1,0:T(8,128)S(1)}) custom-call(f32[3,16,4,32,128]{4,3,2,1,0:T(8,128)S(1)} %get-tuple-element.34.own.own_b, f32[3,12,4,32,128]{4,3,2,1,0:T(8,128)S(1)} %get-tuple-element.35.inner_f, ...), custom_call_target="tpu_custom_call" | custom-call | flops 26214400 | bytes 2621440 | tf_op jit(solution)/shard_map/pallas_call | solution.py:734
  35.9 0.0 copy-done.1
  35.9 0.1 broadcast_in_dim.2.friction
  36.0 0.5 shard_map.46
  36.5 0.2 collective-permute-start.8
  36.7 1.5 %collective-permute-start.9 = (f32[49,4,512]{2,1,0:T(4,128)S(1)}, f32[49,4,512]{2,1,0:T(4,128)S(1)}, u32[]{:S(2)}, u32[]{:S(2)}) collective-permute-start(f32[49,4,512]{2,1,0:T(4,128)S(1)} %get-tuple-element.51), channel_id=1, source_target_pairs={{0,16},{1,17},{2,18},{3,19},{4,8},{5,9},{6,10},{7,11},{8,4},{9,5},... | collective-permute-start | bytes 1204232 | tf_op jit(solution)/shard_map/ppermute | solution.py:59
  38.2 0.3 collective-permute-start.11
  38.6 0.0 collective-permute-start.12
  38.6 0.0 collective-permute-done.8.refs_2_.face_za
  38.6 0.7 %collective-permute-start.10 = (f32[16,4,512]{2,1,0:T(4,128)S(1)}, f32[16,4,512]{2,1,0:T(4,128)S(1)}, u32[]{:S(2)}, u32[]{:S(2)}) collective-permute-start(f32[16,4,512]{2,1,0:T(4,128)S(1)} %get-tuple-element.66), channel_id=1, source_target_pairs={{0,8},{4,12},{8,0},{12,4},{1,9},{5,13},{9,1},{13,5},{2,10},{6,14},... | collective-permute-start | bytes 393224 | tf_op jit(solution)/shard_map/ppermute | solution.py:829
  39.4 11.7 %all_to_all.11.refs_5_.sums0 = f32[16,8,128]{2,1,0:T(8,128)S(1)} all-to-all(f32[16,8,128]{2,1,0:T(8,128)S(1)} %get-tuple-element.49), channel_id=1, replica_groups=mesh['runs'=2,'gz'=4,'gx'=4] {'gz','gx'}, dimensions={0} | all-to-all | bytes 131072 | tf_op jit(solution)/shard_map/all_to_all | solution.py:71
  51.1 0.0 collective-permute-done.9.refs_3_.face_zb
  51.1 0.0 collective-permute-done.10.refs_1_
  51.1 0.4 shard_map.47
  51.5 0.4 collective-permute-start.13
  51.9 0.0 collective-permute-start.14
  51.9 5.8 %shard_map.48 = (f32[3,16,16,512]{3,2,1,0:T(8,128)}, f32[2,16,4,32,128]{4,3,2,1,0:T(8,128)S(1)}, f32[3,14,4,32,128]{4,3,2,1,0:T(8,128)S(1)}, f32[3,12,4,32,128]{...) custom-call(f32[3,16,16,512]{3,2,1,0:T(8,128)S(1)} %get-tuple-elemen, ...), custom_call_target="tpu_custom_call" | custom-call | flops 26214400 | bytes 2621440 | tf_op jit(solution)/shard_map/pallas_call | solution.py:734
  57.7 0.0 collective-permute-done.11.face_xa
  57.7 0.0 collective-permute-done.12.face_xb
  57.7 0.0 collective-permute-done.13.corner_a
  57.7 0.0 collective-permute-done.14.corner_b
  57.8 3.9 %shard_map.49 = f32[3,16,16,512]{3,2,1,0:T(8,128)} custom-call(f32[3,20,4,32,128]{4,3,2,1,0:T(8,128)S(1)} %get-tuple-element.48.refs_4_.bp, f32[16,8,128]{2,1,0:T(8,128)S(1)} %all_to_all.11.refs_5_.sums0, f32[10,16,512]{2,1,0:T(8,128)S(1)} %collective-permute-done.11.face_xa, f32[10,16,512]{2,1,0:T(8,128)S(1)} %collective-permute-done.12.face_xb, ...), custom_call_target="tpu_custom_call" | custom-call | flops 26214400 | bytes 2621440 | tf_op jit(solution)/shard_map/pallas_call | solution.py:734
  (1 shorter events, 0.0 us)
Async XLA Ops:
  0.6 4.8 %copy-start = (f32[3,16,16,512]{3,2,1,0:T(8,128)S(1)}, f32[3,16,16,512]{3,2,1,0:T(8,128)}, u32[]{:S(2)}) copy-start(f32[3,16,16,512]{3,2,1,0:T(8,128)} %magnetic.1) | copy-start | bytes 4718596
  2.3 8.8 %collective-permute-start.1 = (f32[3,16,4,512]{3,2,1,0:T(4,128)S(1)}, f32[3,16,4,512]{3,2,1,0:T(4,128)S(1)}, u32[]{:S(2)}, u32[]{:S(2)}) collective-permute-start(f32[3,16,4,512]{3,2,1,0:T(4,128)S(1)} %get-tuple-element.64), channel_id=1, source_target_pairs={{0,16},{1,17},{2,18},{3,19},{4,8},{5,9},{6,10},{7,11},{8,4},{9,5},... | collective-permute-start | bytes 1179656 | tf_op jit(solution)/shard_map/ppermute | solution.py:59
  5.4 5.8 %collective-permute-start = (f32[3,16,4,512]{3,2,1,0:T(4,128)S(1)}, f32[3,16,4,512]{3,2,1,0:T(4,128)S(1)}, u32[]{:S(2)}, u32[]{:S(2)}) collective-permute-start(f32[3,16,4,512]{3,2,1,0:T(4,128)S(1)} %get-tuple-element.65), channel_id=1, source_target_pairs={{0,4},{1,5},{2,6},{3,7},{4,0},{5,1},{6,2},{7,3},{8,12},{9,13},{10,... | collective-permute-start | bytes 1179656 | tf_op jit(solution)/shard_map/ppermute | solution.py:59
  6.5 10.6 %collective-permute-start.2 = (f32[3,2,16,512]{3,2,1,0:T(8,128)S(1)}, f32[3,2,16,512]{3,2,1,0:T(8,128)S(1)}, u32[]{:S(2)}, u32[]{:S(2)}) collective-permute-start(f32[3,2,16,512]{3,2,1,0:T(8,128)S(1)} %get-tuple-element.37), channel_id=1, source_target_pairs={{0,1},{1,0},{2,3},{3,2},{4,5},{5,4},{6,7},{7,6},{8,9},{9,8},{10,11... | collective-permute-start | bytes 589832 | tf_op jit(solution)/shard_map/ppermute | solution.py:59
  8.1 9.0 %collective-permute-start.3 = (f32[3,2,16,512]{3,2,1,0:T(8,128)S(1)}, f32[3,2,16,512]{3,2,1,0:T(8,128)S(1)}, u32[]{:S(2)}, u32[]{:S(2)}) collective-permute-start(f32[3,2,16,512]{3,2,1,0:T(8,128)S(1)} %get-tuple-element.38), channel_id=1, source_target_pairs={{0,4},{1,2},{2,1},{3,7},{4,0},{5,6},{6,5},{7,3},{8,12},{9,10},{10,... | collective-permute-start | bytes 589832 | tf_op jit(solution)/shard_map/ppermute | solution.py:59
  11.2 5.9 %collective-permute-start.4 = (f32[32,512]{1,0:T(8,128)S(1)}, f32[32,512]{1,0:T(8,128)S(1)}, u32[]{:S(2)}, u32[]{:S(2)}) collective-permute-start(f32[32,512]{1,0:T(8,128)S(1)} %get-tuple-element.39), channel_id=1, source_target_pairs={{0,1},{1,0},{2,3},{3,2},{4,5},{5,4},{6,7},{7,6},{8,9},{9,8},{10,11... | collective-permute-start | bytes 196616 | tf_op jit(solution)/shard_map/ppermute | solution.py:59
  13.3 3.7 %collective-permute-start.5 = (f32[32,512]{1,0:T(8,128)S(1)}, f32[32,512]{1,0:T(8,128)S(1)}, u32[]{:S(2)}, u32[]{:S(2)}) collective-permute-start(f32[32,512]{1,0:T(8,128)S(1)} %get-tuple-element.40), channel_id=1, source_target_pairs={{0,4},{1,2},{2,1},{3,7},{4,0},{5,6},{6,5},{7,3},{8,12},{9,10},{10,... | collective-permute-start | bytes 196616 | tf_op jit(solution)/shard_map/ppermute | solution.py:59
  19.0 12.9 %collective-permute-start.6 = (f32[104,512]{1,0:T(8,128)S(1)}, f32[104,512]{1,0:T(8,128)S(1)}, u32[]{:S(2)}, u32[]{:S(2)}) collective-permute-start(f32[104,512]{1,0:T(8,128)S(1)} %get-tuple-element.43), channel_id=1, source_target_pairs={{0,1},{1,0},{2,3},{3,2},{4,5},{5,4},{6,7},{7,6},{8,9},{9,8},{10,11... | collective-permute-start | bytes 638984 | tf_op jit(solution)/shard_map/ppermute | solution.py:59
  22.2 9.7 %collective-permute-start.7 = (f32[104,512]{1,0:T(8,128)S(1)}, f32[104,512]{1,0:T(8,128)S(1)}, u32[]{:S(2)}, u32[]{:S(2)}) collective-permute-start(f32[104,512]{1,0:T(8,128)S(1)} %get-tuple-element.44), channel_id=1, source_target_pairs={{0,4},{1,2},{2,1},{3,7},{4,0},{5,6},{6,5},{7,3},{8,12},{9,10},{10,... | collective-permute-start | bytes 638984 | tf_op jit(solution)/shard_map/ppermute | solution.py:59
  31.9 4.0 %copy-start.1 = (f32[16]{0:T(128)S(1)}, f32[16]{0:T(128)}, u32[]{:S(2)}) copy-start(f32[16]{0:T(128)} %param.3) | copy-start | bytes 196
  36.5 2.1 %collective-permute-start.8 = (f32[65,4,512]{2,1,0:T(4,128)S(1)}, f32[65,4,512]{2,1,0:T(4,128)S(1)}, u32[]{:S(2)}, u32[]{:S(2)}) collective-permute-start(f32[65,4,512]{2,1,0:T(4,128)S(1)} %get-tuple-element.50), channel_id=1, source_target_pairs={{0,4},{1,5},{2,6},{3,7},{4,0},{5,1},{6,2},{7,3},{8,12},{9,13},{10,... | collective-permute-start | bytes 1597448 | tf_op jit(solution)/shard_map/ppermute | solution.py:59
  36.7 14.4 %collective-permute-start.9 = (f32[49,4,512]{2,1,0:T(4,128)S(1)}, f32[49,4,512]{2,1,0:T(4,128)S(1)}, u32[]{:S(2)}, u32[]{:S(2)}) collective-permute-start(f32[49,4,512]{2,1,0:T(4,128)S(1)} %get-tuple-element.51), channel_id=1, source_target_pairs={{0,16},{1,17},{2,18},{3,19},{4,8},{5,9},{6,10},{7,11},{8,4},{9,5},... | collective-permute-start | bytes 1204232 | tf_op jit(solution)/shard_map/ppermute | solution.py:59
  38.2 19.5 %collective-permute-start.11 = (f32[10,16,512]{2,1,0:T(8,128)S(1)}, f32[10,16,512]{2,1,0:T(8,128)S(1)}, u32[]{:S(2)}, u32[]{:S(2)}) collective-permute-start(f32[10,16,512]{2,1,0:T(8,128)S(1)} %get-tuple-element.54), channel_id=1, source_target_pairs={{0,1},{1,0},{2,3},{3,2},{4,5},{5,4},{6,7},{7,6},{8,9},{9,8},{10,11... | collective-permute-start | bytes 983048 | tf_op jit(solution)/shard_map/ppermute | solution.py:59
  38.6 19.2 %collective-permute-start.12 = (f32[10,16,512]{2,1,0:T(8,128)S(1)}, f32[10,16,512]{2,1,0:T(8,128)S(1)}, u32[]{:S(2)}, u32[]{:S(2)}) collective-permute-start(f32[10,16,512]{2,1,0:T(8,128)S(1)} %get-tuple-element.55), channel_id=1, source_target_pairs={{0,4},{1,2},{2,1},{3,7},{4,0},{5,6},{6,5},{7,3},{8,12},{9,10},{10,... | collective-permute-start | bytes 983048 | tf_op jit(solution)/shard_map/ppermute | solution.py:59
  38.6 12.5 %collective-permute-start.10 = (f32[16,4,512]{2,1,0:T(4,128)S(1)}, f32[16,4,512]{2,1,0:T(4,128)S(1)}, u32[]{:S(2)}, u32[]{:S(2)}) collective-permute-start(f32[16,4,512]{2,1,0:T(4,128)S(1)} %get-tuple-element.66), channel_id=1, source_target_pairs={{0,8},{4,12},{8,0},{12,4},{1,9},{5,13},{9,1},{13,5},{2,10},{6,14},... | collective-permute-start | bytes 393224 | tf_op jit(solution)/shard_map/ppermute | solution.py:829
  51.5 6.2 %collective-permute-start.13 = (f32[2,16,512]{2,1,0:T(8,128)S(1)}, f32[2,16,512]{2,1,0:T(8,128)S(1)}, u32[]{:S(2)}, u32[]{:S(2)}) collective-permute-start(f32[2,16,512]{2,1,0:T(8,128)S(1)} %get-tuple-element.56), channel_id=1, source_target_pairs={{0,1},{1,0},{2,3},{3,2},{4,5},{5,4},{6,7},{7,6},{8,9},{9,8},{10,11... | collective-permute-start | bytes 196616 | tf_op jit(solution)/shard_map/ppermute | solution.py:59
  51.9 5.8 %collective-permute-start.14 = (f32[2,16,512]{2,1,0:T(8,128)S(1)}, f32[2,16,512]{2,1,0:T(8,128)S(1)}, u32[]{:S(2)}, u32[]{:S(2)}) collective-permute-start(f32[2,16,512]{2,1,0:T(8,128)S(1)} %get-tuple-element.57), channel_id=1, source_target_pairs={{0,4},{1,2},{2,1},{3,7},{4,0},{5,6},{6,5},{7,3},{8,12},{9,10},{10,... | collective-permute-start | bytes 196616 | tf_op jit(solution)/shard_map/ppermute | solution.py:59

commit v7 on v6

--- a/solution.py
+++ b/solution.py
@@ -158,7 +158,7 @@
                     parts_ref[k, x, j, r : r + ROWS, :] = value
         return functional
 
-    return lax.fori_loop(0, planes, plane, functional, unroll=2)
+    return lax.fori_loop(0, planes, plane, functional, unroll=4)
 
 
 def forces(parts_ref, at, r, blocks):
@@ -381,7 +381,7 @@
         step(x + 4, own_b, x + 2, inner_f, x)
         return 0
 
-    lax.fori_loop(0, cx - 4, inner_step, 0, unroll=2)
+    lax.fori_loop(0, cx - 4, inner_step, 0, unroll=6)
     for k in range(NEAR):
         step(k + halo, own_b, k, outer_f, k)
         step(k + cx, own_b, k + cx - NEAR, outer_f, k + NEAR)
@@ -571,7 +571,7 @@
                 an[2, out_of(x), j, r : r + ROWS, :] = change[2]
         return 0
 
-    lax.fori_loop(0, planes, plane, 0, unroll=2)
+    lax.fori_loop(0, planes, plane, 0, unroll=4)
 
 
 def last_push(an, bm, out, rub, planes, at_of, cz, blocks):
@@ -621,7 +621,7 @@
                 column(ap, c, x, j, low, own, high, above[x, c : c + 1, cut], rows)
         return 0
 
-    lax.fori_loop(0, cx, own_plane, 0, unroll=2)
+    lax.fori_loop(0, cx, own_plane, 0, unroll=4)
     matrix = dealing(ny, True)
     relaxed[...] = dealt(relaxed[...].reshape(3 * cx * cz, ny), matrix).reshape(relaxed.shape)
     copy = pltpu.make_async_copy(relaxed, out, sent)

time: 61.9 us -> 61.5 us (level)
  no operation moved by 1% of the time
where the time goes in v7:
time: 61.5 us; the launch traced here: 61.3 us
  blocking collectives  21.5 us (35%)
  Pallas kernels  20.9 us (34%)
  starting transfers between devices  13.5 us (22%)
  waiting for transfers between devices  2.9 us (5%)
  local copies, waits for them, and re-layouts  1.75 us (3%)
  between operations  0.8 us (1%)
    all_to_all x2, blocking collectives, shared(): return lax.all_to_all(tile_copies, ('gz', 'gx'), 0, 0)  21.5 us
    pallas_call x9, Pallas kernels, call(): pl.pallas_call(kernel, out_shape=shapes, in_specs=[pl.BlockSpec(memory_sp...  20.9 us
    ppermute x7, starting transfers between devices, swapped(): lax.ppermute(pair[0], AXES, first)  8.02 us
    ppermute x7, starting transfers between devices, swapped(): lax.ppermute(pair[1], AXES, second)  4.72 us
    ppermute x7, waiting for transfers between devices, swapped(): lax.ppermute(pair[1], AXES, second)  2.88 us
    dynamic_slice x1, local copies, waits for them, and re-layouts, body(): lax.dynamic_slice_in_dim(magnetic, jnp.where(even == first, far, 0), HALO...  1.67 us
  transfers between devices with their start and end apart: 15, of which 1 were waited for; matrix products, arithmetic and copies ran while one was open for 0% of the time, Pallas kernels for 18%

profile of v7, /device:TPU:0, one launch (start us, length us, event | category | flops | bytes accessed | tf_op | source)
XLA Modules:
  0.0 61.3 jit_solution(4663160892477221918)
XLA Ops:
  0.6 0.0 copy-start
  0.7 1.7 %constant_dynamic-slice_fusion = (f32[3,16,4,512]{3,2,1,0:T(4,128)S(1)}, f32[3,16,4,512]{3,2,1,0:T(4,128)S(1)}) fusion(f32[3,16,16,512]{3,2,1,0:T(8,128)} %magnetic.1, s32[]{:T(128)S(6)} %select_n.18, s32[]{:T(128)S(6)} %select_n.17), kind=kLoop, calls=%fused_computation.1 | loop fusion | bytes 1572872 | tf_op jit(solution)/shard_map/dynamic_slice | solution.py:766
  2.3 3.0 %collective-permute-start.1 = (f32[3,16,4,512]{3,2,1,0:T(4,128)S(1)}, f32[3,16,4,512]{3,2,1,0:T(4,128)S(1)}, u32[]{:S(2)}, u32[]{:S(2)}) collective-permute-start(f32[3,16,4,512]{3,2,1,0:T(4,128)S(1)} %get-tuple-element.64), channel_id=1, source_target_pairs={{0,16},{1,17},{2,18},{3,19},{4,8},{5,9},{6,10},{7,11},{8,4},{9,5},... | collective-permute-start | bytes 1179656 | tf_op jit(solution)/shard_map/ppermute | solution.py:59
  5.4 0.1 collective-permute-start
  5.5 0.0 copy-done
  5.5 1.0 %shard_map.41 = (f32[3,16,16,512]{3,2,1,0:T(8,128)S(1)}, f32[3,2,16,512]{3,2,1,0:T(8,128)S(1)}, f32[3,2,16,512]{3,2,1,0:T(8,128)S(1)}) custom-call(f32[3,16,16,512]{3,2,1,0:T(8,128)S(1)} %copy-done), custom_call_target="tpu_custom_call" | custom-call | flops 26214400 | bytes 2621440 | tf_op jit(solution)/shard_map/pallas_call | solution.py:734
  6.5 1.6 %collective-permute-start.2 = (f32[3,2,16,512]{3,2,1,0:T(8,128)S(1)}, f32[3,2,16,512]{3,2,1,0:T(8,128)S(1)}, u32[]{:S(2)}, u32[]{:S(2)}) collective-permute-start(f32[3,2,16,512]{3,2,1,0:T(8,128)S(1)} %get-tuple-element.37), channel_id=1, source_target_pairs={{0,1},{1,0},{2,3},{3,2},{4,5},{5,4},{6,7},{7,6},{8,9},{9,8},{10,11... | collective-permute-start | bytes 589832 | tf_op jit(solution)/shard_map/ppermute | solution.py:59
  8.1 0.2 collective-permute-start.3
  8.3 2.9 %collective-permute-done.1.face_zb = f32[3,16,4,512]{3,2,1,0:T(4,128)S(1)} collective-permute-done((f32[3,16,4,512]{3,2,1,0:T(4,128)S(1)}, f32[3,16,4,512]{3,2,1,0:T(4,128)S(1)}, u32[]{:S(2)}, u32[]{:S(2)}) %collective-permute-start.1) | collective-permute-done | bytes 393248 | tf_op jit(solution)/shard_map/ppermute | solution.py:59
  11.1 0.0 collective-permute-done.face_za
  11.1 0.1 shard_map.43
  11.2 2.1 %collective-permute-start.4 = (f32[32,512]{1,0:T(8,128)S(1)}, f32[32,512]{1,0:T(8,128)S(1)}, u32[]{:S(2)}, u32[]{:S(2)}) collective-permute-start(f32[32,512]{1,0:T(8,128)S(1)} %get-tuple-element.39), channel_id=1, source_target_pairs={{0,1},{1,0},{2,3},{3,2},{4,5},{5,4},{6,7},{7,6},{8,9},{9,8},{10,11... | collective-permute-start | bytes 196616 | tf_op jit(solution)/shard_map/ppermute | solution.py:59
  13.3 0.0 collective-permute-start.5
  13.3 3.6 %shard_map.42 = (f32[3,16,4,32,128]{4,3,2,1,0:T(8,128)S(1)}, f32[3,12,4,32,128]{4,3,2,1,0:T(8,128)S(1)}, f32[2,8,128]{2,1,0:T(8,128)S(1)}) custom-call(f32[3,16,16,512]{3,2,1,0:T(8,128)S(1)} %get-tuple-element.33.core, f32[3,16,4,512]{3,2,1,0:T(4,128)S(1)} %collective-permute-done.face_za, f32[3,16,4,512]{3,2,1,0:T(4,128)S(1)} %collective-permute-done.1.face_zb), custom_call_target="tpu_custom_call" | custom-call | flops 26214400 | bytes 2621440 | tf_op jit(solution)/shard_map/pallas_call | solution.py:734
  17.0 0.0 collective-permute-done.2.face_xa
  17.0 0.0 collective-permute-done.3.face_xb
  17.0 0.0 collective-permute-done.4.corner_a
  17.0 0.0 collective-permute-done.5.corner_b
  17.0 1.9 %shard_map.44 = (f32[3,12,4,32,128]{4,3,2,1,0:T(8,128)S(1)}, f32[3,4,4,32,128]{4,3,2,1,0:T(8,128)S(1)}, f32[16,8,128]{2,1,0:T(8,128)S(1)}, f32[104,512]{1,0:T(8,128)S(1)}, f32[104,512]{1,0:T(8,128)S(1)}) custom-call(f32[3,16,4,32,128]{4,3,2,1,0:T(8,128)S(1)} %get-tuple-element.34.own.own_b, f32[2,8,128]{2,1,0:T(8,128)S(1)} %get-tuple-element.36.part, ...), custom_call_target="tpu_custom_call" | custom-call | flops 26214400 | bytes 2621440 | tf_op jit(solution)/shard_map/pallas_call | solution.py:734
  18.9 3.2 %collective-permute-start.6 = (f32[104,512]{1,0:T(8,128)S(1)}, f32[104,512]{1,0:T(8,128)S(1)}, u32[]{:S(2)}, u32[]{:S(2)}) collective-permute-start(f32[104,512]{1,0:T(8,128)S(1)} %get-tuple-element.43), channel_id=1, source_target_pairs={{0,1},{1,0},{2,3},{3,2},{4,5},{5,4},{6,7},{7,6},{8,9},{9,8},{10,11... | collective-permute-start | bytes 638984 | tf_op jit(solution)/shard_map/ppermute | solution.py:59
  22.1 0.0 collective-permute-start.7
  22.1 9.7 %all_to_all.10.sums0 = f32[16,8,128]{2,1,0:T(8,128)S(1)} all-to-all(f32[16,8,128]{2,1,0:T(8,128)S(1)} %get-tuple-element.45), channel_id=1, replica_groups=mesh['runs'=2,'gz'=4,'gx'=4] {'gz','gx'}, dimensions={0} | all-to-all | bytes 131072 | tf_op jit(solution)/shard_map/all_to_all | solution.py:71
  31.9 0.0 collective-permute-done.6.rim_a
  31.9 0.0 collective-permute-done.7.rim_b
  31.9 0.0 copy-start.1
  31.9 3.8 %shard_map.45 = (f32[3,16,16,512]{3,2,1,0:T(8,128)S(1)}, f32[3,16,16,512]{3,2,1,0:T(8,128)S(1)}, f32[3,20,4,32,128]{4,3,2,1,0:T(8,128)S(1)}, f32[16,8,128]{2,1,0:T(8,128)S(1)}) custom-call(f32[3,16,4,32,128]{4,3,2,1,0:T(8,128)S(1)} %get-tuple-element.34.own.own_b, f32[3,12,4,32,128]{4,3,2,1,0:T(8,128)S(1)} %get-tuple-element.35.inner_f, ...), custom_call_target="tpu_custom_call" | custom-call | flops 26214400 | bytes 2621440 | tf_op jit(solution)/shard_map/pallas_call | solution.py:734
  35.7 0.0 copy-done.1
  35.7 0.1 broadcast_in_dim.2.friction
  35.8 0.5 shard_map.46
  36.3 0.2 collective-permute-start.8
  36.5 1.5 %collective-permute-start.9 = (f32[49,4,512]{2,1,0:T(4,128)S(1)}, f32[49,4,512]{2,1,0:T(4,128)S(1)}, u32[]{:S(2)}, u32[]{:S(2)}) collective-permute-start(f32[49,4,512]{2,1,0:T(4,128)S(1)} %get-tuple-element.51), channel_id=1, source_target_pairs={{0,16},{1,17},{2,18},{3,19},{4,8},{5,9},{6,10},{7,11},{8,4},{9,5},... | collective-permute-start | bytes 1204232 | tf_op jit(solution)/shard_map/ppermute | solution.py:59
  38.0 0.3 collective-permute-start.11
  38.3 0.0 collective-permute-start.12
  38.3 0.0 collective-permute-done.8.refs_2_.face_za
  38.4 0.7 %collective-permute-start.10 = (f32[16,4,512]{2,1,0:T(4,128)S(1)}, f32[16,4,512]{2,1,0:T(4,128)S(1)}, u32[]{:S(2)}, u32[]{:S(2)}) collective-permute-start(f32[16,4,512]{2,1,0:T(4,128)S(1)} %get-tuple-element.66), channel_id=1, source_target_pairs={{0,8},{4,12},{8,0},{12,4},{1,9},{5,13},{9,1},{13,5},{2,10},{6,14},... | collective-permute-start | bytes 393224 | tf_op jit(solution)/shard_map/ppermute | solution.py:829
  39.1 11.7 %all_to_all.11.refs_5_.sums0 = f32[16,8,128]{2,1,0:T(8,128)S(1)} all-to-all(f32[16,8,128]{2,1,0:T(8,128)S(1)} %get-tuple-element.49), channel_id=1, replica_groups=mesh['runs'=2,'gz'=4,'gx'=4] {'gz','gx'}, dimensions={0} | all-to-all | bytes 131072 | tf_op jit(solution)/shard_map/all_to_all | solution.py:71
  50.8 0.0 collective-permute-done.9.refs_3_.face_zb
  50.9 0.0 collective-permute-done.10.refs_1_
  50.9 0.4 shard_map.47
  51.3 0.4 collective-permute-start.13
  51.7 0.0 collective-permute-start.14
  51.7 5.7 %shard_map.48 = (f32[3,16,16,512]{3,2,1,0:T(8,128)}, f32[2,16,4,32,128]{4,3,2,1,0:T(8,128)S(1)}, f32[3,14,4,32,128]{4,3,2,1,0:T(8,128)S(1)}, f32[3,12,4,32,128]{...) custom-call(f32[3,16,16,512]{3,2,1,0:T(8,128)S(1)} %get-tuple-elemen, ...), custom_call_target="tpu_custom_call" | custom-call | flops 26214400 | bytes 2621440 | tf_op jit(solution)/shard_map/pallas_call | solution.py:734
  57.4 0.0 collective-permute-done.11.face_xa
  57.4 0.0 collective-permute-done.12.face_xb
  57.4 0.0 collective-permute-done.13.corner_a
  57.4 0.0 collective-permute-done.14.corner_b
  57.4 3.9 %shard_map.49 = f32[3,16,16,512]{3,2,1,0:T(8,128)} custom-call(f32[3,20,4,32,128]{4,3,2,1,0:T(8,128)S(1)} %get-tuple-element.48.refs_4_.bp, f32[16,8,128]{2,1,0:T(8,128)S(1)} %all_to_all.11.refs_5_.sums0, f32[10,16,512]{2,1,0:T(8,128)S(1)} %collective-permute-done.11.face_xa, f32[10,16,512]{2,1,0:T(8,128)S(1)} %collective-permute-done.12.face_xb, ...), custom_call_target="tpu_custom_call" | custom-call | flops 26214400 | bytes 2621440 | tf_op jit(solution)/shard_map/pallas_call | solution.py:734
  (1 shorter events, 0.0 us)
Async XLA Ops:
  0.6 4.8 %copy-start = (f32[3,16,16,512]{3,2,1,0:T(8,128)S(1)}, f32[3,16,16,512]{3,2,1,0:T(8,128)}, u32[]{:S(2)}) copy-start(f32[3,16,16,512]{3,2,1,0:T(8,128)} %magnetic.1) | copy-start | bytes 4718596
  2.3 8.8 %collective-permute-start.1 = (f32[3,16,4,512]{3,2,1,0:T(4,128)S(1)}, f32[3,16,4,512]{3,2,1,0:T(4,128)S(1)}, u32[]{:S(2)}, u32[]{:S(2)}) collective-permute-start(f32[3,16,4,512]{3,2,1,0:T(4,128)S(1)} %get-tuple-element.64), channel_id=1, source_target_pairs={{0,16},{1,17},{2,18},{3,19},{4,8},{5,9},{6,10},{7,11},{8,4},{9,5},... | collective-permute-start | bytes 1179656 | tf_op jit(solution)/shard_map/ppermute | solution.py:59
  5.4 5.8 %collective-permute-start = (f32[3,16,4,512]{3,2,1,0:T(4,128)S(1)}, f32[3,16,4,512]{3,2,1,0:T(4,128)S(1)}, u32[]{:S(2)}, u32[]{:S(2)}) collective-permute-start(f32[3,16,4,512]{3,2,1,0:T(4,128)S(1)} %get-tuple-element.65), channel_id=1, source_target_pairs={{0,4},{1,5},{2,6},{3,7},{4,0},{5,1},{6,2},{7,3},{8,12},{9,13},{10,... | collective-permute-start | bytes 1179656 | tf_op jit(solution)/shard_map/ppermute | solution.py:59
  6.5 10.5 %collective-permute-start.2 = (f32[3,2,16,512]{3,2,1,0:T(8,128)S(1)}, f32[3,2,16,512]{3,2,1,0:T(8,128)S(1)}, u32[]{:S(2)}, u32[]{:S(2)}) collective-permute-start(f32[3,2,16,512]{3,2,1,0:T(8,128)S(1)} %get-tuple-element.37), channel_id=1, source_target_pairs={{0,1},{1,0},{2,3},{3,2},{4,5},{5,4},{6,7},{7,6},{8,9},{9,8},{10,11... | collective-permute-start | bytes 589832 | tf_op jit(solution)/shard_map/ppermute | solution.py:59
  8.1 8.9 %collective-permute-start.3 = (f32[3,2,16,512]{3,2,1,0:T(8,128)S(1)}, f32[3,2,16,512]{3,2,1,0:T(8,128)S(1)}, u32[]{:S(2)}, u32[]{:S(2)}) collective-permute-start(f32[3,2,16,512]{3,2,1,0:T(8,128)S(1)} %get-tuple-element.38), channel_id=1, source_target_pairs={{0,4},{1,2},{2,1},{3,7},{4,0},{5,6},{6,5},{7,3},{8,12},{9,10},{10,... | collective-permute-start | bytes 589832 | tf_op jit(solution)/shard_map/ppermute | solution.py:59
  11.2 5.8 %collective-permute-start.4 = (f32[32,512]{1,0:T(8,128)S(1)}, f32[32,512]{1,0:T(8,128)S(1)}, u32[]{:S(2)}, u32[]{:S(2)}) collective-permute-start(f32[32,512]{1,0:T(8,128)S(1)} %get-tuple-element.39), channel_id=1, source_target_pairs={{0,1},{1,0},{2,3},{3,2},{4,5},{5,4},{6,7},{7,6},{8,9},{9,8},{10,11... | collective-permute-start | bytes 196616 | tf_op jit(solution)/shard_map/ppermute | solution.py:59
  13.3 3.7 %collective-permute-start.5 = (f32[32,512]{1,0:T(8,128)S(1)}, f32[32,512]{1,0:T(8,128)S(1)}, u32[]{:S(2)}, u32[]{:S(2)}) collective-permute-start(f32[32,512]{1,0:T(8,128)S(1)} %get-tuple-element.40), channel_id=1, source_target_pairs={{0,4},{1,2},{2,1},{3,7},{4,0},{5,6},{6,5},{7,3},{8,12},{9,10},{10,... | collective-permute-start | bytes 196616 | tf_op jit(solution)/shard_map/ppermute | solution.py:59
  18.9 12.9 %collective-permute-start.6 = (f32[104,512]{1,0:T(8,128)S(1)}, f32[104,512]{1,0:T(8,128)S(1)}, u32[]{:S(2)}, u32[]{:S(2)}) collective-permute-start(f32[104,512]{1,0:T(8,128)S(1)} %get-tuple-element.43), channel_id=1, source_target_pairs={{0,1},{1,0},{2,3},{3,2},{4,5},{5,4},{6,7},{7,6},{8,9},{9,8},{10,11... | collective-permute-start | bytes 638984 | tf_op jit(solution)/shard_map/ppermute | solution.py:59
  22.1 9.7 %collective-permute-start.7 = (f32[104,512]{1,0:T(8,128)S(1)}, f32[104,512]{1,0:T(8,128)S(1)}, u32[]{:S(2)}, u32[]{:S(2)}) collective-permute-start(f32[104,512]{1,0:T(8,128)S(1)} %get-tuple-element.44), channel_id=1, source_target_pairs={{0,4},{1,2},{2,1},{3,7},{4,0},{5,6},{6,5},{7,3},{8,12},{9,10},{10,... | collective-permute-start | bytes 638984 | tf_op jit(solution)/shard_map/ppermute | solution.py:59
  31.9 3.8 %copy-start.1 = (f32[16]{0:T(128)S(1)}, f32[16]{0:T(128)}, u32[]{:S(2)}) copy-start(f32[16]{0:T(128)} %param.3) | copy-start | bytes 196
  36.3 2.1 %collective-permute-start.8 = (f32[65,4,512]{2,1,0:T(4,128)S(1)}, f32[65,4,512]{2,1,0:T(4,128)S(1)}, u32[]{:S(2)}, u32[]{:S(2)}) collective-permute-start(f32[65,4,512]{2,1,0:T(4,128)S(1)} %get-tuple-element.50), channel_id=1, source_target_pairs={{0,4},{1,5},{2,6},{3,7},{4,0},{5,1},{6,2},{7,3},{8,12},{9,13},{10,... | collective-permute-start | bytes 1597448 | tf_op jit(solution)/shard_map/ppermute | solution.py:59
  36.5 14.4 %collective-permute-start.9 = (f32[49,4,512]{2,1,0:T(4,128)S(1)}, f32[49,4,512]{2,1,0:T(4,128)S(1)}, u32[]{:S(2)}, u32[]{:S(2)}) collective-permute-start(f32[49,4,512]{2,1,0:T(4,128)S(1)} %get-tuple-element.51), channel_id=1, source_target_pairs={{0,16},{1,17},{2,18},{3,19},{4,8},{5,9},{6,10},{7,11},{8,4},{9,5},... | collective-permute-start | bytes 1204232 | tf_op jit(solution)/shard_map/ppermute | solution.py:59
  38.0 19.4 %collective-permute-start.11 = (f32[10,16,512]{2,1,0:T(8,128)S(1)}, f32[10,16,512]{2,1,0:T(8,128)S(1)}, u32[]{:S(2)}, u32[]{:S(2)}) collective-permute-start(f32[10,16,512]{2,1,0:T(8,128)S(1)} %get-tuple-element.54), channel_id=1, source_target_pairs={{0,1},{1,0},{2,3},{3,2},{4,5},{5,4},{6,7},{7,6},{8,9},{9,8},{10,11... | collective-permute-start | bytes 983048 | tf_op jit(solution)/shard_map/ppermute | solution.py:59
  38.3 19.1 %collective-permute-start.12 = (f32[10,16,512]{2,1,0:T(8,128)S(1)}, f32[10,16,512]{2,1,0:T(8,128)S(1)}, u32[]{:S(2)}, u32[]{:S(2)}) collective-permute-start(f32[10,16,512]{2,1,0:T(8,128)S(1)} %get-tuple-element.55), channel_id=1, source_target_pairs={{0,4},{1,2},{2,1},{3,7},{4,0},{5,6},{6,5},{7,3},{8,12},{9,10},{10,... | collective-permute-start | bytes 983048 | tf_op jit(solution)/shard_map/ppermute | solution.py:59
  38.4 12.5 %collective-permute-start.10 = (f32[16,4,512]{2,1,0:T(4,128)S(1)}, f32[16,4,512]{2,1,0:T(4,128)S(1)}, u32[]{:S(2)}, u32[]{:S(2)}) collective-permute-start(f32[16,4,512]{2,1,0:T(4,128)S(1)} %get-tuple-element.66), channel_id=1, source_target_pairs={{0,8},{4,12},{8,0},{12,4},{1,9},{5,13},{9,1},{13,5},{2,10},{6,14},... | collective-permute-start | bytes 393224 | tf_op jit(solution)/shard_map/ppermute | solution.py:829
  51.3 6.1 %collective-permute-start.13 = (f32[2,16,512]{2,1,0:T(8,128)S(1)}, f32[2,16,512]{2,1,0:T(8,128)S(1)}, u32[]{:S(2)}, u32[]{:S(2)}) collective-permute-start(f32[2,16,512]{2,1,0:T(8,128)S(1)} %get-tuple-element.56), channel_id=1, source_target_pairs={{0,1},{1,0},{2,3},{3,2},{4,5},{5,4},{6,7},{7,6},{8,9},{9,8},{10,11... | collective-permute-start | bytes 196616 | tf_op jit(solution)/shard_map/ppermute | solution.py:59
  51.7 5.7 %collective-permute-start.14 = (f32[2,16,512]{2,1,0:T(8,128)S(1)}, f32[2,16,512]{2,1,0:T(8,128)S(1)}, u32[]{:S(2)}, u32[]{:S(2)}) collective-permute-start(f32[2,16,512]{2,1,0:T(8,128)S(1)} %get-tuple-element.57), channel_id=1, source_target_pairs={{0,4},{1,2},{2,1},{3,7},{4,0},{5,6},{6,5},{7,3},{8,12},{9,10},{10,... | collective-permute-start | bytes 196616 | tf_op jit(solution)/shard_map/ppermute | solution.py:59
